TPU v7x, 128 devices: a whole 4x4x4 slice. The times are simulated.
128 devices in a mesh: section: 4 (over y), fsdp: 32 (over x, z, core).
Axes of the slice: x: 4, y: 4, z: 4, core: 2. Of those that a mesh axis runs over, the one named last changes fastest.
Arguments:
- weights: bfloat16 [4, 4096, 4096], P('section', 'fsdp'), may hold values from -0.09375 to 0.09375
- kv_weights: bfloat16 [4, 4096, 256], P('section', 'fsdp'), may hold values from -0.09375 to 0.09375
- gammas: float32 [4, 3], P('section'), may hold values from 1 to 3
- gains: bfloat16 [4, 4096], P('section'), may hold values from 0.5 to 1.5
- starts: bfloat16 [4, 3, 4096], P('section', None, 'fsdp'), may hold values from -6 to 6
- source: bfloat16 [2, 32, 128, 4096], P(None, 'fsdp'), may hold values from -6 to 6
- target: bfloat16 [2, 32, 128, 4096], P(None, 'fsdp'), may hold values from -6 to 6
- lengths: int32 [2, 32], P(None, 'fsdp'), may hold values from 32 to 128, as said below
Outputs:
- states: bfloat16 [4, 2, 32, 128, 4096], P('section', None, 'fsdp')
- next_starts: float32 [4, 3, 4096], P('section', None, 'fsdp')
Inputs may be any that keep to these rules, and one draw needn't show every extreme that they name: `lengths`: key positions at or beyond a sequence's length are padding; some sequence has all 128 tokens.
All inputs are finite; a program needn't handle non-finite values.
Results may differ from a plain program's by a relative error of at most 0.024.
Values may be sent and summed in bfloat16 or wider, within the bound.
No kernel may reach another device: no remote copies, remote signals or barrier semaphores. Data moves between devices by JAX's collectives and lax.ppermute only.
A program may use at most 192 MiB of HBM per device.

v0:
```python
import functools
import math

import jax
import jax.numpy as jnp
from jax import lax
from jax.experimental import pallas as pl
from jax.experimental.pallas import tpu as pltpu
from jax.sharding import PartitionSpec as P

HEAD = 128
EPS = 1e-06
F32 = jnp.float32
BF16 = jnp.bfloat16
VMEM_LIMIT = 48 * 1024 * 1024
BLOCK = 512
ROUTE = (0, -1, 1, 2)
PARTS = (1024, 1024, 1024, 1024)
SLOTS = 3
LOG2E_SCALED = math.log2(math.e) / math.sqrt(HEAD)
ANY = pl.BlockSpec(memory_space=pl.ANY)
VMEM = pl.BlockSpec(memory_space=pltpu.VMEM)
SMEM = pl.BlockSpec(memory_space=pltpu.SMEM)


def dot(a, b):
    return jnp.dot(a, b, preferred_element_type=F32)


def moves(fn):
    pairs = []
    for index in range(32):
        x, z, core = index // 8, (index // 2) % 4, index % 2
        x2, z2, core2 = fn(x, z, core)
        pairs.append((index, (x2 % 4) * 8 + (z2 % 4) * 2 + core2))
    return pairs


def first_move(step):
    return moves(lambda x, z, c: (x, z + step, c) if c == 0 else (x + step, z, c))


def second_move(step):
    return moves(lambda x, z, c: (x + step, z, c) if c == 0 else (x, z + step, c))


CORE_SWAP = moves(lambda x, z, c: (x, z, 1 - c))
DOUBLING = (
    CORE_SWAP,
    moves(lambda x, z, c: (x, z ^ 1, c)),
    moves(lambda x, z, c: (x ^ 1, z, c)),
    moves(lambda x, z, c: (x, z ^ 2, c)),
    moves(lambda x, z, c: (x ^ 2, z, c)),
)


def send(value, pairs):
    return lax.ppermute(value, "fsdp", pairs)


def ring(block, move, forward):
    before = send(block, move(1))
    after = send(block, move(-1))
    far = send(before, move(1)) if forward else send(after, move(-1))
    return [block, before, after, far]


def row_order():
    index = lax.axis_index("fsdp")
    x, z, core = index // 8, (index // 2) % 4, index % 2
    first = jnp.array(ROUTE, jnp.int32)
    line = jnp.tile(first, 4)
    plane = jnp.repeat(first, 4)

    def order(kind):
        zs = z + jnp.where(kind == 0, line, plane)
        xs = x + jnp.where(kind == 0, plane, line)
        return ((xs + 8) % 4) * 8 + ((zs + 8) % 4) * 2 + kind

    return jnp.concatenate([order(core), order(1 - core)]).astype(jnp.int32)


def total(value):
    for pairs in DOUBLING:
        value = value + send(value, pairs)
    return value


def params():
    return pltpu.CompilerParams(vmem_limit_bytes=VMEM_LIMIT)


def cost(flops, size, exps=0):
    return pl.CostEstimate(flops=int(flops), bytes_accessed=int(size), transcendentals=int(exps))


def stack_kernel(count, *refs):
    sources, out, sems = refs[:count], refs[count], refs[count + 1]
    rows = sources[0].shape[0]
    copies = [
        pltpu.make_async_copy(source, out.at[pl.ds(i * rows, rows)], sems.at[i])
        for i, source in enumerate(sources)
    ]
    for copy in copies:
        copy.start()
    for copy in copies:
        copy.wait()


def stack(blocks):
    count = len(blocks)
    rows, width = blocks[0].shape
    return pl.pallas_call(
        functools.partial(stack_kernel, count),
        out_shape=jax.ShapeDtypeStruct((count * rows, width), blocks[0].dtype),
        in_specs=[ANY] * count,
        out_specs=ANY,
        scratch_shapes=[pltpu.SemaphoreType.DMA((count,))],
        compiler_params=pltpu.CompilerParams(vmem_limit_bytes=1024 * 1024),
        cost_estimate=cost(0, 4 * count * rows * width),
    )(*blocks)


def norm_into(xn_ref, x_ref, gain_ref, row, order_ref):
    wide = x_ref[...].astype(F32)
    inv = lax.rsqrt(jnp.mean(wide * wide, axis=-1, keepdims=True) + EPS)
    for k in range(32):
        at = pl.ds(pl.multiple_of(order_ref[k] * 128, 128), 128)
        part = x_ref[:, at].astype(F32) * inv * gain_ref[row : row + 1, at]
        xn_ref[:, k * 128 : (k + 1) * 128] = part.astype(BF16)


def attend(q, keys_ref, values_ref, resid, lengths_ref):
    seqs, heads = q.shape[0] // 128, q.shape[1] // HEAD
    position = lax.broadcasted_iota(jnp.int32, (heads * 128, 128), 1)
    made = []
    for m in range(seqs):
        rows = slice(m * 128, (m + 1) * 128)
        stacked = jnp.concatenate([q[rows, h * HEAD : (h + 1) * HEAD] for h in range(heads)], 0)
        scores = lax.dot_general(
            stacked, keys_ref[rows, :], (((1,), (1,)), ((), ())), preferred_element_type=F32
        )
        expd = jnp.where(position < lengths_ref[m], jnp.exp2(scores * LOG2E_SCALED), 0.0)
        probs = (expd * (1.0 / jnp.sum(expd, axis=-1, keepdims=True))).astype(BF16)
        context = dot(probs, values_ref[rows, :])
        made.append(jnp.concatenate([context[h * 128 : (h + 1) * 128] for h in range(heads)], 1))
    return (resid.astype(F32) + jnp.concatenate(made, 0)).astype(BF16)


def project_into(keys_ref, values_ref, xn_ref, kv, key_scale, value_scale):
    projected = dot(xn_ref[...], kv)
    keys_ref[...] = (projected[:, :HEAD] * key_scale).astype(BF16)
    values_ref[...] = (projected[:, HEAD:] * value_scale).astype(BF16)


def enter_kernel(order_ref, section_ref, source_ref, target_ref, gain_ref, x_ref, xn_ref):
    @pl.when(section_ref[0] == 2)
    def _():
        x_ref[...] = target_ref[...]

    @pl.when(section_ref[0] != 2)
    def _():
        x_ref[...] = source_ref[...]

    norm_into(xn_ref, x_ref, gain_ref, 0, order_ref)


def project_kernel(scale_ref, xn_ref, own_ref, other_ref, keys_ref, values_ref):
    kv = jnp.concatenate([own_ref[...], other_ref[...]], 0)
    project_into(keys_ref, values_ref, xn_ref, kv, scale_ref[1], scale_ref[2])


def part_kernel(lengths_ref, section_ref, scale_ref, xn_ref, own_ref, other_ref, k_ref, v_ref, x_ref, out_ref):
    half = own_ref.shape[0]
    acc = dot(xn_ref[:, :half], own_ref[...]) + dot(xn_ref[:, half:], other_ref[...])
    q = (acc * scale_ref[0]).astype(BF16)

    @pl.when(section_ref[0] != 2)
    def _():
        out_ref[...] = attend(q, k_ref, v_ref, x_ref[...], lengths_ref)

    @pl.when(section_ref[0] == 2)
    def _():
        out_ref[...] = q


def layer_part(xn, own, other, keys, values, x, at, width, lengths, section, scales, block):
    rows = xn.shape[0]
    depth = own.shape[0]
    whole = lambda a: pl.BlockSpec(a.shape, lambda j: (0, 0))
    return pl.pallas_call(
        part_kernel,
        grid=(width // block,),
        out_shape=jax.ShapeDtypeStruct((rows, width), BF16),
        in_specs=[
            SMEM,
            SMEM,
            SMEM,
            whole(xn),
            pl.BlockSpec((depth, block), lambda j: (0, j)),
            pl.BlockSpec((depth, block), lambda j: (0, j)),
            whole(keys),
            whole(values),
            pl.BlockSpec((rows, block), lambda j: (0, at // block + j)),
        ],
        out_specs=pl.BlockSpec((rows, block), lambda j: (0, j)),
        compiler_params=params(),
        cost_estimate=cost(4 * rows * depth * width, 4 * depth * width, rows * width),
    )(lengths, section, scales, xn, own, other, keys, values, x)


def stream_layer(parts, buf, sems, xn_ref, q_ref, k_ref, v_ref, x_ref, lengths_ref, scale, out_ref):
    half = buf.shape[1] // 2
    firsts = [0]
    for width in PARTS:
        firsts.append(firsts[-1] + width // BLOCK)
    blocks = firsts[-1]

    def pair(own, other, at, slot):
        columns = pl.ds(at, BLOCK)
        return (
            pltpu.make_async_copy(own.at[:, columns], buf.at[slot, pl.ds(0, half)], sems.at[slot, 0]),
            pltpu.make_async_copy(other.at[:, columns], buf.at[slot, pl.ds(half, half)], sems.at[slot, 1]),
        )

    def begin(b):
        slot = lax.rem(b, SLOTS)
        for i, (own, other) in enumerate(parts):

            @pl.when((b >= firsts[i]) & (b < firsts[i + 1]))
            def _():
                for copy in pair(own, other, pl.multiple_of((b - firsts[i]) * BLOCK, BLOCK), slot):
                    copy.start()

    def start():
        for b in range(SLOTS - 1):
            begin(jnp.int32(b))

    def run():
        q_ref[...] = jnp.zeros_like(q_ref)

        def emit(b):
            columns = pl.ds(pl.multiple_of(b * BLOCK, BLOCK), BLOCK)
            out_ref[:, columns] = attend(q_ref[...], k_ref, v_ref, x_ref[:, columns], lengths_ref)

        def step(b, carry):
            slot = lax.rem(b, SLOTS)
            for copy in pair(*parts[0], 0, slot):
                copy.wait()

            @pl.when(b + SLOTS - 1 < blocks)
            def _():
                begin(b + SLOTS - 1)

            acc = dot(xn_ref[...], buf[slot])
            emit(jnp.maximum(b - 1, 0))
            q_ref[...] = (acc * scale).astype(BF16)
            return carry

        lax.fori_loop(0, blocks, step, 0)
        emit(jnp.int32(blocks - 1))

    return start, run


def bring(pieces, out_ref, sems):
    at = 0
    copies = []
    for i, piece in enumerate(pieces):
        copies.append(pltpu.make_async_copy(piece, out_ref.at[:, pl.ds(at, piece.shape[1])], sems.at[i]))
        at += piece.shape[1]
    return copies


def encoder_kernel(*refs):
    n = len(PARTS)
    order_ref, section_ref, lengths_ref, scale_ref, gain_ref = refs[:5]
    pieces = refs[5 : 5 + n]
    flat = refs[5 + n : 5 + 3 * n]
    parts = [(flat[2 * i], flat[2 * i + 1]) for i in range(n)]
    kv_refs = refs[5 + 3 * n : 9 + 3 * n]
    out_ref, cross_ref = refs[9 + 3 * n : 11 + 3 * n]
    buf, sems, kv_buf, kv_sems, x_ref, x_sems, xn_ref, q_ref, k_ref, v_ref = refs[11 + 3 * n :]
    half = kv_buf.shape[1] // 2
    kv_at = pl.ds(PARTS[0], 2 * HEAD)

    @pl.when(section_ref[0] == 1)
    def _():
        arrive = bring(pieces, x_ref, x_sems)
        for copy in arrive:
            copy.start()
        kv_parts = [
            (parts[0][0].at[:, kv_at], parts[0][1].at[:, kv_at]),
            (kv_refs[0], kv_refs[1]),
            (kv_refs[2], kv_refs[3]),
        ]
        kv_copies = []
        for i, halves in enumerate(kv_parts):
            for c, ref in enumerate(halves):
                kv_copies.append(
                    pltpu.make_async_copy(ref, kv_buf.at[i, pl.ds(c * half, half)], kv_sems.at[i, c])
                )
        for copy in kv_copies[:2]:
            copy.start()
        start, run = stream_layer(
            parts, buf, sems, xn_ref, q_ref, k_ref, v_ref, x_ref, lengths_ref, scale_ref[0], out_ref
        )
        start()
        for copy in kv_copies[2:]:
            copy.start()
        for copy in arrive:
            copy.wait()
        norm_into(xn_ref, x_ref, gain_ref, 0, order_ref)
        for copy in kv_copies[:2]:
            copy.wait()
        project_into(k_ref, v_ref, xn_ref, kv_buf[0], scale_ref[1], scale_ref[2])
        run()
        for copy in kv_copies[2:]:
            copy.wait()
        for i in (1, 2):
            norm_into(xn_ref, out_ref, gain_ref, i, order_ref)
            at = (i - 1) * 2 * HEAD
            project_into(
                cross_ref.at[:, pl.ds(at, HEAD)],
                cross_ref.at[:, pl.ds(at + HEAD, HEAD)],
                xn_ref,
                kv_buf[i],
                scale_ref[3 * i + 1],
                scale_ref[3 * i + 2],
            )


def decoder_kernel(*refs):
    n = len(PARTS)
    order_ref, section_ref, lengths_ref, scale_ref, gain_ref, cross_ref, first_out, target = refs[:8]
    made = refs[8 : 8 + n]
    passed = refs[8 + n : 8 + 2 * n]
    flat = refs[8 + 2 * n : 8 + 4 * n]
    parts = [(flat[2 * i], flat[2 * i + 1]) for i in range(n)]
    out_ref = refs[8 + 4 * n]
    buf, sems, x_ref, x_sems, mid_ref, xn_ref, q_ref = refs[9 + 4 * n :]
    section = section_ref[0]
    blocks = sum(PARTS) // BLOCK
    cols = lambda i: cross_ref.at[:, pl.ds(i * HEAD, HEAD)]

    def fetch(pieces, into):
        copies = bring(pieces, into, x_sems)
        for copy in copies:
            copy.start()
        for copy in copies:
            copy.wait()

    def attend_all(resid_ref, into):
        def step(b, carry):
            columns = pl.ds(pl.multiple_of(b * BLOCK, BLOCK), BLOCK)
            into[:, columns] = attend(x_ref[:, columns], cols(0), cols(1), resid_ref[:, columns], lengths_ref)
            return carry

        lax.fori_loop(0, blocks, step, 0)

    @pl.when(section == 0)
    def _():
        fetch(made, out_ref)

    @pl.when(section == 1)
    def _():
        fetch([first_out], out_ref)

    @pl.when(section == 2)
    def _():
        fetch(made, x_ref)
        attend_all(target, out_ref)

    @pl.when(section == 3)
    def _():
        start, run = stream_layer(
            parts, buf, sems, xn_ref, q_ref, cols(2), cols(3), mid_ref, lengths_ref, scale_ref[0], out_ref
        )
        copies = bring(passed, x_ref, x_sems)
        for copy in copies:
            copy.start()
        start()
        for copy in copies:
            copy.wait()
        attend_all(target, mid_ref)
        norm_into(xn_ref, mid_ref, gain_ref, 0, order_ref)
        run()


def unit_direction(along):
    return (along * lax.rsqrt(jnp.sum(along * along) + EPS)).astype(BF16)


def spectral(weight, kv_part, start_rows, gamma):
    width = weight.shape[1]
    of_kv = dot(start_rows, kv_part)
    parts = jnp.concatenate([dot(start_rows[0:1], weight)[0], of_kv[1, :HEAD], of_kv[2, HEAD:]])
    along = total(parts.reshape(-1, 128)).reshape(-1)
    images = jnp.stack(
        [
            dot(weight, unit_direction(along[:width])),
            dot(kv_part[:, :HEAD], unit_direction(along[width : width + HEAD])),
            dot(kv_part[:, HEAD:], unit_direction(along[width + HEAD :])),
        ]
    )
    squares = jnp.sum(images * images, axis=1)
    totals = total(jnp.broadcast_to(squares[:, None], (3, 128)))[:, 0]
    sigmas = jnp.sqrt(totals + EPS)
    return gamma / sigmas, images / sigmas[:, None], along


def shards(weights, kv_weights, gammas, gains, starts, source, target, lengths):
    weight, kv_part, gamma, gain, start_rows = weights[0], kv_weights[0], gammas[0], gains[0], starts[0]
    width = weight.shape[1]
    section = lax.axis_index("section").astype(jnp.int32).reshape(1)
    micro, seqs, length, _ = source.shape
    rows = micro * seqs * length
    seq_lengths = lengths.reshape(-1)
    source2 = source.reshape(rows, width)
    target2 = target.reshape(rows, width)
    wide_gain = gain.astype(F32).reshape(1, width)
    row_shape = jax.ShapeDtypeStruct((rows, width), BF16)
    head_shape = jax.ShapeDtypeStruct((rows, HEAD), BF16)

    hop = lambda value, pairs: lax.ppermute(value, "section", pairs)
    order = row_order()
    scales, next_part, along = spectral(weight, kv_part, start_rows, gamma)

    x0, xn0 = pl.pallas_call(
        enter_kernel,
        out_shape=(row_shape, row_shape),
        in_specs=[SMEM, SMEM, VMEM, VMEM, VMEM],
        out_specs=(VMEM, VMEM),
        compiler_params=params(),
        cost_estimate=cost(8 * rows * width, 8 * rows * width),
    )(order, section, source2, target2, wide_gain)

    ends = [sum(PARTS[: i + 1]) for i in range(len(PARTS))]
    head_block = jnp.concatenate([weight[:, : ends[0]], kv_part], 1)
    tail_block = weight[:, ends[0] :]
    head_line = ring(head_block, first_move, True)
    tail_block, _ = lax.optimization_barrier((tail_block, along))
    tail_line = ring(tail_block, first_move, False)
    gathered = []
    for i in range(len(PARTS)):
        if i == 0:
            line = stack(head_line)
        else:
            line = stack([a[:, ends[i - 1] - ends[0] : ends[i] - ends[0]] for a in tail_line])
        if i == 1:
            line, scales = lax.optimization_barrier((line, scales))
        own = stack(ring(line, second_move, i % 2 == 0))
        gathered.append((own, send(own, CORE_SWAP)))
    kv_own, kv_other = (a[:, PARTS[0] :] for a in gathered[0])

    kv2_own = hop(kv_own, [(2, 1)])
    kv3_own = hop(kv_own, [(3, 1)])
    kv2_other = send(kv2_own, CORE_SWAP)
    kv3_other = send(kv3_own, CORE_SWAP)
    small = jnp.concatenate([gain.astype(F32), jnp.pad(scales, (0, 125))]).reshape(-1, 128)
    small2 = hop(small, [(2, 1)]).reshape(-1)
    small3 = hop(small, [(3, 1)]).reshape(-1)

    depth = gathered[0][0].shape[0]
    kv_block = pl.BlockSpec((depth, 2 * HEAD), lambda j: (0, PARTS[0] // (2 * HEAD)))
    whole = lambda shape: pl.BlockSpec(shape, lambda j: (0, 0))
    keys, values = pl.pallas_call(
        project_kernel,
        grid=(1,),
        out_shape=(head_shape, head_shape),
        in_specs=[SMEM, whole((rows, width)), kv_block, kv_block],
        out_specs=(whole((rows, HEAD)), whole((rows, HEAD))),
        compiler_params=params(),
        cost_estimate=cost(4 * rows * width * HEAD, 4 * width * HEAD),
    )(scales, xn0, *gathered[0])

    made, passed = [], []
    for i, (own, other) in enumerate(gathered):
        part = layer_part(
            xn0, own, other, keys, values, x0, ends[i] - PARTS[i], PARTS[i], seq_lengths, section, scales, BLOCK
        )
        made.append(part)
        passed.append(hop(part, [(0, 1), (2, 3)]))
    flat = [half for halves in gathered for half in halves]

    scratch = [
        pltpu.VMEM((SLOTS, 2 * depth, BLOCK), BF16),
        pltpu.SemaphoreType.DMA((SLOTS, 2)),
    ]
    n = len(PARTS)
    all_scales = jnp.concatenate([scales, small2[width : width + 3], small3[width : width + 3]])
    all_gains = jnp.concatenate([wide_gain, small2[None, :width], small3[None, :width]], 0)
    layer_cost = cost(2 * rows * width * width, 2 * width * width, rows * width)
    out1, cross = pl.pallas_call(
        encoder_kernel,
        out_shape=(row_shape, jax.ShapeDtypeStruct((rows, 4 * HEAD), BF16)),
        in_specs=[SMEM] * 4 + [VMEM] + [ANY] * (3 * n + 4),
        out_specs=(VMEM, VMEM),
        scratch_shapes=scratch
        + [
            pltpu.VMEM((3, 2 * depth, 2 * HEAD), BF16),
            pltpu.SemaphoreType.DMA((3, 2)),
            pltpu.VMEM((rows, width), BF16),
            pltpu.SemaphoreType.DMA((n,)),
            pltpu.VMEM((rows, width), BF16),
            pltpu.VMEM((rows, BLOCK), BF16),
            pltpu.VMEM((rows, HEAD), BF16),
            pltpu.VMEM((rows, HEAD), BF16),
        ],
        compiler_params=params(),
        cost_estimate=layer_cost,
    )(order, section, seq_lengths, all_scales, all_gains, *passed, *flat, kv2_own, kv2_other, kv3_own, kv3_other)
    cross = hop(cross, [(1, 2)]) + hop(cross, [(1, 3)])

    result = pl.pallas_call(
        decoder_kernel,
        out_shape=row_shape,
        in_specs=[SMEM] * 4 + [VMEM, VMEM, ANY, VMEM] + [ANY] * (4 * n),
        out_specs=VMEM,
        scratch_shapes=scratch
        + [
            pltpu.VMEM((rows, width), BF16),
            pltpu.SemaphoreType.DMA((n,)),
            pltpu.VMEM((rows, width), BF16),
            pltpu.VMEM((rows, width), BF16),
            pltpu.VMEM((rows, BLOCK), BF16),
        ],
        compiler_params=params(),
        cost_estimate=layer_cost,
    )(order, section, seq_lengths, scales, wide_gain, cross, out1, target2, *made, *passed, *flat)
    return result.reshape(1, micro, seqs, length, width), next_part[None]


def solution(mesh):
    in_specs = (
        P("section", "fsdp", None),
        P("section", "fsdp", None),
        P("section", None),
        P("section", None),
        P("section", None, "fsdp"),
        P(None, "fsdp", None, None),
        P(None, "fsdp", None, None),
        P(None, "fsdp"),
    )
    out_specs = (P("section", None, "fsdp", None, None), P("section", None, "fsdp"))
    return jax.shard_map(shards, mesh=mesh, in_specs=in_specs, out_specs=out_specs, check_vma=False)
```

profile of v0, /device:TPU:24, one launch (start us, length us, event | category | flops | bytes accessed | tf_op | source)
XLA Modules:
  0.0 330.0 jit_solution(5448113691923814317)
XLA Ops:
  9.9 2.3 collective-permute-done.5
  12.2 3.9 %collective-permute-start.6 = (f32[34,128]{1,0:T(8,128)S(1)}, f32[34,128]{1,0:T(8,128)S(1)}, u32[]{:S(2)}, u32[]{:S(2)}) collective-permute-start(f32[34,128]{1,0:T(8,128)S(1)} %add.170), channel_id=1, source_target_pairs={{0,4},{1,5},{2,6},{3,7},{4,0},{5,1},{6,2},{7,3},{8,12},{9,13},{10,... | collective-permute-start | bytes 52232 | tf_op jit(solution)/shard_map/ppermute | solution.py:58
  17.8 3.0 collective-permute-start.7
  34.1 6.3 %collective-permute-done.9 = f32[3,128]{0,1:T(8,128)S(1)} collective-permute-done((f32[3,128]{0,1:T(8,128)S(1)}, f32[3,128]{0,1:T(8,128)S(1)}, u32[]{:S(2)}, u32[]{:S(2)}) %collective-permute-start.9) | collective-permute-done | bytes 1568 | tf_op jit(solution)/shard_map/ppermute | solution.py:58
  41.1 3.7 %collective-permute-done.10 = f32[3,128]{0,1:T(8,128)S(1)} collective-permute-done((f32[3,128]{0,1:T(8,128)S(1)}, f32[3,128]{0,1:T(8,128)S(1)}, u32[]{:S(2)}, u32[]{:S(2)}) %collective-permute-start.10) | collective-permute-done | bytes 1568 | tf_op jit(solution)/shard_map/ppermute | solution.py:58
  44.8 3.7 %collective-permute-start.11 = (f32[3,128]{0,1:T(8,128)S(1)}, f32[3,128]{0,1:T(8,128)S(1)}, u32[]{:S(2)}, u32[]{:S(2)}) collective-permute-start(f32[3,128]{0,1:T(8,128)S(1)} %add.178), channel_id=1, source_target_pairs={{0,4},{1,5},{2,6},{3,7},{4,0},{5,1},{6,2},{7,3},{8,12},{9,13},{10,... | collective-permute-start | bytes 4616 | tf_op jit(solution)/shard_map/ppermute | solution.py:58
  48.4 2.9 collective-permute-done.11
  60.5 14.2 %collective-permute-done.2 = bf16[128,3072]{1,0:T(8,128)(2,1)S(1)} collective-permute-done((bf16[128,3072]{1,0:T(8,128)(2,1)}, bf16[128,3072]{1,0:T(8,128)(2,1)S(1)}, u32[]{:S(2)}, u32[]{:S(2)}) %collective-permute-start.2) | collective-permute-done | bytes 786464 | tf_op jit(solution)/shard_map/ppermute | solution.py:58
  80.0 2.5 collective-permute-start.34
  82.5 7.5 %collective-permute-done.24.refs_2_ = bf16[512,1024]{1,0:T(8,128)(2,1)S(1)} collective-permute-done((bf16[512,1024]{1,0:T(8,128)(2,1)S(1)}, bf16[512,1024]{1,0:T(8,128)(2,1)S(1)}, u32[]{:S(2)}, u32[]{:S(2)}) %collective-permute-start.24) | collective-permute-done | bytes 1048608 | tf_op jit(solution)/shard_map/ppermute | solution.py:58
  90.1 3.7 %collective-permute-start.25 = (bf16[512,1024]{1,0:T(8,128)(2,1)S(1)}, bf16[512,1024]{1,0:T(8,128)(2,1)S(1)}, u32[]{:S(2)}, u32[]{:S(2)}) collective-permute-start(bf16[512,1024]{1,0:T(8,128)(2,1)S(1)} %collective-permute-done.24.refs_2_), channel_id=1, source_target_pairs={{0,24},{1,7},{2,26},{3,1},{4,28},{5,3},{6,30},{7,5},{8,0},{9,15},{... | collective-permute-start | bytes 3145736 | tf_op jit(solution)/shard_map/ppermute | solution.py:58
  95.9 2.4 shard_map.107.own_ref.refs_9_.refs_16_
  98.4 8.8 %collective-permute-done.23.refs_1_ = bf16[512,1024]{1,0:T(8,128)(2,1)S(1)} collective-permute-done((bf16[512,1024]{1,0:T(8,128)(2,1)S(1)}, bf16[512,1024]{1,0:T(8,128)(2,1)S(1)}, u32[]{:S(2)}, u32[]{:S(2)}) %collective-permute-start.23) | collective-permute-done | bytes 1048608 | tf_op jit(solution)/shard_map/ppermute | solution.py:58
  107.1 11.2 %collective-permute-done.28.refs_1_ = bf16[512,1024]{1,0:T(8,128)(2,1)S(1)} collective-permute-done((bf16[512,1024]{1,0:T(8,128)(2,1)S(1)}, bf16[512,1024]{1,0:T(8,128)(2,1)S(1)}, u32[]{:S(2)}, u32[]{:S(2)}) %collective-permute-start.28) | collective-permute-done | bytes 1048608 | tf_op jit(solution)/shard_map/ppermute | solution.py:58
  118.4 3.3 collective-permute-start.35
  125.9 8.5 %collective-permute-done.30.refs_3_ = bf16[512,1024]{1,0:T(8,128)(2,1)S(1)} collective-permute-done((bf16[512,1024]{1,0:T(8,128)(2,1)S(1)}, bf16[512,1024]{1,0:T(8,128)(2,1)S(1)}, u32[]{:S(2)}, u32[]{:S(2)}) %collective-permute-start.30) | collective-permute-done | bytes 1048608 | tf_op jit(solution)/shard_map/ppermute | solution.py:58
  136.8 8.8 %collective-permute-done.33.refs_1_ = bf16[512,1024]{1,0:T(8,128)(2,1)S(1)} collective-permute-done((bf16[512,1024]{1,0:T(8,128)(2,1)S(1)}, bf16[512,1024]{1,0:T(8,128)(2,1)S(1)}, u32[]{:S(2)}, u32[]{:S(2)}) %collective-permute-start.33) | collective-permute-done | bytes 1048608 | tf_op jit(solution)/shard_map/ppermute | solution.py:58
  147.9 3.1 collective-permute-start.14
  154.4 9.5 %collective-permute-start.40 = (bf16[2048,256]{1,0:T(8,128)(2,1)S(1)}, bf16[2048,256]{1,0:T(8,128)(2,1)S(1)}, u32[]{:S(2)}, u32[]{:S(2)}) collective-permute-start(bf16[2048,256]{1,0:T(8,128)(2,1)S(1)} %slice.145), channel_id=1, source_target_pairs={{96,32},{97,33},{98,34},{99,35},{100,36},{101,37},{102,38},{103,39... | collective-permute-start | bytes 3145736 | tf_op jit(solution)/shard_map/ppermute | solution.py:425
  163.9 20.7 %collective-permute-done.40.refs_19_ = bf16[2048,256]{1,0:T(8,128)(2,1)S(1)} collective-permute-done((bf16[2048,256]{1,0:T(8,128)(2,1)S(1)}, bf16[2048,256]{1,0:T(8,128)(2,1)S(1)}, u32[]{:S(2)}, u32[]{:S(2)}) %collective-permute-start.40) | collective-permute-done | bytes 1048608 | tf_op jit(solution)/shard_map/ppermute | solution.py:425
  185.9 3.8 %shard_map.105 = (bf16[256,4096]{1,0:T(8,128)(2,1)S(1)}, bf16[256,4096]{1,0:T(8,128)(2,1)S(1)}) custom-call(s32[32]{0:T(128)S(1)} %pad_add_fusion.order_ref.refs_0_, s32[1]{0:T(128)} %bitcast.section_ref.refs_1_, bf16[256,4096]{1,0:T(8,128)(2,1)} %bitcast.79, bf16[256,4096]{1,0:T(8,128)(2,1)} %bitcast.76, f32[1,4096]{1,0:T(1,128)S(1)} %convert_element_type.36.gain_ref.refs_4_), custom_call_target="tpu_custom_call" | custom-call | flops 8388608 | bytes 8388608 | tf_op jit(solution)/shard_map/pallas_call | solution.py:429
  190.3 2.3 shard_map.108
  192.6 6.3 %shard_map.109.refs_8_ = bf16[256,1024]{1,0:T(8,128)(2,1)S(1)} custom-call(s32[2]{0:T(128)S(1)} %bitcast.68, s32[1]{0:T(128)} %bitcast.section_ref.refs_1_, f32[3]{0:T(128)S(1)} %bitcast_multiply_fusion.scale_ref.refs_3_, bf16[256,4096]{1,0:T(8,128)(2,1)S(1)} %get-tuple-element.11.xn_ref, bf16[2048,1280]{1,0:T(8,128)(2,1)} %shard_map.107.own_ref.refs_9_.refs_16_, ...), custom_call_target="tpu_custom_call" | custom-call | flops 2147483648 | bytes 8388608 | tf_op jit(solution)/shard_map/pallas_call | solution.py:191
  200.3 6.4 %shard_map.111.refs_9_ = bf16[256,1024]{1,0:T(8,128)(2,1)S(1)} custom-call(s32[2]{0:T(128)S(1)} %bitcast.69, s32[1]{0:T(128)} %bitcast.section_ref.refs_1_, f32[3]{0:T(128)S(1)} %bitcast_multiply_fusion.scale_ref.refs_3_, bf16[256,4096]{1,0:T(8,128)(2,1)S(1)} %get-tuple-element.11.xn_ref, bf16[2048,1024]{1,0:T(8,128)(2,1)} %shard_map.110.own_ref.refs_11_.refs_18_, ...), custom_call_target="tpu_custom_call" | custom-call | flops 2147483648 | bytes 8388608 | tf_op jit(solution)/shard_map/pallas_call | solution.py:191
  208.0 6.3 %shard_map.114.refs_10_ = bf16[256,1024]{1,0:T(8,128)(2,1)S(1)} custom-call(s32[2]{0:T(128)S(1)} %bitcast.70, s32[1]{0:T(128)} %bitcast.section_ref.refs_1_, f32[3]{0:T(128)S(1)} %bitcast_multiply_fusion.scale_ref.refs_3_, bf16[256,4096]{1,0:T(8,128)(2,1)S(1)} %get-tuple-element.11.xn_ref, bf16[2048,1024]{1,0:T(8,128)(2,1)} %shard_map.113.own_ref.refs_13_.refs_20_, ...), custom_call_target="tpu_custom_call" | custom-call | flops 2147483648 | bytes 8388608 | tf_op jit(solution)/shard_map/pallas_call | solution.py:191
  215.7 6.4 %shard_map.117.refs_11_ = bf16[256,1024]{1,0:T(8,128)(2,1)S(1)} custom-call(s32[2]{0:T(128)S(1)} %bitcast.71, s32[1]{0:T(128)} %bitcast.section_ref.refs_1_, f32[3]{0:T(128)S(1)} %bitcast_multiply_fusion.scale_ref.refs_3_, bf16[256,4096]{1,0:T(8,128)(2,1)S(1)} %get-tuple-element.11.xn_ref, bf16[2048,1024]{1,0:T(8,128)(2,1)} %shard_map.116.own_ref.refs_15_.refs_22_, ...), custom_call_target="tpu_custom_call" | custom-call | flops 2147483648 | bytes 8388608 | tf_op jit(solution)/shard_map/pallas_call | solution.py:191
  223.5 12.6 %collective-permute-done.22.refs_5_.refs_12_ = bf16[256,1024]{1,0:T(8,128)(2,1)S(1)} collective-permute-done((bf16[256,1024]{1,0:T(8,128)(2,1)S(1)}, bf16[256,1024]{1,0:T(8,128)(2,1)S(1)}, u32[]{:S(2)}, u32[]{:S(2)}) %collective-permute-start.22) | collective-permute-done | bytes 524320 | tf_op jit(solution)/shard_map/ppermute | solution.py:425
  236.1 11.2 %collective-permute-done.27.refs_6_.refs_13_ = bf16[256,1024]{1,0:T(8,128)(2,1)S(1)} collective-permute-done((bf16[256,1024]{1,0:T(8,128)(2,1)S(1)}, bf16[256,1024]{1,0:T(8,128)(2,1)S(1)}, u32[]{:S(2)}, u32[]{:S(2)}) %collective-permute-start.27) | collective-permute-done | bytes 524320 | tf_op jit(solution)/shard_map/ppermute | solution.py:425
  247.4 11.2 %collective-permute-done.32.refs_7_.refs_14_ = bf16[256,1024]{1,0:T(8,128)(2,1)S(1)} collective-permute-done((bf16[256,1024]{1,0:T(8,128)(2,1)S(1)}, bf16[256,1024]{1,0:T(8,128)(2,1)S(1)}, u32[]{:S(2)}, u32[]{:S(2)}) %collective-permute-start.32) | collective-permute-done | bytes 524320 | tf_op jit(solution)/shard_map/ppermute | solution.py:425
  258.6 10.6 %collective-permute-done.37.refs_8_.refs_15_ = bf16[256,1024]{1,0:T(8,128)(2,1)S(1)} collective-permute-done((bf16[256,1024]{1,0:T(8,128)(2,1)S(1)}, bf16[256,1024]{1,0:T(8,128)(2,1)S(1)}, u32[]{:S(2)}, u32[]{:S(2)}) %collective-permute-start.37) | collective-permute-done | bytes 524320 | tf_op jit(solution)/shard_map/ppermute | solution.py:425
  274.1 31.6 %collective-permute-done.43 = bf16[256,512]{1,0:T(8,128)(2,1)S(1)} collective-permute-done((bf16[256,512]{1,0:T(8,128)(2,1)S(1)}, bf16[256,512]{1,0:T(8,128)(2,1)S(1)}, u32[]{:S(2)}, u32[]{:S(2)}) %collective-permute-start.43) | collective-permute-done | bytes 262176 | tf_op jit(solution)/shard_map/ppermute | solution.py:425
  305.8 24.0 %shard_map.119 = bf16[256,4096]{1,0:T(8,128)(2,1)} custom-call(s32[32]{0:T(128)S(1)} %pad_add_fusion.order_ref.refs_0_, s32[1]{0:T(128)} %bitcast.section_ref.refs_1_, s32[2]{0:T(128)S(1)} %bitcast.73, f32[3]{0:T(128)S(1)} %bitcast_multiply_fusion.scale_ref.refs_3_, f32[1,4096]{1,0:T(1,128)S(1)} %convert_element_type.36.gain_ref.refs_4_, ...), custom_call_target="tpu_custom_call" | custom-call | flops 8589934592 | bytes 33554432 | tf_op jit(solution)/shard_map/pallas_call | solution.py:515
  (136 shorter events, 63.8 us)
Async XLA Ops:
  21.7 10.3 %collective-permute-start.15 = (bf16[128,1280]{1,0:T(8,128)(2,1)S(1)}, bf16[128,1280]{1,0:T(8,128)(2,1)S(1)}, u32[]{:S(2)}, u32[]{:S(2)}) collective-permute-start(bf16[128,1280]{1,0:T(8,128)(2,1)S(1)} %pad_maximum_fusion.refs_0_), channel_id=1, source_target_pairs={{0,2},{1,9},{2,4},{3,11},{4,6},{5,13},{6,0},{7,15},{8,10},{9,17},{... | collective-permute-start | bytes 983048 | tf_op jit(solution)/shard_map/ppermute | solution.py:58
  23.4 31.2 %collective-permute-start.1 = (bf16[128,3072]{1,0:T(8,128)(2,1)S(1)}, bf16[128,3072]{1,0:T(8,128)(2,1)}, u32[]{:S(2)}, u32[]{:S(2)}) collective-permute-start(bf16[128,3072]{1,0:T(8,128)(2,1)S(1)} %slice.118), channel_id=1, source_target_pairs={{0,6},{1,25},{2,0},{3,27},{4,2},{5,29},{6,4},{7,31},{8,14},{9,1},{... | collective-permute-start | bytes 2359304 | tf_op jit(solution)/shard_map/ppermute | solution.py:58
  29.9 22.8 %collective-permute-start.16 = (bf16[128,1280]{1,0:T(8,128)(2,1)S(1)}, bf16[128,1280]{1,0:T(8,128)(2,1)S(1)}, u32[]{:S(2)}, u32[]{:S(2)}) collective-permute-start(bf16[128,1280]{1,0:T(8,128)(2,1)S(1)} %pad_maximum_fusion.refs_0_), channel_id=1, source_target_pairs={{0,6},{1,25},{2,0},{3,27},{4,2},{5,29},{6,4},{7,31},{8,14},{9,1},{... | collective-permute-start | bytes 983048 | tf_op jit(solution)/shard_map/ppermute | solution.py:58
  32.0 20.7 %collective-permute-start.17 = (bf16[128,1280]{1,0:T(8,128)(2,1)S(1)}, bf16[128,1280]{1,0:T(8,128)(2,1)S(1)}, u32[]{:S(2)}, u32[]{:S(2)}) collective-permute-start(bf16[128,1280]{1,0:T(8,128)(2,1)S(1)} %collective-permute-done.15.refs_1_), channel_id=1, source_target_pairs={{0,2},{1,9},{2,4},{3,11},{4,6},{5,13},{6,0},{7,15},{8,10},{9,17},{... | collective-permute-start | bytes 983048 | tf_op jit(solution)/shard_map/ppermute | solution.py:58
  32.0 8.4 %collective-permute-start.9 = (f32[3,128]{0,1:T(8,128)S(1)}, f32[3,128]{0,1:T(8,128)S(1)}, u32[]{:S(2)}, u32[]{:S(2)}) collective-permute-start(f32[3,128]{0,1:T(8,128)S(1)} %broadcast_add_fusion), channel_id=1, source_target_pairs={{0,2},{1,3},{2,0},{3,1},{4,6},{5,7},{6,4},{7,5},{8,10},{9,11},{10,... | collective-permute-start | bytes 4616 | tf_op jit(solution)/shard_map/ppermute | solution.py:58
  32.4 28.0 %collective-permute-start = (bf16[128,3072]{1,0:T(8,128)(2,1)S(1)}, bf16[128,3072]{1,0:T(8,128)(2,1)S(1)}, u32[]{:S(2)}, u32[]{:S(2)}) collective-permute-start(bf16[128,3072]{1,0:T(8,128)(2,1)S(1)} %slice.118), channel_id=1, source_target_pairs={{0,2},{1,9},{2,4},{3,11},{4,6},{5,13},{6,0},{7,15},{8,10},{9,17},{... | collective-permute-start | bytes 2359304 | tf_op jit(solution)/shard_map/ppermute | solution.py:58
  53.2 23.9 %collective-permute-start.18 = (bf16[512,1280]{1,0:T(8,128)(2,1)S(1)}, bf16[512,1280]{1,0:T(8,128)(2,1)S(1)}, u32[]{:S(2)}, u32[]{:S(2)}) collective-permute-start(bf16[512,1280]{1,0:T(8,128)(2,1)S(1)} %shard_map.106.refs_0_), channel_id=1, source_target_pairs={{0,8},{1,3},{2,10},{3,5},{4,12},{5,7},{6,14},{7,1},{8,16},{9,11},{... | collective-permute-start | bytes 3932168 | tf_op jit(solution)/shard_map/ppermute | solution.py:58
  54.6 20.1 %collective-permute-start.2 = (bf16[128,3072]{1,0:T(8,128)(2,1)}, bf16[128,3072]{1,0:T(8,128)(2,1)S(1)}, u32[]{:S(2)}, u32[]{:S(2)}) collective-permute-start(bf16[128,3072]{1,0:T(8,128)(2,1)} %collective-permute-done.1), channel_id=1, source_target_pairs={{0,6},{1,25},{2,0},{3,27},{4,2},{5,29},{6,4},{7,31},{8,14},{9,1},{... | collective-permute-start | bytes 2359304 | tf_op jit(solution)/shard_map/ppermute | solution.py:58
  57.2 22.8 %collective-permute-start.19 = (bf16[512,1280]{1,0:T(8,128)(2,1)S(1)}, bf16[512,1280]{1,0:T(8,128)(2,1)S(1)}, u32[]{:S(2)}, u32[]{:S(2)}) collective-permute-start(bf16[512,1280]{1,0:T(8,128)(2,1)S(1)} %shard_map.106.refs_0_), channel_id=1, source_target_pairs={{0,24},{1,7},{2,26},{3,1},{4,28},{5,3},{6,30},{7,5},{8,0},{9,15},{... | collective-permute-start | bytes 3932168 | tf_op jit(solution)/shard_map/ppermute | solution.py:58
  74.9 15.2 %collective-permute-start.24 = (bf16[512,1024]{1,0:T(8,128)(2,1)S(1)}, bf16[512,1024]{1,0:T(8,128)(2,1)S(1)}, u32[]{:S(2)}, u32[]{:S(2)}) collective-permute-start(bf16[512,1024]{1,0:T(8,128)(2,1)S(1)} %shard_map.104.refs_0_), channel_id=1, source_target_pairs={{0,24},{1,7},{2,26},{3,1},{4,28},{5,3},{6,30},{7,5},{8,0},{9,15},{... | collective-permute-start | bytes 3145736 | tf_op jit(solution)/shard_map/ppermute | solution.py:58
  77.1 18.8 %collective-permute-start.20 = (bf16[512,1280]{1,0:T(8,128)(2,1)S(1)}, bf16[512,1280]{1,0:T(8,128)(2,1)S(1)}, u32[]{:S(2)}, u32[]{:S(2)}) collective-permute-start(bf16[512,1280]{1,0:T(8,128)(2,1)S(1)} %collective-permute-done.18.refs_1_), channel_id=1, source_target_pairs={{0,8},{1,3},{2,10},{3,5},{4,12},{5,7},{6,14},{7,1},{8,16},{9,11},{... | collective-permute-start | bytes 3932168 | tf_op jit(solution)/shard_map/ppermute | solution.py:58
  77.1 30.1 %collective-permute-start.23 = (bf16[512,1024]{1,0:T(8,128)(2,1)S(1)}, bf16[512,1024]{1,0:T(8,128)(2,1)S(1)}, u32[]{:S(2)}, u32[]{:S(2)}) collective-permute-start(bf16[512,1024]{1,0:T(8,128)(2,1)S(1)} %shard_map.104.refs_0_), channel_id=1, source_target_pairs={{0,8},{1,3},{2,10},{3,5},{4,12},{5,7},{6,14},{7,1},{8,16},{9,11},{... | collective-permute-start | bytes 3145736 | tf_op jit(solution)/shard_map/ppermute | solution.py:58
  77.9 40.5 %collective-permute-start.28 = (bf16[512,1024]{1,0:T(8,128)(2,1)S(1)}, bf16[512,1024]{1,0:T(8,128)(2,1)S(1)}, u32[]{:S(2)}, u32[]{:S(2)}) collective-permute-start(bf16[512,1024]{1,0:T(8,128)(2,1)S(1)} %shard_map.112.refs_0_), channel_id=1, source_target_pairs={{0,8},{1,3},{2,10},{3,5},{4,12},{5,7},{6,14},{7,1},{8,16},{9,11},{... | collective-permute-start | bytes 3145736 | tf_op jit(solution)/shard_map/ppermute | solution.py:58
  80.0 38.4 %collective-permute-start.34 = (bf16[512,1024]{1,0:T(8,128)(2,1)S(1)}, bf16[512,1024]{1,0:T(8,128)(2,1)S(1)}, u32[]{:S(2)}, u32[]{:S(2)}) collective-permute-start(bf16[512,1024]{1,0:T(8,128)(2,1)S(1)} %shard_map.115.refs_0_), channel_id=1, source_target_pairs={{0,24},{1,7},{2,26},{3,1},{4,28},{5,3},{6,30},{7,5},{8,0},{9,15},{... | collective-permute-start | bytes 3145736 | tf_op jit(solution)/shard_map/ppermute | solution.py:58
  90.1 28.3 %collective-permute-start.25 = (bf16[512,1024]{1,0:T(8,128)(2,1)S(1)}, bf16[512,1024]{1,0:T(8,128)(2,1)S(1)}, u32[]{:S(2)}, u32[]{:S(2)}) collective-permute-start(bf16[512,1024]{1,0:T(8,128)(2,1)S(1)} %collective-permute-done.24.refs_2_), channel_id=1, source_target_pairs={{0,24},{1,7},{2,26},{3,1},{4,28},{5,3},{6,30},{7,5},{8,0},{9,15},{... | collective-permute-start | bytes 3145736 | tf_op jit(solution)/shard_map/ppermute | solution.py:58
  98.3 91.5 %collective-permute-start.21 = (bf16[2048,1280]{1,0:T(8,128)(2,1)}, bf16[2048,1280]{1,0:T(8,128)(2,1)}, u32[]{:S(2)}, u32[]{:S(2)}) collective-permute-start(bf16[2048,1280]{1,0:T(8,128)(2,1)} %shard_map.107.own_ref.refs_9_.refs_16_), channel_id=1, source_target_pairs={{0,1},{1,0},{2,3},{3,2},{4,5},{5,4},{6,7},{7,6},{8,9},{9,8},{10,11... | collective-permute-start | bytes 15728648 | tf_op jit(solution)/shard_map/ppermute | solution.py:58
  107.1 16.6 %collective-permute-start.29 = (bf16[512,1024]{1,0:T(8,128)(2,1)S(1)}, bf16[512,1024]{1,0:T(8,128)(2,1)S(1)}, u32[]{:S(2)}, u32[]{:S(2)}) collective-permute-start(bf16[512,1024]{1,0:T(8,128)(2,1)S(1)} %shard_map.112.refs_0_), channel_id=1, source_target_pairs={{0,24},{1,7},{2,26},{3,1},{4,28},{5,3},{6,30},{7,5},{8,0},{9,15},{... | collective-permute-start | bytes 3145736 | tf_op jit(solution)/shard_map/ppermute | solution.py:58
  118.4 16.0 %collective-permute-start.30 = (bf16[512,1024]{1,0:T(8,128)(2,1)S(1)}, bf16[512,1024]{1,0:T(8,128)(2,1)S(1)}, u32[]{:S(2)}, u32[]{:S(2)}) collective-permute-start(bf16[512,1024]{1,0:T(8,128)(2,1)S(1)} %collective-permute-done.28.refs_1_), channel_id=1, source_target_pairs={{0,8},{1,3},{2,10},{3,5},{4,12},{5,7},{6,14},{7,1},{8,16},{9,11},{... | collective-permute-start | bytes 3145736 | tf_op jit(solution)/shard_map/ppermute | solution.py:58
  118.4 27.2 %collective-permute-start.33 = (bf16[512,1024]{1,0:T(8,128)(2,1)S(1)}, bf16[512,1024]{1,0:T(8,128)(2,1)S(1)}, u32[]{:S(2)}, u32[]{:S(2)}) collective-permute-start(bf16[512,1024]{1,0:T(8,128)(2,1)S(1)} %shard_map.115.refs_0_), channel_id=1, source_target_pairs={{0,8},{1,3},{2,10},{3,5},{4,12},{5,7},{6,14},{7,1},{8,16},{9,11},{... | collective-permute-start | bytes 3145736 | tf_op jit(solution)/shard_map/ppermute | solution.py:58
  118.4 27.2 %collective-permute-start.35 = (bf16[512,1024]{1,0:T(8,128)(2,1)S(1)}, bf16[512,1024]{1,0:T(8,128)(2,1)S(1)}, u32[]{:S(2)}, u32[]{:S(2)}) collective-permute-start(bf16[512,1024]{1,0:T(8,128)(2,1)S(1)} %collective-permute-done.34.refs_2_), channel_id=1, source_target_pairs={{0,24},{1,7},{2,26},{3,1},{4,28},{5,3},{6,30},{7,5},{8,0},{9,15},{... | collective-permute-start | bytes 3145736 | tf_op jit(solution)/shard_map/ppermute | solution.py:58
  123.8 75.2 %collective-permute-start.26 = (bf16[2048,1024]{1,0:T(8,128)(2,1)}, bf16[2048,1024]{1,0:T(8,128)(2,1)}, u32[]{:S(2)}, u32[]{:S(2)}) collective-permute-start(bf16[2048,1024]{1,0:T(8,128)(2,1)} %shard_map.110.own_ref.refs_11_.refs_18_), channel_id=1, source_target_pairs={{0,1},{1,0},{2,3},{3,2},{4,5},{5,4},{6,7},{7,6},{8,9},{9,8},{10,11... | collective-permute-start | bytes 12582920 | tf_op jit(solution)/shard_map/ppermute | solution.py:58
  136.5 70.2 %collective-permute-start.31 = (bf16[2048,1024]{1,0:T(8,128)(2,1)}, bf16[2048,1024]{1,0:T(8,128)(2,1)}, u32[]{:S(2)}, u32[]{:S(2)}) collective-permute-start(bf16[2048,1024]{1,0:T(8,128)(2,1)} %shard_map.113.own_ref.refs_13_.refs_20_), channel_id=1, source_target_pairs={{0,1},{1,0},{2,3},{3,2},{4,5},{5,4},{6,7},{7,6},{8,9},{9,8},{10,11... | collective-permute-start | bytes 12582920 | tf_op jit(solution)/shard_map/ppermute | solution.py:58
  147.7 66.6 %collective-permute-start.36 = (bf16[2048,1024]{1,0:T(8,128)(2,1)}, bf16[2048,1024]{1,0:T(8,128)(2,1)}, u32[]{:S(2)}, u32[]{:S(2)}) collective-permute-start(bf16[2048,1024]{1,0:T(8,128)(2,1)} %shard_map.116.own_ref.refs_15_.refs_22_), channel_id=1, source_target_pairs={{0,1},{1,0},{2,3},{3,2},{4,5},{5,4},{6,7},{7,6},{8,9},{9,8},{10,11... | collective-permute-start | bytes 12582920 | tf_op jit(solution)/shard_map/ppermute | solution.py:58
  154.4 30.2 %collective-permute-start.40 = (bf16[2048,256]{1,0:T(8,128)(2,1)S(1)}, bf16[2048,256]{1,0:T(8,128)(2,1)S(1)}, u32[]{:S(2)}, u32[]{:S(2)}) collective-permute-start(bf16[2048,256]{1,0:T(8,128)(2,1)S(1)} %slice.145), channel_id=1, source_target_pairs={{96,32},{97,33},{98,34},{99,35},{100,36},{101,37},{102,38},{103,39... | collective-permute-start | bytes 3145736 | tf_op jit(solution)/shard_map/ppermute | solution.py:425
  185.8 36.2 %collective-permute-start.41 = (bf16[2048,256]{1,0:T(8,128)(2,1)S(1)}, bf16[2048,256]{1,0:T(8,128)(2,1)S(1)}, u32[]{:S(2)}, u32[]{:S(2)}) collective-permute-start(bf16[2048,256]{1,0:T(8,128)(2,1)S(1)} %collective-permute-done.40.refs_19_), channel_id=1, source_target_pairs={{0,1},{1,0},{2,3},{3,2},{4,5},{5,4},{6,7},{7,6},{8,9},{9,8},{10,11... | collective-permute-start | bytes 3145736 | tf_op jit(solution)/shard_map/ppermute | solution.py:58
  189.8 33.7 %collective-permute-start.39 = (bf16[2048,256]{1,0:T(8,128)(2,1)S(1)}, bf16[2048,256]{1,0:T(8,128)(2,1)S(1)}, u32[]{:S(2)}, u32[]{:S(2)}) collective-permute-start(bf16[2048,256]{1,0:T(8,128)(2,1)S(1)} %collective-permute-done.38.refs_17_), channel_id=1, source_target_pairs={{0,1},{1,0},{2,3},{3,2},{4,5},{5,4},{6,7},{7,6},{8,9},{9,8},{10,11... | collective-permute-start | bytes 3145736 | tf_op jit(solution)/shard_map/ppermute | solution.py:58
  199.0 37.1 %collective-permute-start.22 = (bf16[256,1024]{1,0:T(8,128)(2,1)S(1)}, bf16[256,1024]{1,0:T(8,128)(2,1)S(1)}, u32[]{:S(2)}, u32[]{:S(2)}) collective-permute-start(bf16[256,1024]{1,0:T(8,128)(2,1)S(1)} %shard_map.109.refs_8_), channel_id=1, source_target_pairs={{0,32},{64,96},{1,33},{65,97},{2,34},{66,98},{3,35},{67,99},{4,36}... | collective-permute-start | bytes 1572872 | tf_op jit(solution)/shard_map/ppermute | solution.py:425
  206.7 40.7 %collective-permute-start.27 = (bf16[256,1024]{1,0:T(8,128)(2,1)S(1)}, bf16[256,1024]{1,0:T(8,128)(2,1)S(1)}, u32[]{:S(2)}, u32[]{:S(2)}) collective-permute-start(bf16[256,1024]{1,0:T(8,128)(2,1)S(1)} %shard_map.111.refs_9_), channel_id=1, source_target_pairs={{0,32},{64,96},{1,33},{65,97},{2,34},{66,98},{3,35},{67,99},{4,36}... | collective-permute-start | bytes 1572872 | tf_op jit(solution)/shard_map/ppermute | solution.py:425
  214.4 44.2 %collective-permute-start.32 = (bf16[256,1024]{1,0:T(8,128)(2,1)S(1)}, bf16[256,1024]{1,0:T(8,128)(2,1)S(1)}, u32[]{:S(2)}, u32[]{:S(2)}) collective-permute-start(bf16[256,1024]{1,0:T(8,128)(2,1)S(1)} %shard_map.114.refs_10_), channel_id=1, source_target_pairs={{0,32},{64,96},{1,33},{65,97},{2,34},{66,98},{3,35},{67,99},{4,36}... | collective-permute-start | bytes 1572872 | tf_op jit(solution)/shard_map/ppermute | solution.py:425
  222.0 47.2 %collective-permute-start.37 = (bf16[256,1024]{1,0:T(8,128)(2,1)S(1)}, bf16[256,1024]{1,0:T(8,128)(2,1)S(1)}, u32[]{:S(2)}, u32[]{:S(2)}) collective-permute-start(bf16[256,1024]{1,0:T(8,128)(2,1)S(1)} %shard_map.117.refs_11_), channel_id=1, source_target_pairs={{0,32},{64,96},{1,33},{65,97},{2,34},{66,98},{3,35},{67,99},{4,36}... | collective-permute-start | bytes 1572872 | tf_op jit(solution)/shard_map/ppermute | solution.py:425
  271.5 34.2 %collective-permute-start.43 = (bf16[256,512]{1,0:T(8,128)(2,1)S(1)}, bf16[256,512]{1,0:T(8,128)(2,1)S(1)}, u32[]{:S(2)}, u32[]{:S(2)}) collective-permute-start(bf16[256,512]{1,0:T(8,128)(2,1)S(1)} %get-tuple-element.16), channel_id=1, source_target_pairs={{32,96},{33,97},{34,98},{35,99},{36,100},{37,101},{38,102},{39,103... | collective-permute-start | bytes 786440 | tf_op jit(solution)/shard_map/ppermute | solution.py:425
  272.8 33.0 %collective-permute-start.42 = (bf16[256,512]{1,0:T(8,128)(2,1)S(1)}, bf16[256,512]{1,0:T(8,128)(2,1)S(1)}, u32[]{:S(2)}, u32[]{:S(2)}) collective-permute-start(bf16[256,512]{1,0:T(8,128)(2,1)S(1)} %get-tuple-element.16), channel_id=1, source_target_pairs={{32,64},{33,65},{34,66},{35,67},{36,68},{37,69},{38,70},{39,71},{4... | collective-permute-start | bytes 786440 | tf_op jit(solution)/shard_map/ppermute | solution.py:425
  (19 other events, 203.4 us)
where the time goes:
time: 331 us; the launch traced here: 330 us
  waiting for transfers between devices  181 us (55%)
  starting transfers between devices  67.5 us (20%)
  Pallas kernels  67.2 us (20%)
  local copies, waits for them, and re-layouts  4.65 us (1%)
  between operations  3.52 us (1%)
    ppermute x10, waiting for transfers between devices, shards(): hop = lambda value, pairs: lax.ppermute(value, 'section', pairs)  99.5 us
    ppermute x34, waiting for transfers between devices, send(): return lax.ppermute(value, 'fsdp', pairs)  81.6 us
    ppermute x34, starting transfers between devices, send(): return lax.ppermute(value, 'fsdp', pairs)  46.4 us
    pallas_call x4, Pallas kernels, layer_part(): pl.pallas_call(part_kernel, grid=(width // block,), out_shape=jax.ShapeDt...  25.4 us
    pallas_call x1, Pallas kernels, shards(): pl.pallas_call(decoder_kernel, out_shape=row_shape, in_specs=[SMEM] * 4 +...  24 us
    ppermute x10, starting transfers between devices, shards(): hop = lambda value, pairs: lax.ppermute(value, 'section', pairs)  21.1 us
    pallas_call x8, Pallas kernels, stack(): pl.pallas_call(functools.partial(stack_kernel, count), out_shape=jax.Shap...  9.44 us
  transfers between devices with their start and end apart: 44, of which 22 were waited for; matrix products, arithmetic and copies ran while one was open for 2% of the time, Pallas kernels for 12%

commit v1 on v0

--- a/solution.py
+++ b/solution.py
@@ -58,11 +58,17 @@
     return lax.ppermute(value, "fsdp", pairs)
 
 
-def ring(block, move, forward):
-    before = send(block, move(1))
-    after = send(block, move(-1))
-    far = send(before, move(1)) if forward else send(after, move(-1))
-    return [block, before, after, far]
+def behind(value, *others):
+    return lax.optimization_barrier((value, *others))[0]
+
+
+def near(block, move):
+    return [block, send(block, move(1)), send(block, move(-1))]
+
+
+def ring(blocks, move, forward, *first):
+    far = send(behind(blocks[1], *first), move(1)) if forward else send(behind(blocks[2], *first), move(-1))
+    return blocks + [far]
 
 
 def row_order():
@@ -80,8 +86,10 @@
     return jnp.concatenate([order(core), order(1 - core)]).astype(jnp.int32)
 
 
-def total(value):
-    for pairs in DOUBLING:
+def total(value, blocks):
+    for i, pairs in enumerate(DOUBLING):
+        if i == 3:
+            value = behind(value, *blocks)
         value = value + send(value, pairs)
     return value
 
@@ -91,7 +99,8 @@
 
 
 def cost(flops, size, exps=0):
-    return pl.CostEstimate(flops=int(flops), bytes_accessed=int(size), transcendentals=int(exps))
+    share = 64
+    return pl.CostEstimate(flops=int(flops) // share, bytes_accessed=int(size) // share, transcendentals=int(exps) // share)
 
 
 def stack_kernel(count, *refs):
@@ -130,7 +139,7 @@
         xn_ref[:, k * 128 : (k + 1) * 128] = part.astype(BF16)
 
 
-def attend(q, keys_ref, values_ref, resid, lengths_ref):
+def attend(q, keys_ref, values_ref, resid, lengths_ref, key_scale, value_scale):
     seqs, heads = q.shape[0] // 128, q.shape[1] // HEAD
     position = lax.broadcasted_iota(jnp.int32, (heads * 128, 128), 1)
     made = []
@@ -140,17 +149,17 @@
         scores = lax.dot_general(
             stacked, keys_ref[rows, :], (((1,), (1,)), ((), ())), preferred_element_type=F32
         )
-        expd = jnp.where(position < lengths_ref[m], jnp.exp2(scores * LOG2E_SCALED), 0.0)
+        expd = jnp.where(position < lengths_ref[m], jnp.exp2(scores * (key_scale * LOG2E_SCALED)), 0.0)
         probs = (expd * (1.0 / jnp.sum(expd, axis=-1, keepdims=True))).astype(BF16)
-        context = dot(probs, values_ref[rows, :])
+        context = dot(probs, values_ref[rows, :]) * value_scale
         made.append(jnp.concatenate([context[h * 128 : (h + 1) * 128] for h in range(heads)], 1))
     return (resid.astype(F32) + jnp.concatenate(made, 0)).astype(BF16)
 
 
-def project_into(keys_ref, values_ref, xn_ref, kv, key_scale, value_scale):
-    projected = dot(xn_ref[...], kv)
-    keys_ref[...] = (projected[:, :HEAD] * key_scale).astype(BF16)
-    values_ref[...] = (projected[:, HEAD:] * value_scale).astype(BF16)
+def project_into(keys_ref, values_ref, xn_ref, kv):
+    projected = dot(xn_ref[...], kv).astype(BF16)
+    keys_ref[...] = projected[:, :HEAD]
+    values_ref[...] = projected[:, HEAD:]
 
 
 def enter_kernel(order_ref, section_ref, source_ref, target_ref, gain_ref, x_ref, xn_ref):
@@ -165,9 +174,8 @@
     norm_into(xn_ref, x_ref, gain_ref, 0, order_ref)
 
 
-def project_kernel(scale_ref, xn_ref, own_ref, other_ref, keys_ref, values_ref):
-    kv = jnp.concatenate([own_ref[...], other_ref[...]], 0)
-    project_into(keys_ref, values_ref, xn_ref, kv, scale_ref[1], scale_ref[2])
+def project_kernel(xn_ref, own_ref, other_ref, keys_ref, values_ref):
+    project_into(keys_ref, values_ref, xn_ref, jnp.concatenate([own_ref[...], other_ref[...]], 0))
 
 
 def part_kernel(lengths_ref, section_ref, scale_ref, xn_ref, own_ref, other_ref, k_ref, v_ref, x_ref, out_ref):
@@ -177,7 +185,7 @@
 
     @pl.when(section_ref[0] != 2)
     def _():
-        out_ref[...] = attend(q, k_ref, v_ref, x_ref[...], lengths_ref)
+        out_ref[...] = attend(q, k_ref, v_ref, x_ref[...], lengths_ref, scale_ref[1], scale_ref[2])
 
     @pl.when(section_ref[0] == 2)
     def _():
@@ -209,7 +217,7 @@
     )(lengths, section, scales, xn, own, other, keys, values, x)
 
 
-def stream_layer(parts, buf, sems, xn_ref, q_ref, k_ref, v_ref, x_ref, lengths_ref, scale, out_ref):
+def stream_layer(parts, buf, sems, xn_ref, q_ref, k_ref, v_ref, x_ref, lengths_ref, scale_ref, out_ref):
     half = buf.shape[1] // 2
     firsts = [0]
     for width in PARTS:
@@ -241,7 +249,9 @@
 
         def emit(b):
             columns = pl.ds(pl.multiple_of(b * BLOCK, BLOCK), BLOCK)
-            out_ref[:, columns] = attend(q_ref[...], k_ref, v_ref, x_ref[:, columns], lengths_ref)
+            out_ref[:, columns] = attend(
+                q_ref[...], k_ref, v_ref, x_ref[:, columns], lengths_ref, scale_ref[1], scale_ref[2]
+            )
 
         def step(b, carry):
             slot = lax.rem(b, SLOTS)
@@ -254,7 +264,7 @@
 
             acc = dot(xn_ref[...], buf[slot])
             emit(jnp.maximum(b - 1, 0))
-            q_ref[...] = (acc * scale).astype(BF16)
+            q_ref[...] = (acc * scale_ref[0]).astype(BF16)
             return carry
 
         lax.fori_loop(0, blocks, step, 0)
@@ -278,32 +288,27 @@
     pieces = refs[5 : 5 + n]
     flat = refs[5 + n : 5 + 3 * n]
     parts = [(flat[2 * i], flat[2 * i + 1]) for i in range(n)]
-    kv_refs = refs[5 + 3 * n : 9 + 3 * n]
-    out_ref, cross_ref = refs[9 + 3 * n : 11 + 3 * n]
-    buf, sems, kv_buf, kv_sems, x_ref, x_sems, xn_ref, q_ref, k_ref, v_ref = refs[11 + 3 * n :]
+    out_ref, cross_ref = refs[5 + 3 * n : 7 + 3 * n]
+    buf, sems, kv_buf, kv_sems, x_ref, x_sems, xn_ref, q_ref, k_ref, v_ref = refs[7 + 3 * n :]
     half = kv_buf.shape[1] // 2
-    kv_at = pl.ds(PARTS[0], 2 * HEAD)
 
     @pl.when(section_ref[0] == 1)
     def _():
         arrive = bring(pieces, x_ref, x_sems)
         for copy in arrive:
             copy.start()
-        kv_parts = [
-            (parts[0][0].at[:, kv_at], parts[0][1].at[:, kv_at]),
-            (kv_refs[0], kv_refs[1]),
-            (kv_refs[2], kv_refs[3]),
-        ]
         kv_copies = []
-        for i, halves in enumerate(kv_parts):
-            for c, ref in enumerate(halves):
+        for i, (part, at) in enumerate(((0, PARTS[0]), (1, PARTS[1]), (1, PARTS[1] + 2 * HEAD))):
+            for c, ref in enumerate(parts[part]):
                 kv_copies.append(
-                    pltpu.make_async_copy(ref, kv_buf.at[i, pl.ds(c * half, half)], kv_sems.at[i, c])
+                    pltpu.make_async_copy(
+                        ref.at[:, pl.ds(at, 2 * HEAD)], kv_buf.at[i, pl.ds(c * half, half)], kv_sems.at[i, c]
+                    )
                 )
         for copy in kv_copies[:2]:
             copy.start()
         start, run = stream_layer(
-            parts, buf, sems, xn_ref, q_ref, k_ref, v_ref, x_ref, lengths_ref, scale_ref[0], out_ref
+            parts, buf, sems, xn_ref, q_ref, k_ref, v_ref, x_ref, lengths_ref, scale_ref, out_ref
         )
         start()
         for copy in kv_copies[2:]:
@@ -313,7 +318,7 @@
         norm_into(xn_ref, x_ref, gain_ref, 0, order_ref)
         for copy in kv_copies[:2]:
             copy.wait()
-        project_into(k_ref, v_ref, xn_ref, kv_buf[0], scale_ref[1], scale_ref[2])
+        project_into(k_ref, v_ref, xn_ref, kv_buf[0])
         run()
         for copy in kv_copies[2:]:
             copy.wait()
@@ -325,8 +330,6 @@
                 cross_ref.at[:, pl.ds(at + HEAD, HEAD)],
                 xn_ref,
                 kv_buf[i],
-                scale_ref[3 * i + 1],
-                scale_ref[3 * i + 2],
             )
 
 
@@ -353,7 +356,9 @@
     def attend_all(resid_ref, into):
         def step(b, carry):
             columns = pl.ds(pl.multiple_of(b * BLOCK, BLOCK), BLOCK)
-            into[:, columns] = attend(x_ref[:, columns], cols(0), cols(1), resid_ref[:, columns], lengths_ref)
+            into[:, columns] = attend(
+                x_ref[:, columns], cols(0), cols(1), resid_ref[:, columns], lengths_ref, scale_ref[4], scale_ref[5]
+            )
             return carry
 
         lax.fori_loop(0, blocks, step, 0)
@@ -374,7 +379,7 @@
     @pl.when(section == 3)
     def _():
         start, run = stream_layer(
-            parts, buf, sems, xn_ref, q_ref, cols(2), cols(3), mid_ref, lengths_ref, scale_ref[0], out_ref
+            parts, buf, sems, xn_ref, q_ref, cols(2), cols(3), mid_ref, lengths_ref, scale_ref, out_ref
         )
         copies = bring(passed, x_ref, x_sems)
         for copy in copies:
@@ -391,11 +396,14 @@
     return (along * lax.rsqrt(jnp.sum(along * along) + EPS)).astype(BF16)
 
 
-def spectral(weight, kv_part, start_rows, gamma):
-    width = weight.shape[1]
+def spectral_along(weight, kv_part, start_rows, block):
     of_kv = dot(start_rows, kv_part)
     parts = jnp.concatenate([dot(start_rows[0:1], weight)[0], of_kv[1, :HEAD], of_kv[2, HEAD:]])
-    along = total(parts.reshape(-1, 128)).reshape(-1)
+    return total(parts.reshape(-1, 128), block).reshape(-1)
+
+
+def spectral_scales(weight, kv_part, along, gamma, block):
+    width = weight.shape[1]
     images = jnp.stack(
         [
             dot(weight, unit_direction(along[:width])),
@@ -404,9 +412,9 @@
         ]
     )
     squares = jnp.sum(images * images, axis=1)
-    totals = total(jnp.broadcast_to(squares[:, None], (3, 128)))[:, 0]
+    totals = total(jnp.broadcast_to(squares[:, None], (3, 128)), block)[:, 0]
     sigmas = jnp.sqrt(totals + EPS)
-    return gamma / sigmas, images / sigmas[:, None], along
+    return gamma / sigmas, images / sigmas[:, None]
 
 
 def shards(weights, kv_weights, gammas, gains, starts, source, target, lengths):
@@ -424,7 +432,24 @@
 
     hop = lambda value, pairs: lax.ppermute(value, "section", pairs)
     order = row_order()
-    scales, next_part, along = spectral(weight, kv_part, start_rows, gamma)
+
+    ends = [sum(PARTS[: i + 1]) for i in range(len(PARTS))]
+    head_block = jnp.concatenate([weight[:, : ends[0]], kv_part], 1)
+    head_line = ring(near(head_block, first_move), first_move, True)
+    extra = jnp.concatenate([kv_part, gain.reshape(-1, 2 * HEAD)], 0)
+    extra2 = hop(extra, [(2, 1)])
+    extra3 = hop(extra, [(3, 1)])
+    local = kv_part.shape[0]
+    tail_block = jnp.concatenate(
+        [weight[:, ends[0] : ends[1]], extra2[:local], extra3[:local], weight[:, ends[1] :]], 1
+    )
+    tail_line = ring(near(behind(tail_block, head_line[1], head_line[2]), first_move), first_move, False)
+
+    def line_of(i):
+        if i == 0:
+            return stack(head_line)
+        low, high = ends[i - 1] - ends[0], ends[i] - ends[0] + 4 * HEAD
+        return stack([a[:, (low if i == 1 else low + 4 * HEAD) : high] for a in tail_line])
 
     x0, xn0 = pl.pallas_call(
         enter_kernel,
@@ -435,31 +460,30 @@
         cost_estimate=cost(8 * rows * width, 8 * rows * width),
     )(order, section, source2, target2, wide_gain)
 
-    ends = [sum(PARTS[: i + 1]) for i in range(len(PARTS))]
-    head_block = jnp.concatenate([weight[:, : ends[0]], kv_part], 1)
-    tail_block = weight[:, ends[0] :]
-    head_line = ring(head_block, first_move, True)
-    tail_block, _ = lax.optimization_barrier((tail_block, along))
-    tail_line = ring(tail_block, first_move, False)
-    gathered = []
-    for i in range(len(PARTS)):
-        if i == 0:
-            line = stack(head_line)
-        else:
-            line = stack([a[:, ends[i - 1] - ends[0] : ends[i] - ends[0]] for a in tail_line])
-        if i == 1:
-            line, scales = lax.optimization_barrier((line, scales))
-        own = stack(ring(line, second_move, i % 2 == 0))
+    gathered, made, passed = [], [], []
+
+    def first_part(i):
+        own, other = gathered[i]
+        part = layer_part(
+            xn0, own, other, keys, values, x0, ends[i] - PARTS[i], PARTS[i], seq_lengths, section, scales, BLOCK
+        )
+        made.append(part)
+        passed.append(hop(part, [(0, 1), (2, 3)]))
+
+    def finish(i, blocks, *first, late=()):
+        blocks = ring(blocks, second_move, i % 2 == 0, *first)
+        own = stack(blocks[:3] + [behind(blocks[3], *late)])
         gathered.append((own, send(own, CORE_SWAP)))
-    kv_own, kv_other = (a[:, PARTS[0] :] for a in gathered[0])
-
-    kv2_own = hop(kv_own, [(2, 1)])
-    kv3_own = hop(kv_own, [(3, 1)])
-    kv2_other = send(kv2_own, CORE_SWAP)
-    kv3_other = send(kv3_own, CORE_SWAP)
-    small = jnp.concatenate([gain.astype(F32), jnp.pad(scales, (0, 125))]).reshape(-1, 128)
-    small2 = hop(small, [(2, 1)]).reshape(-1)
-    small3 = hop(small, [(3, 1)]).reshape(-1)
+        return blocks
+
+    line = line_of(0)
+    blocks0 = near(line, second_move)
+    along = spectral_along(weight, kv_part, behind(start_rows, line), blocks0[1:2])
+    blocks0 = finish(0, blocks0, along)
+    blocks1 = near(line_of(1), second_move)
+    scales, next_part = spectral_scales(weight, kv_part, behind(along, blocks0[2]), gamma, (blocks0[3], blocks1[1]))
+    lines = {2: line_of(2)}
+    finish(1, blocks1, scales, gathered[0][0], late=(lines[2],))
 
     depth = gathered[0][0].shape[0]
     kv_block = pl.BlockSpec((depth, 2 * HEAD), lambda j: (0, PARTS[0] // (2 * HEAD)))
@@ -468,19 +492,20 @@
         project_kernel,
         grid=(1,),
         out_shape=(head_shape, head_shape),
-        in_specs=[SMEM, whole((rows, width)), kv_block, kv_block],
+        in_specs=[whole((rows, width)), kv_block, kv_block],
         out_specs=(whole((rows, HEAD)), whole((rows, HEAD))),
         compiler_params=params(),
         cost_estimate=cost(4 * rows * width * HEAD, 4 * width * HEAD),
-    )(scales, xn0, *gathered[0])
-
-    made, passed = [], []
-    for i, (own, other) in enumerate(gathered):
-        part = layer_part(
-            xn0, own, other, keys, values, x0, ends[i] - PARTS[i], PARTS[i], seq_lengths, section, scales, BLOCK
-        )
-        made.append(part)
-        passed.append(hop(part, [(0, 1), (2, 3)]))
+    )(xn0, *gathered[0])
+    scales2 = hop(jnp.broadcast_to(scales[:, None], (3, 128)), [(2, 3)])[:, 0]
+    for i in range(2, len(PARTS)):
+        blocks = near(behind(lines[i], gathered[i - 2][0]), second_move)
+        if i + 1 < len(PARTS):
+            lines[i + 1] = line_of(i + 1)
+        first_part(i - 2)
+        finish(i, blocks, made[-1], scales2, late=(lines[i + 1],) if i + 1 in lines else ())
+    for i in range(len(made), len(PARTS)):
+        first_part(i)
     flat = [half for halves in gathered for half in halves]
 
     scratch = [
@@ -488,13 +513,13 @@
         pltpu.SemaphoreType.DMA((SLOTS, 2)),
     ]
     n = len(PARTS)
-    all_scales = jnp.concatenate([scales, small2[width : width + 3], small3[width : width + 3]])
-    all_gains = jnp.concatenate([wide_gain, small2[None, :width], small3[None, :width]], 0)
+    all_gains = jnp.stack([gain, extra2[local:].reshape(-1), extra3[local:].reshape(-1)]).astype(F32)
+    all_scales = jnp.concatenate([scales, jnp.where(section == 3, scales2, scales)])
     layer_cost = cost(2 * rows * width * width, 2 * width * width, rows * width)
     out1, cross = pl.pallas_call(
         encoder_kernel,
         out_shape=(row_shape, jax.ShapeDtypeStruct((rows, 4 * HEAD), BF16)),
-        in_specs=[SMEM] * 4 + [VMEM] + [ANY] * (3 * n + 4),
+        in_specs=[SMEM] * 4 + [VMEM] + [ANY] * (3 * n),
         out_specs=(VMEM, VMEM),
         scratch_shapes=scratch
         + [
@@ -509,7 +534,7 @@
         ],
         compiler_params=params(),
         cost_estimate=layer_cost,
-    )(order, section, seq_lengths, all_scales, all_gains, *passed, *flat, kv2_own, kv2_other, kv3_own, kv3_other)
+    )(order, section, seq_lengths, scales, all_gains, *passed, *flat)
     cross = hop(cross, [(1, 2)]) + hop(cross, [(1, 3)])
 
     result = pl.pallas_call(
@@ -527,7 +552,7 @@
         ],
         compiler_params=params(),
         cost_estimate=layer_cost,
-    )(order, section, seq_lengths, scales, wide_gain, cross, out1, target2, *made, *passed, *flat)
+    )(order, section, seq_lengths, all_scales, wide_gain, cross, out1, target2, *made, *passed, *flat)
     return result.reshape(1, micro, seqs, length, width), next_part[None]
 
 

time: 331 us -> 412 us (1.24)
  Pallas kernels: 67.2 us -> 161 us
  starting transfers between devices: 67.5 us -> 49.8 us
  local copies, waits for them, and re-layouts: 4.65 us -> 13.6 us
  waiting for transfers between devices: 181 us -> 176 us
    pallas_call x8, Pallas kernels: 9.44 us -> 104 us  [stack(): pl.pallas_call(functools.partial(stack_kernel, count), out_shape=jax.Shap...]
    ppermute x10 -> x9, waiting for transfers between devices: 99.5 us -> 56.7 us  [shards(): hop = lambda value, pairs: lax.ppermute(value, 'section', pairs)]
    ppermute x34 -> x32, waiting for transfers between devices: 81.6 us -> 119 us  [send(): return lax.ppermute(value, 'fsdp', pairs)]
    unnamed x15 -> x73, local copies, waits for them, and re-layouts: 0.61 us -> 11.7 us
    ppermute x10 -> x9, starting transfers between devices: 21.1 us -> 12.2 us  [shards(): hop = lambda value, pairs: lax.ppermute(value, 'section', pairs)]
    ppermute x34 -> x32, starting transfers between devices: 46.4 us -> 37.5 us  [send(): return lax.ppermute(value, 'fsdp', pairs)]
  transfers between devices with their start and end apart: 44 -> 41, of which waited for: 22 -> 24; matrix products, arithmetic and copies ran while one was open for 2% -> 2% of each run, Pallas kernels for 12% -> 9%
where the time goes in v1:
time: 412 us; the launch traced here: 411 us
  waiting for transfers between devices  176 us (43%)
  Pallas kernels  161 us (39%)
  starting transfers between devices  49.8 us (12%)
  local copies, waits for them, and re-layouts  13.6 us (3%)
  other arithmetic  4.58 us (1%)
    ppermute x32, waiting for transfers between devices, send(): return lax.ppermute(value, 'fsdp', pairs)  119 us
    pallas_call x8, Pallas kernels, stack(): pl.pallas_call(functools.partial(stack_kernel, count), out_shape=jax.Shap...  104 us
    ppermute x9, waiting for transfers between devices, shards(): hop = lambda value, pairs: lax.ppermute(value, 'section', pairs)  56.7 us
    ppermute x32, starting transfers between devices, send(): return lax.ppermute(value, 'fsdp', pairs)  37.5 us
    pallas_call x4, Pallas kernels, layer_part(): pl.pallas_call(part_kernel, grid=(width // block,), out_shape=jax.ShapeDt...  25.4 us
    pallas_call x1, Pallas kernels, shards(): pl.pallas_call(decoder_kernel, out_shape=row_shape, in_specs=[SMEM] * 4 +...  24.4 us
    ppermute x9, starting transfers between devices, shards(): hop = lambda value, pairs: lax.ppermute(value, 'section', pairs)  12.2 us
    unnamed x73, local copies, waits for them, and re-layouts  11.7 us
  transfers between devices with their start and end apart: 41, of which 24 were waited for; matrix products, arithmetic and copies ran while one was open for 2% of the time, Pallas kernels for 9%

profile of v1, /device:TPU:24, one launch (start us, length us, event | category | flops | bytes accessed | tf_op | source)
XLA Modules:
  0.0 410.8 jit_solution(3484169110219912875)
XLA Ops:
  2.4 3.1 collective-permute-start.15
  8.1 4.1 collective-permute-start.1
  12.4 4.4 %collective-permute-done.1.refs_2_ = bf16[128,1280]{1,0:T(8,128)(2,1)S(1)} collective-permute-done((bf16[128,1280]{1,0:T(8,128)(2,1)S(1)}, bf16[128,1280]{1,0:T(8,128)(2,1)S(1)}, u32[]{:S(2)}, u32[]{:S(2)}) %collective-permute-start.1) | collective-permute-done | bytes 327712 | tf_op jit(solution)/shard_map/ppermute | solution.py:58
  16.8 3.7 collective-permute-done.refs_1_
  22.6 6.2 %collective-permute-done.2.refs_3_ = bf16[128,1280]{1,0:T(8,128)(2,1)S(1)} collective-permute-done((bf16[128,1280]{1,0:T(8,128)(2,1)S(1)}, bf16[128,1280]{1,0:T(8,128)(2,1)S(1)}, u32[]{:S(2)}, u32[]{:S(2)}) %collective-permute-start.2) | collective-permute-done | bytes 327712 | tf_op jit(solution)/shard_map/ppermute | solution.py:58
  29.3 2.8 collective-permute-start.9
  32.5 7.4 %collective-permute-done.17 = bf16[128,3584]{1,0:T(8,128)(2,1)S(1)} collective-permute-done((bf16[128,3584]{1,0:T(8,128)(2,1)S(1)}, bf16[128,3584]{1,0:T(8,128)(2,1)S(1)}, u32[]{:S(2)}, u32[]{:S(2)}) %collective-permute-start.17) | collective-permute-done | bytes 917536 | tf_op jit(solution)/shard_map/ppermute | solution.py:58
  43.2 15.1 %collective-permute-done.4 = f32[34,128]{1,0:T(8,128)S(1)} collective-permute-done((f32[34,128]{1,0:T(8,128)S(1)}, f32[34,128]{1,0:T(8,128)S(1)}, u32[]{:S(2)}, u32[]{:S(2)}) %collective-permute-start.4) | collective-permute-done | bytes 17440 | tf_op jit(solution)/shard_map/ppermute | solution.py:58
  62.2 5.3 %collective-permute-done.7 = f32[34,128]{1,0:T(8,128)S(1)} collective-permute-done((f32[34,128]{1,0:T(8,128)S(1)}, f32[34,128]{1,0:T(8,128)S(1)}, u32[]{:S(2)}, u32[]{:S(2)}) %collective-permute-start.7) | collective-permute-done | bytes 17440 | tf_op jit(solution)/shard_map/ppermute | solution.py:58
  67.5 3.3 collective-permute-start.8
  86.7 5.0 %collective-permute-done.11 = f32[3,128]{0,1:T(8,128)S(1)} collective-permute-done((f32[3,128]{0,1:T(8,128)S(1)}, f32[3,128]{0,1:T(8,128)S(1)}, u32[]{:S(2)}, u32[]{:S(2)}) %collective-permute-start.11) | collective-permute-done | bytes 1568 | tf_op jit(solution)/shard_map/ppermute | solution.py:58
  92.1 17.9 %collective-permute-done.12 = f32[3,128]{0,1:T(8,128)S(1)} collective-permute-done((f32[3,128]{0,1:T(8,128)S(1)}, f32[3,128]{0,1:T(8,128)S(1)}, u32[]{:S(2)}, u32[]{:S(2)}) %collective-permute-start.12) | collective-permute-done | bytes 1568 | tf_op jit(solution)/shard_map/ppermute | solution.py:58
  111.7 5.8 %collective-permute-done.20 = f32[3,128]{0,1:T(8,128)S(1)} collective-permute-done((f32[3,128]{0,1:T(8,128)S(1)}, f32[3,128]{0,1:T(8,128)S(1)}, u32[]{:S(2)}, u32[]{:S(2)}) %collective-permute-start.20) | collective-permute-done | bytes 1568 | tf_op jit(solution)/shard_map/ppermute | solution.py:58
  119.6 3.7 collective-permute-done.21
  131.1 3.2 collective-permute-start.26
  134.7 17.9 %collective-permute-done.26.refs_3_ = bf16[512,1536]{1,0:T(8,128)(2,1)S(1)} collective-permute-done((bf16[512,1536]{1,0:T(8,128)(2,1)}, bf16[512,1536]{1,0:T(8,128)(2,1)S(1)}, u32[]{:S(2)}, u32[]{:S(2)}) %collective-permute-start.26) | collective-permute-done | bytes 1572896 | tf_op jit(solution)/shard_map/ppermute | solution.py:58
  152.5 96.4 %shard_map.111.own_ref.refs_11_.refs_18_ = bf16[2048,1536]{1,0:T(8,128)(2,1)} custom-call(bf16[512,1536]{1,0:T(8,128)(2,1)S(1)} %shard_map.105.refs_0_, bf16[512,1536]{1,0:T(8,128)(2,1)} %collective-permute-done.19.refs_1_, bf16[512,1536]{1,0:T(8,128)(2,1)} %collective-permute-done.25.refs_2_, bf16[512,1536]{1,0:T(8,128)(2,1)S(1)} %collective-permute-done.26.refs_3_), custom_call_target="tpu_custom_call" | custom-call | bytes 196608 | tf_op jit(solution)/shard_map/pallas_call | solution.py:122
  251.8 2.5 collective-permute-start.35
  254.8 3.9 shard_map.106
  260.8 6.2 %collective-permute-done.23.other_ref.refs_10_.refs_17_ = bf16[2048,1280]{1,0:T(8,128)(2,1)} collective-permute-done((bf16[2048,1280]{1,0:T(8,128)(2,1)}, bf16[2048,1280]{1,0:T(8,128)(2,1)}, u32[]{:S(2)}, u32[]{:S(2)}) %collective-permute-start.23) | collective-permute-done | bytes 5242912 | tf_op jit(solution)/shard_map/ppermute | solution.py:58
  269.4 6.4 %shard_map.109.refs_8_ = bf16[256,1024]{1,0:T(8,128)(2,1)S(1)} custom-call(s32[2]{0:T(128)S(1)} %bitcast.77, s32[1]{0:T(128)} %bitcast.section_ref.refs_1_, f32[3]{0:T(128)S(1)} %get-tuple-element.47.scale_ref.refs_3_, bf16[256,4096]{1,0:T(8,128)(2,1)S(1)} %get-tuple-element.27.xn_ref, bf16[2048,1280]{1,0:T(8,128)(2,1)} %shard_map.107.own_ref.refs_9_.refs_16_, ...), custom_call_target="tpu_custom_call" | custom-call | flops 33554432 | bytes 131072 | tf_op jit(solution)/shard_map/pallas_call | solution.py:199
  277.0 6.4 %shard_map.112.refs_9_ = bf16[256,1024]{1,0:T(8,128)(2,1)S(1)} custom-call(s32[2]{0:T(128)S(1)} %bitcast.78, s32[1]{0:T(128)} %bitcast.section_ref.refs_1_, f32[3]{0:T(128)S(1)} %get-tuple-element.47.scale_ref.refs_3_, bf16[256,4096]{1,0:T(8,128)(2,1)S(1)} %get-tuple-element.27.xn_ref, bf16[2048,1536]{1,0:T(8,128)(2,1)} %shard_map.111.own_ref.refs_11_.refs_18_, ...), custom_call_target="tpu_custom_call" | custom-call | flops 33554432 | bytes 131072 | tf_op jit(solution)/shard_map/pallas_call | solution.py:199
  283.4 2.6 collective-permute-start.36
  286.0 6.4 %collective-permute-done.31.refs_3_ = bf16[512,1024]{1,0:T(8,128)(2,1)S(1)} collective-permute-done((bf16[512,1024]{1,0:T(8,128)(2,1)}, bf16[512,1024]{1,0:T(8,128)(2,1)S(1)}, u32[]{:S(2)}, u32[]{:S(2)}) %collective-permute-start.31) | collective-permute-done | bytes 1048608 | tf_op jit(solution)/shard_map/ppermute | solution.py:58
  298.3 5.4 %collective-permute-done.34.refs_1_ = bf16[512,1024]{1,0:T(8,128)(2,1)S(1)} collective-permute-done((bf16[512,1024]{1,0:T(8,128)(2,1)}, bf16[512,1024]{1,0:T(8,128)(2,1)S(1)}, u32[]{:S(2)}, u32[]{:S(2)}) %collective-permute-start.34) | collective-permute-done | bytes 1048608 | tf_op jit(solution)/shard_map/ppermute | solution.py:58
  308.9 6.4 %shard_map.115.refs_10_ = bf16[256,1024]{1,0:T(8,128)(2,1)S(1)} custom-call(s32[2]{0:T(128)S(1)} %bitcast.79, s32[1]{0:T(128)} %bitcast.section_ref.refs_1_, f32[3]{0:T(128)S(1)} %get-tuple-element.47.scale_ref.refs_3_, bf16[256,4096]{1,0:T(8,128)(2,1)S(1)} %get-tuple-element.27.xn_ref, bf16[2048,1024]{1,0:T(8,128)(2,1)} %copy-done, ...), custom_call_target="tpu_custom_call" | custom-call | flops 33554432 | bytes 131072 | tf_op jit(solution)/shard_map/pallas_call | solution.py:199
  316.6 6.3 %shard_map.117.refs_11_ = bf16[256,1024]{1,0:T(8,128)(2,1)S(1)} custom-call(s32[2]{0:T(128)S(1)} %bitcast.80, s32[1]{0:T(128)} %bitcast.section_ref.refs_1_, f32[3]{0:T(128)S(1)} %get-tuple-element.47.scale_ref.refs_3_, bf16[256,4096]{1,0:T(8,128)(2,1)S(1)} %get-tuple-element.27.xn_ref, bf16[2048,1024]{1,0:T(8,128)(2,1)} %copy-done.1, ...), custom_call_target="tpu_custom_call" | custom-call | flops 33554432 | bytes 131072 | tf_op jit(solution)/shard_map/pallas_call | solution.py:199
  324.4 9.7 %collective-permute-done.28.refs_6_.refs_13_ = bf16[256,1024]{1,0:T(8,128)(2,1)S(1)} collective-permute-done((bf16[256,1024]{1,0:T(8,128)(2,1)S(1)}, bf16[256,1024]{1,0:T(8,128)(2,1)S(1)}, u32[]{:S(2)}, u32[]{:S(2)}) %collective-permute-start.28) | collective-permute-done | bytes 524320 | tf_op jit(solution)/shard_map/ppermute | solution.py:433
  334.1 11.2 %collective-permute-done.33.refs_7_.refs_14_ = bf16[256,1024]{1,0:T(8,128)(2,1)S(1)} collective-permute-done((bf16[256,1024]{1,0:T(8,128)(2,1)S(1)}, bf16[256,1024]{1,0:T(8,128)(2,1)S(1)}, u32[]{:S(2)}, u32[]{:S(2)}) %collective-permute-start.33) | collective-permute-done | bytes 524320 | tf_op jit(solution)/shard_map/ppermute | solution.py:433
  345.4 10.8 %collective-permute-done.38.refs_8_.refs_15_ = bf16[256,1024]{1,0:T(8,128)(2,1)S(1)} collective-permute-done((bf16[256,1024]{1,0:T(8,128)(2,1)S(1)}, bf16[256,1024]{1,0:T(8,128)(2,1)S(1)}, u32[]{:S(2)}, u32[]{:S(2)}) %collective-permute-start.38) | collective-permute-done | bytes 524320 | tf_op jit(solution)/shard_map/ppermute | solution.py:433
  361.1 25.0 %collective-permute-done.40 = bf16[256,512]{1,0:T(8,128)(2,1)S(1)} collective-permute-done((bf16[256,512]{1,0:T(8,128)(2,1)S(1)}, bf16[256,512]{1,0:T(8,128)(2,1)S(1)}, u32[]{:S(2)}, u32[]{:S(2)}) %collective-permute-start.40) | collective-permute-done | bytes 262176 | tf_op jit(solution)/shard_map/ppermute | solution.py:433
  386.2 24.4 %shard_map.119 = bf16[256,4096]{1,0:T(8,128)(2,1)} custom-call(s32[32]{0:T(128)S(1)} %pad_add_fusion.order_ref.refs_0_, s32[1]{0:T(128)} %bitcast.section_ref.refs_1_, s32[2]{0:T(128)S(1)} %bitcast.82, f32[6]{0:T(128)S(1)} %pad_maximum_fusion.3.refs_3_, f32[1,4096]{1,0:T(1,128)S(1)} %get-tuple-element.58.gain_ref.refs_4_, ...), custom_call_target="tpu_custom_call" | custom-call | flops 134217728 | bytes 524288 | tf_op jit(solution)/shard_map/pallas_call | solution.py:540
  (193 shorter events, 68.3 us)
Async XLA Ops:
  2.4 9.9 %collective-permute-start.15 = (bf16[144,256]{1,0:T(8,128)(2,1)S(1)}, bf16[144,256]{1,0:T(8,128)(2,1)S(1)}, u32[]{:S(2)}, u32[]{:S(2)}) collective-permute-start(bf16[144,256]{1,0:T(8,128)(2,1)S(1)} %pad_maximum_fusion.2), channel_id=1, source_target_pairs={{96,32},{97,33},{98,34},{99,35},{100,36},{101,37},{102,38},{103,39... | collective-permute-start | bytes 221192 | tf_op jit(solution)/shard_map/ppermute | solution.py:433
  8.1 8.7 %collective-permute-start.1 = (bf16[128,1280]{1,0:T(8,128)(2,1)S(1)}, bf16[128,1280]{1,0:T(8,128)(2,1)S(1)}, u32[]{:S(2)}, u32[]{:S(2)}) collective-permute-start(bf16[128,1280]{1,0:T(8,128)(2,1)S(1)} %pad_maximum_fusion.1.refs_0_), channel_id=1, source_target_pairs={{0,6},{1,25},{2,0},{3,27},{4,2},{5,29},{6,4},{7,31},{8,14},{9,1},{... | collective-permute-start | bytes 983048 | tf_op jit(solution)/shard_map/ppermute | solution.py:58
  12.2 8.3 %collective-permute-start = (bf16[128,1280]{1,0:T(8,128)(2,1)S(1)}, bf16[128,1280]{1,0:T(8,128)(2,1)S(1)}, u32[]{:S(2)}, u32[]{:S(2)}) collective-permute-start(bf16[128,1280]{1,0:T(8,128)(2,1)S(1)} %pad_maximum_fusion.1.refs_0_), channel_id=1, source_target_pairs={{0,2},{1,9},{2,4},{3,11},{4,6},{5,13},{6,0},{7,15},{8,10},{9,17},{... | collective-permute-start | bytes 983048 | tf_op jit(solution)/shard_map/ppermute | solution.py:58
  20.5 19.3 %collective-permute-start.17 = (bf16[128,3584]{1,0:T(8,128)(2,1)S(1)}, bf16[128,3584]{1,0:T(8,128)(2,1)S(1)}, u32[]{:S(2)}, u32[]{:S(2)}) collective-permute-start(bf16[128,3584]{1,0:T(8,128)(2,1)S(1)} %pad_maximum_fusion), channel_id=1, source_target_pairs={{0,6},{1,25},{2,0},{3,27},{4,2},{5,29},{6,4},{7,31},{8,14},{9,1},{... | collective-permute-start | bytes 2752520 | tf_op jit(solution)/shard_map/ppermute | solution.py:58
  20.5 8.3 %collective-permute-start.2 = (bf16[128,1280]{1,0:T(8,128)(2,1)S(1)}, bf16[128,1280]{1,0:T(8,128)(2,1)S(1)}, u32[]{:S(2)}, u32[]{:S(2)}) collective-permute-start(bf16[128,1280]{1,0:T(8,128)(2,1)S(1)} %collective-permute-done.refs_1_), channel_id=1, source_target_pairs={{0,2},{1,9},{2,4},{3,11},{4,6},{5,13},{6,0},{7,15},{8,10},{9,17},{... | collective-permute-start | bytes 983048 | tf_op jit(solution)/shard_map/ppermute | solution.py:58
  22.6 48.3 %collective-permute-start.16 = (bf16[128,3584]{1,0:T(8,128)(2,1)S(1)}, bf16[128,3584]{1,0:T(8,128)(2,1)S(1)}, u32[]{:S(2)}, u32[]{:S(2)}) collective-permute-start(bf16[128,3584]{1,0:T(8,128)(2,1)S(1)} %pad_maximum_fusion), channel_id=1, source_target_pairs={{0,2},{1,9},{2,4},{3,11},{4,6},{5,13},{6,0},{7,15},{8,10},{9,17},{... | collective-permute-start | bytes 2752520 | tf_op jit(solution)/shard_map/ppermute | solution.py:58
  29.3 43.6 %collective-permute-start.9 = (bf16[512,1280]{1,0:T(8,128)(2,1)S(1)}, bf16[512,1280]{1,0:T(8,128)(2,1)S(1)}, u32[]{:S(2)}, u32[]{:S(2)}) collective-permute-start(bf16[512,1280]{1,0:T(8,128)(2,1)S(1)} %shard_map.104.refs_0_), channel_id=1, source_target_pairs={{0,24},{1,7},{2,26},{3,1},{4,28},{5,3},{6,30},{7,5},{8,0},{9,15},{... | collective-permute-start | bytes 3932168 | tf_op jit(solution)/shard_map/ppermute | solution.py:58
  32.1 30.0 %collective-permute-start.6 = (bf16[512,1280]{1,0:T(8,128)(2,1)S(1)}, bf16[512,1280]{1,0:T(8,128)(2,1)S(1)}, u32[]{:S(2)}, u32[]{:S(2)}) collective-permute-start(bf16[512,1280]{1,0:T(8,128)(2,1)S(1)} %shard_map.104.refs_0_), channel_id=1, source_target_pairs={{0,8},{1,3},{2,10},{3,5},{4,12},{5,7},{6,14},{7,1},{8,16},{9,11},{... | collective-permute-start | bytes 3932168 | tf_op jit(solution)/shard_map/ppermute | solution.py:58
  39.9 34.1 %collective-permute-start.18 = (bf16[128,3584]{1,0:T(8,128)(2,1)S(1)}, bf16[128,3584]{1,0:T(8,128)(2,1)S(1)}, u32[]{:S(2)}, u32[]{:S(2)}) collective-permute-start(bf16[128,3584]{1,0:T(8,128)(2,1)S(1)} %collective-permute-done.17), channel_id=1, source_target_pairs={{0,6},{1,25},{2,0},{3,27},{4,2},{5,29},{6,4},{7,31},{8,14},{9,1},{... | collective-permute-start | bytes 2752520 | tf_op jit(solution)/shard_map/ppermute | solution.py:58
  41.2 17.1 %collective-permute-start.4 = (f32[34,128]{1,0:T(8,128)S(1)}, f32[34,128]{1,0:T(8,128)S(1)}, u32[]{:S(2)}, u32[]{:S(2)}) collective-permute-start(f32[34,128]{1,0:T(8,128)S(1)} %fusion.37), channel_id=1, source_target_pairs={{0,2},{1,3},{2,0},{3,1},{4,6},{5,7},{6,4},{7,5},{8,10},{9,11},{10,... | collective-permute-start | bytes 52232 | tf_op jit(solution)/shard_map/ppermute | solution.py:58
  74.9 36.8 %collective-permute-start.19 = (bf16[512,1536]{1,0:T(8,128)(2,1)S(1)}, bf16[512,1536]{1,0:T(8,128)(2,1)}, u32[]{:S(2)}, u32[]{:S(2)}) collective-permute-start(bf16[512,1536]{1,0:T(8,128)(2,1)S(1)} %shard_map.105.refs_0_), channel_id=1, source_target_pairs={{0,8},{1,3},{2,10},{3,5},{4,12},{5,7},{6,14},{7,1},{8,16},{9,11},{... | collective-permute-start | bytes 4718600 | tf_op jit(solution)/shard_map/ppermute | solution.py:58
  79.9 30.7 %collective-permute-start.13 = (bf16[512,1280]{1,0:T(8,128)(2,1)}, bf16[512,1280]{1,0:T(8,128)(2,1)S(1)}, u32[]{:S(2)}, u32[]{:S(2)}) collective-permute-start(bf16[512,1280]{1,0:T(8,128)(2,1)} %copy-done.11), channel_id=1, source_target_pairs={{0,8},{1,3},{2,10},{3,5},{4,12},{5,7},{6,14},{7,1},{8,16},{9,11},{... | collective-permute-start | bytes 3932168 | tf_op jit(solution)/shard_map/ppermute | solution.py:58
  81.6 49.5 %collective-permute-start.25 = (bf16[512,1536]{1,0:T(8,128)(2,1)S(1)}, bf16[512,1536]{1,0:T(8,128)(2,1)}, u32[]{:S(2)}, u32[]{:S(2)}) collective-permute-start(bf16[512,1536]{1,0:T(8,128)(2,1)S(1)} %shard_map.105.refs_0_), channel_id=1, source_target_pairs={{0,24},{1,7},{2,26},{3,1},{4,28},{5,3},{6,30},{7,5},{8,0},{9,15},{... | collective-permute-start | bytes 4718600 | tf_op jit(solution)/shard_map/ppermute | solution.py:58
  91.7 18.3 %collective-permute-start.12 = (f32[3,128]{0,1:T(8,128)S(1)}, f32[3,128]{0,1:T(8,128)S(1)}, u32[]{:S(2)}, u32[]{:S(2)}) collective-permute-start(f32[3,128]{0,1:T(8,128)S(1)} %fusion.47), channel_id=1, source_target_pairs={{0,8},{1,9},{2,10},{3,11},{4,12},{5,13},{6,14},{7,15},{8,0},{9,1},... | collective-permute-start | bytes 4616 | tf_op jit(solution)/shard_map/ppermute | solution.py:58
  123.3 7.7 %collective-permute-start.22 = (f32[3,128]{0,1:T(8,128)S(1)}, f32[3,128]{0,1:T(8,128)S(1)}, u32[]{:S(2)}, u32[]{:S(2)}) collective-permute-start(f32[3,128]{0,1:T(8,128)S(1)} %broadcast_in_dim.34), channel_id=1, source_target_pairs={{64,96},{65,97},{66,98},{67,99},{68,100},{69,101},{70,102},{71,103... | collective-permute-start | bytes 4616 | tf_op jit(solution)/shard_map/ppermute | solution.py:433
  131.1 21.4 %collective-permute-start.26 = (bf16[512,1536]{1,0:T(8,128)(2,1)}, bf16[512,1536]{1,0:T(8,128)(2,1)S(1)}, u32[]{:S(2)}, u32[]{:S(2)}) collective-permute-start(bf16[512,1536]{1,0:T(8,128)(2,1)} %collective-permute-done.25.refs_2_), channel_id=1, source_target_pairs={{0,24},{1,7},{2,26},{3,1},{4,28},{5,3},{6,30},{7,5},{8,0},{9,15},{... | collective-permute-start | bytes 4718600 | tf_op jit(solution)/shard_map/ppermute | solution.py:58
  249.0 28.0 %collective-permute-start.27 = (bf16[2048,1536]{1,0:T(8,128)(2,1)}, bf16[2048,1536]{1,0:T(8,128)(2,1)}, u32[]{:S(2)}, u32[]{:S(2)}) collective-permute-start(bf16[2048,1536]{1,0:T(8,128)(2,1)} %shard_map.111.own_ref.refs_11_.refs_18_), channel_id=1, source_target_pairs={{0,1},{1,0},{2,3},{3,2},{4,5},{5,4},{6,7},{7,6},{8,9},{9,8},{10,11... | collective-permute-start | bytes 18874376 | tf_op jit(solution)/shard_map/ppermute | solution.py:58
  249.1 18.0 %collective-permute-start.23 = (bf16[2048,1280]{1,0:T(8,128)(2,1)}, bf16[2048,1280]{1,0:T(8,128)(2,1)}, u32[]{:S(2)}, u32[]{:S(2)}) collective-permute-start(bf16[2048,1280]{1,0:T(8,128)(2,1)} %shard_map.107.own_ref.refs_9_.refs_16_), channel_id=1, source_target_pairs={{0,1},{1,0},{2,3},{3,2},{4,5},{5,4},{6,7},{7,6},{8,9},{9,8},{10,11... | collective-permute-start | bytes 15728648 | tf_op jit(solution)/shard_map/ppermute | solution.py:58
  249.6 26.2 %collective-permute-start.29 = (bf16[512,1024]{1,0:T(8,128)(2,1)S(1)}, bf16[512,1024]{1,0:T(8,128)(2,1)}, u32[]{:S(2)}, u32[]{:S(2)}) collective-permute-start(bf16[512,1024]{1,0:T(8,128)(2,1)S(1)} %shard_map.110.refs_0_), channel_id=1, source_target_pairs={{0,8},{1,3},{2,10},{3,5},{4,12},{5,7},{6,14},{7,1},{8,16},{9,11},{... | collective-permute-start | bytes 3145736 | tf_op jit(solution)/shard_map/ppermute | solution.py:58
  251.8 31.6 %collective-permute-start.35 = (bf16[512,1024]{1,0:T(8,128)(2,1)}, bf16[512,1024]{1,0:T(8,128)(2,1)S(1)}, u32[]{:S(2)}, u32[]{:S(2)}) collective-permute-start(bf16[512,1024]{1,0:T(8,128)(2,1)} %shard_map.113.refs_0_), channel_id=1, source_target_pairs={{0,24},{1,7},{2,26},{3,1},{4,28},{5,3},{6,30},{7,5},{8,0},{9,15},{... | collective-permute-start | bytes 3145736 | tf_op jit(solution)/shard_map/ppermute | solution.py:58
  258.7 34.7 %collective-permute-start.30 = (bf16[512,1024]{1,0:T(8,128)(2,1)S(1)}, bf16[512,1024]{1,0:T(8,128)(2,1)S(1)}, u32[]{:S(2)}, u32[]{:S(2)}) collective-permute-start(bf16[512,1024]{1,0:T(8,128)(2,1)S(1)} %shard_map.110.refs_0_), channel_id=1, source_target_pairs={{0,24},{1,7},{2,26},{3,1},{4,28},{5,3},{6,30},{7,5},{8,0},{9,15},{... | collective-permute-start | bytes 3145736 | tf_op jit(solution)/shard_map/ppermute | solution.py:58
  275.8 16.6 %collective-permute-start.31 = (bf16[512,1024]{1,0:T(8,128)(2,1)}, bf16[512,1024]{1,0:T(8,128)(2,1)S(1)}, u32[]{:S(2)}, u32[]{:S(2)}) collective-permute-start(bf16[512,1024]{1,0:T(8,128)(2,1)} %collective-permute-done.29.refs_1_), channel_id=1, source_target_pairs={{0,8},{1,3},{2,10},{3,5},{4,12},{5,7},{6,14},{7,1},{8,16},{9,11},{... | collective-permute-start | bytes 3145736 | tf_op jit(solution)/shard_map/ppermute | solution.py:58
  283.4 14.9 %collective-permute-start.36 = (bf16[512,1024]{1,0:T(8,128)(2,1)S(1)}, bf16[512,1024]{1,0:T(8,128)(2,1)S(1)}, u32[]{:S(2)}, u32[]{:S(2)}) collective-permute-start(bf16[512,1024]{1,0:T(8,128)(2,1)S(1)} %collective-permute-done.35.refs_2_), channel_id=1, source_target_pairs={{0,24},{1,7},{2,26},{3,1},{4,28},{5,3},{6,30},{7,5},{8,0},{9,15},{... | collective-permute-start | bytes 3145736 | tf_op jit(solution)/shard_map/ppermute | solution.py:58
  286.0 17.7 %collective-permute-start.34 = (bf16[512,1024]{1,0:T(8,128)(2,1)}, bf16[512,1024]{1,0:T(8,128)(2,1)S(1)}, u32[]{:S(2)}, u32[]{:S(2)}) collective-permute-start(bf16[512,1024]{1,0:T(8,128)(2,1)} %shard_map.113.refs_0_), channel_id=1, source_target_pairs={{0,8},{1,3},{2,10},{3,5},{4,12},{5,7},{6,14},{7,1},{8,16},{9,11},{... | collective-permute-start | bytes 3145736 | tf_op jit(solution)/shard_map/ppermute | solution.py:58
  296.1 12.8 %collective-permute-start.32 = (bf16[2048,1024]{1,0:T(8,128)(2,1)S(1)}, bf16[2048,1024]{1,0:T(8,128)(2,1)}, u32[]{:S(2)}, u32[]{:S(2)}) collective-permute-start(bf16[2048,1024]{1,0:T(8,128)(2,1)S(1)} %shard_map.114.own_ref.refs_13_.refs_20_), channel_id=1, source_target_pairs={{0,1},{1,0},{2,3},{3,2},{4,5},{5,4},{6,7},{7,6},{8,9},{9,8},{10,11... | collective-permute-start | bytes 12582920 | tf_op jit(solution)/shard_map/ppermute | solution.py:58
  306.2 10.4 %collective-permute-start.37 = (bf16[2048,1024]{1,0:T(8,128)(2,1)S(1)}, bf16[2048,1024]{1,0:T(8,128)(2,1)}, u32[]{:S(2)}, u32[]{:S(2)}) collective-permute-start(bf16[2048,1024]{1,0:T(8,128)(2,1)S(1)} %shard_map.116.own_ref.refs_15_.refs_22_), channel_id=1, source_target_pairs={{0,1},{1,0},{2,3},{3,2},{4,5},{5,4},{6,7},{7,6},{8,9},{9,8},{10,11... | collective-permute-start | bytes 12582920 | tf_op jit(solution)/shard_map/ppermute | solution.py:58
  306.3 18.1 %collective-permute-start.24 = (bf16[256,1024]{1,0:T(8,128)(2,1)S(1)}, bf16[256,1024]{1,0:T(8,128)(2,1)S(1)}, u32[]{:S(2)}, u32[]{:S(2)}) collective-permute-start(bf16[256,1024]{1,0:T(8,128)(2,1)S(1)} %shard_map.109.refs_8_), channel_id=1, source_target_pairs={{0,32},{64,96},{1,33},{65,97},{2,34},{66,98},{3,35},{67,99},{4,36}... | collective-permute-start | bytes 1572872 | tf_op jit(solution)/shard_map/ppermute | solution.py:433
  307.6 26.5 %collective-permute-start.28 = (bf16[256,1024]{1,0:T(8,128)(2,1)S(1)}, bf16[256,1024]{1,0:T(8,128)(2,1)S(1)}, u32[]{:S(2)}, u32[]{:S(2)}) collective-permute-start(bf16[256,1024]{1,0:T(8,128)(2,1)S(1)} %shard_map.112.refs_9_), channel_id=1, source_target_pairs={{0,32},{64,96},{1,33},{65,97},{2,34},{66,98},{3,35},{67,99},{4,36}... | collective-permute-start | bytes 1572872 | tf_op jit(solution)/shard_map/ppermute | solution.py:433
  315.3 30.1 %collective-permute-start.33 = (bf16[256,1024]{1,0:T(8,128)(2,1)S(1)}, bf16[256,1024]{1,0:T(8,128)(2,1)S(1)}, u32[]{:S(2)}, u32[]{:S(2)}) collective-permute-start(bf16[256,1024]{1,0:T(8,128)(2,1)S(1)} %shard_map.115.refs_10_), channel_id=1, source_target_pairs={{0,32},{64,96},{1,33},{65,97},{2,34},{66,98},{3,35},{67,99},{4,36}... | collective-permute-start | bytes 1572872 | tf_op jit(solution)/shard_map/ppermute | solution.py:433
  322.9 33.2 %collective-permute-start.38 = (bf16[256,1024]{1,0:T(8,128)(2,1)S(1)}, bf16[256,1024]{1,0:T(8,128)(2,1)S(1)}, u32[]{:S(2)}, u32[]{:S(2)}) collective-permute-start(bf16[256,1024]{1,0:T(8,128)(2,1)S(1)} %shard_map.117.refs_11_), channel_id=1, source_target_pairs={{0,32},{64,96},{1,33},{65,97},{2,34},{66,98},{3,35},{67,99},{4,36}... | collective-permute-start | bytes 1572872 | tf_op jit(solution)/shard_map/ppermute | solution.py:433
  358.4 27.6 %collective-permute-start.40 = (bf16[256,512]{1,0:T(8,128)(2,1)S(1)}, bf16[256,512]{1,0:T(8,128)(2,1)S(1)}, u32[]{:S(2)}, u32[]{:S(2)}) collective-permute-start(bf16[256,512]{1,0:T(8,128)(2,1)S(1)} %get-tuple-element.38), channel_id=1, source_target_pairs={{32,96},{33,97},{34,98},{35,99},{36,100},{37,101},{38,102},{39,103... | collective-permute-start | bytes 786440 | tf_op jit(solution)/shard_map/ppermute | solution.py:433
  359.7 26.4 %collective-permute-start.39 = (bf16[256,512]{1,0:T(8,128)(2,1)S(1)}, bf16[256,512]{1,0:T(8,128)(2,1)S(1)}, u32[]{:S(2)}, u32[]{:S(2)}) collective-permute-start(bf16[256,512]{1,0:T(8,128)(2,1)S(1)} %get-tuple-element.38), channel_id=1, source_target_pairs={{32,64},{33,65},{34,66},{35,67},{36,68},{37,69},{38,70},{39,71},{4... | collective-permute-start | bytes 786440 | tf_op jit(solution)/shard_map/ppermute | solution.py:433
  (43 other events, 533.8 us)

commit v2 on v1

v2 whole, which is shorter than its diff:
```python
import functools
import math

import jax
import jax.numpy as jnp
from jax import lax
from jax.experimental import pallas as pl
from jax.experimental.pallas import tpu as pltpu
from jax.sharding import PartitionSpec as P

HEAD = 128
EPS = 1e-06
F32 = jnp.float32
BF16 = jnp.bfloat16
VMEM_LIMIT = 48 * 1024 * 1024
BLOCK = 512
PIECE = 1024
SLOTS = 3
LOG2E_SCALED = math.log2(math.e) / math.sqrt(HEAD)
ANY = pl.BlockSpec(memory_space=pl.ANY)
VMEM = pl.BlockSpec(memory_space=pltpu.VMEM)
SMEM = pl.BlockSpec(memory_space=pltpu.SMEM)


def dot(a, b):
    return jnp.dot(a, b, preferred_element_type=F32)


def moves(fn):
    pairs = []
    for index in range(32):
        x, z, core = index // 8, (index // 2) % 4, index % 2
        x2, z2, core2 = fn(x, z, core)
        pairs.append((index, (x2 % 4) * 8 + (z2 % 4) * 2 + core2))
    return pairs


CORE_SWAP = moves(lambda x, z, c: (x, z, 1 - c))
DOUBLING = (
    CORE_SWAP,
    moves(lambda x, z, c: (x, z ^ 1, c)),
    moves(lambda x, z, c: (x ^ 1, z, c)),
    moves(lambda x, z, c: (x, z ^ 2, c)),
    moves(lambda x, z, c: (x ^ 2, z, c)),
)


def send(value, pairs):
    return lax.ppermute(value, "fsdp", pairs)


def total(value):
    for pairs in DOUBLING:
        value = value + send(value, pairs)
    return value


def params():
    return pltpu.CompilerParams(vmem_limit_bytes=VMEM_LIMIT)


def cost(flops, size, exps=0):
    share = 64
    return pl.CostEstimate(flops=int(flops) // share, bytes_accessed=int(size) // share, transcendentals=int(exps) // share)


def norm_into(xn_ref, x_ref, gain_ref, row):
    wide = x_ref[...].astype(F32)
    inv = lax.rsqrt(jnp.mean(wide * wide, axis=-1, keepdims=True) + EPS)
    xn_ref[...] = (wide * inv * gain_ref[row : row + 1, :]).astype(BF16)


def attend(q, keys_ref, values_ref, resid, lengths_ref, key_scale, value_scale):
    seqs, heads = q.shape[0] // 128, q.shape[1] // HEAD
    position = lax.broadcasted_iota(jnp.int32, (heads * 128, 128), 1)
    made = []
    for m in range(seqs):
        rows = slice(m * 128, (m + 1) * 128)
        stacked = jnp.concatenate([q[rows, h * HEAD : (h + 1) * HEAD] for h in range(heads)], 0)
        scores = lax.dot_general(
            stacked, keys_ref[rows, :], (((1,), (1,)), ((), ())), preferred_element_type=F32
        )
        expd = jnp.where(position < lengths_ref[m], jnp.exp2(scores * (key_scale * LOG2E_SCALED)), 0.0)
        probs = (expd * (1.0 / jnp.sum(expd, axis=-1, keepdims=True))).astype(BF16)
        context = dot(probs, values_ref[rows, :]) * value_scale
        made.append(jnp.concatenate([context[h * 128 : (h + 1) * 128] for h in range(heads)], 1))
    return (resid.astype(F32) + jnp.concatenate(made, 0)).astype(BF16)


def project_into(keys_ref, values_ref, xn, kv):
    projected = dot(xn, kv).astype(BF16)
    keys_ref[...] = projected[:, :HEAD]
    values_ref[...] = projected[:, HEAD:]


def enter_kernel(section_ref, source_ref, target_ref, gain_ref, x_ref, xn_ref):
    @pl.when(section_ref[0] == 2)
    def _():
        x_ref[...] = target_ref[...]

    @pl.when(section_ref[0] != 2)
    def _():
        x_ref[...] = source_ref[...]

    norm_into(xn_ref, x_ref, gain_ref, 0)


def project_kernel(xn_ref, kv_ref, keys_ref, values_ref):
    project_into(keys_ref, values_ref, xn_ref[...], kv_ref[...])


def part_kernel(lengths_ref, section_ref, scale_ref, xn_ref, w_ref, k_ref, v_ref, x_ref, out_ref):
    q = (dot(xn_ref[...], w_ref[...]) * scale_ref[0]).astype(BF16)

    @pl.when(section_ref[0] != 2)
    def _():
        out_ref[...] = attend(q, k_ref, v_ref, x_ref[...], lengths_ref, scale_ref[1], scale_ref[2])

    @pl.when(section_ref[0] == 2)
    def _():
        out_ref[...] = q


def layer_part(xn, full, keys, values, x, at, lengths, section, scales):
    rows, width = xn.shape
    first = at // BLOCK
    whole = lambda a: pl.BlockSpec(a.shape, lambda j: (0, 0))
    return pl.pallas_call(
        part_kernel,
        grid=(PIECE // BLOCK,),
        out_shape=jax.ShapeDtypeStruct((rows, PIECE), BF16),
        in_specs=[
            SMEM,
            SMEM,
            SMEM,
            whole(xn),
            pl.BlockSpec((width, BLOCK), lambda j: (0, first + j)),
            whole(keys),
            whole(values),
            pl.BlockSpec((rows, BLOCK), lambda j: (0, first + j)),
        ],
        out_specs=pl.BlockSpec((rows, BLOCK), lambda j: (0, j)),
        compiler_params=params(),
        cost_estimate=cost(2 * rows * width * PIECE, 2 * width * PIECE, rows * PIECE),
    )(lengths, section, scales, xn, full, keys, values, x)


def stream_layer(full, buf, sems, xn_ref, q_ref, k_ref, v_ref, x_ref, lengths_ref, scale_ref, out_ref):
    blocks = x_ref.shape[1] // BLOCK

    def block(b):
        slot = lax.rem(b, SLOTS)
        at = pl.ds(pl.multiple_of(b * BLOCK, BLOCK), BLOCK)
        return pltpu.make_async_copy(full.at[:, at], buf.at[slot], sems.at[slot])

    def start():
        for b in range(SLOTS - 1):
            block(jnp.int32(b)).start()

    def run():
        q_ref[...] = jnp.zeros_like(q_ref)

        def emit(b):
            columns = pl.ds(pl.multiple_of(b * BLOCK, BLOCK), BLOCK)
            out_ref[:, columns] = attend(
                q_ref[...], k_ref, v_ref, x_ref[:, columns], lengths_ref, scale_ref[1], scale_ref[2]
            )

        def step(b, carry):
            slot = lax.rem(b, SLOTS)
            block(b).wait()

            @pl.when(b + SLOTS - 1 < blocks)
            def _():
                block(b + SLOTS - 1).start()

            acc = dot(xn_ref[...], buf[slot])
            emit(jnp.maximum(b - 1, 0))
            q_ref[...] = (acc * scale_ref[0]).astype(BF16)
            return carry

        lax.fori_loop(0, blocks, step, 0)
        emit(jnp.int32(blocks - 1))

    return start, run


def bring(pieces, out_ref, sems):
    at = 0
    copies = []
    for i, piece in enumerate(pieces):
        copies.append(pltpu.make_async_copy(piece, out_ref.at[:, pl.ds(at, piece.shape[1])], sems.at[i]))
        at += piece.shape[1]
    return copies


def encoder_kernel(count, *refs):
    section_ref, lengths_ref, scale_ref, gain_ref, full = refs[:5]
    pieces = refs[5 : 5 + count]
    out_ref, cross_ref = refs[5 + count : 7 + count]
    buf, sems, xn_ref, q_ref, x_ref, x_sems, kv_buf, kv_sems, k_ref, v_ref = refs[7 + count :]
    width = x_ref.shape[1]

    @pl.when(section_ref[0] == 1)
    def _():
        arrive = bring(pieces, x_ref, x_sems)
        for copy in arrive:
            copy.start()
        kv_copies = [
            pltpu.make_async_copy(
                full.at[:, pl.ds(width + i * 2 * HEAD, 2 * HEAD)], kv_buf.at[i], kv_sems.at[i]
            )
            for i in range(3)
        ]
        for copy in kv_copies[:1]:
            copy.start()
        start, run = stream_layer(
            full, buf, sems, xn_ref, q_ref, k_ref, v_ref, x_ref, lengths_ref, scale_ref, out_ref
        )
        start()
        for copy in kv_copies[1:]:
            copy.start()
        for copy in arrive:
            copy.wait()
        norm_into(xn_ref, x_ref, gain_ref, 0)
        for copy in kv_copies[:1]:
            copy.wait()
        project_into(k_ref, v_ref, xn_ref[...], kv_buf[0])
        run()
        for copy in kv_copies[1:]:
            copy.wait()
        for i in (1, 2):
            norm_into(xn_ref, out_ref, gain_ref, i)
            at = (i - 1) * 2 * HEAD
            project_into(
                cross_ref.at[:, pl.ds(at, HEAD)],
                cross_ref.at[:, pl.ds(at + HEAD, HEAD)],
                xn_ref[...],
                kv_buf[i],
            )


def decoder_kernel(count, *refs):
    section_ref, lengths_ref, scale_ref, gain_ref, full, cross_ref, first_out, target = refs[:8]
    made, passed = refs[8 : 8 + count], refs[8 + count : 8 + 2 * count]
    out_ref = refs[8 + 2 * count]
    buf, sems, xn_ref, q_ref, x_ref, x_sems, mid_ref = refs[9 + 2 * count :]
    section = section_ref[0]
    blocks = x_ref.shape[1] // BLOCK
    cols = lambda i: cross_ref.at[:, pl.ds(i * HEAD, HEAD)]

    def fetch(pieces, into):
        copies = bring(pieces, into, x_sems)
        for copy in copies:
            copy.start()
        for copy in copies:
            copy.wait()

    def attend_all(resid_ref, into):
        def step(b, carry):
            columns = pl.ds(pl.multiple_of(b * BLOCK, BLOCK), BLOCK)
            into[:, columns] = attend(
                x_ref[:, columns], cols(0), cols(1), resid_ref[:, columns], lengths_ref, scale_ref[4], scale_ref[5]
            )
            return carry

        lax.fori_loop(0, blocks, step, 0)

    @pl.when(section == 0)
    def _():
        fetch(made, out_ref)

    @pl.when(section == 1)
    def _():
        fetch([first_out], out_ref)

    @pl.when(section == 2)
    def _():
        fetch(made, x_ref)
        attend_all(target, out_ref)

    @pl.when(section == 3)
    def _():
        start, run = stream_layer(
            full, buf, sems, xn_ref, q_ref, cols(2), cols(3), mid_ref, lengths_ref, scale_ref, out_ref
        )
        copies = bring(passed, x_ref, x_sems)
        for copy in copies:
            copy.start()
        start()
        for copy in copies:
            copy.wait()
        attend_all(target, mid_ref)
        norm_into(xn_ref, mid_ref, gain_ref, 0)
        run()


def unit_direction(along):
    return (along * lax.rsqrt(jnp.sum(along * along) + EPS)).astype(BF16)


def spectral_along(weight, kv_part, start_rows):
    of_kv = dot(start_rows, kv_part)
    parts = jnp.concatenate([dot(start_rows[0:1], weight)[0], of_kv[1, :HEAD], of_kv[2, HEAD:]])
    return total(parts.reshape(-1, 128))


def spectral_images(weight, kv_part, along):
    width = weight.shape[1]
    return jnp.stack(
        [
            dot(weight, unit_direction(along[:width])),
            dot(kv_part[:, :HEAD], unit_direction(along[width : width + HEAD])),
            dot(kv_part[:, HEAD:], unit_direction(along[width + HEAD :])),
        ]
    )


def shards(weights, kv_weights, gammas, gains, starts, source, target, lengths):
    weight, kv_part, gamma, gain, start_rows = weights[0], kv_weights[0], gammas[0], gains[0], starts[0]
    width = weight.shape[1]
    section = lax.axis_index("section").astype(jnp.int32).reshape(1)
    micro, seqs, length, _ = source.shape
    rows = micro * seqs * length
    seq_lengths = lengths.reshape(-1)
    source2 = source.reshape(rows, width)
    target2 = target.reshape(rows, width)
    wide_gain = gain.astype(F32).reshape(1, width)
    row_shape = jax.ShapeDtypeStruct((rows, width), BF16)
    head_shape = jax.ShapeDtypeStruct((rows, HEAD), BF16)

    hop = lambda value, pairs: lax.ppermute(value, "section", pairs)

    extra = jnp.concatenate([kv_part, gain.reshape(-1, 2 * HEAD)], 0)
    extra2 = hop(extra, [(2, 1)])
    extra3 = hop(extra, [(3, 1)])
    local = kv_part.shape[0]

    full = jnp.concatenate([weight, kv_part, extra2[:local], extra3[:local]], 1)
    full = lax.all_gather(full, "fsdp", axis=0, tiled=True)

    along = spectral_along(weight, kv_part, start_rows).reshape(-1)
    images = spectral_images(weight, kv_part, along)
    squares = jnp.broadcast_to(jnp.sum(images * images, axis=1)[:, None], (3, 128))
    sigmas = jnp.sqrt(total(squares)[:, 0] + EPS)
    scales, next_part = gamma / sigmas, images / sigmas[:, None]
    scales2 = hop(jnp.broadcast_to(scales[:, None], (3, 128)), [(2, 3)])[:, 0]

    x0, xn0 = pl.pallas_call(
        enter_kernel,
        out_shape=(row_shape, row_shape),
        in_specs=[SMEM, VMEM, VMEM, VMEM],
        out_specs=(VMEM, VMEM),
        compiler_params=params(),
        cost_estimate=cost(8 * rows * width, 8 * rows * width),
    )(section, source2, target2, wide_gain)

    kv_block = pl.BlockSpec((width, 2 * HEAD), lambda j: (0, width // (2 * HEAD)))
    whole = lambda shape: pl.BlockSpec(shape, lambda j: (0, 0))
    keys, values = pl.pallas_call(
        project_kernel,
        grid=(1,),
        out_shape=(head_shape, head_shape),
        in_specs=[whole((rows, width)), kv_block],
        out_specs=(whole((rows, HEAD)), whole((rows, HEAD))),
        compiler_params=params(),
        cost_estimate=cost(4 * rows * width * HEAD, 4 * width * HEAD),
    )(xn0, full)

    made, passed = [], []
    for at in range(0, width, PIECE):
        made.append(layer_part(xn0, full, keys, values, x0, at, seq_lengths, section, scales))
        passed.append(hop(made[-1], [(0, 1), (2, 3)]))

    scratch = [
        pltpu.VMEM((SLOTS, width, BLOCK), BF16),
        pltpu.SemaphoreType.DMA((SLOTS,)),
        pltpu.VMEM((rows, width), BF16),
        pltpu.VMEM((rows, BLOCK), BF16),
        pltpu.VMEM((rows, width), BF16),
        pltpu.SemaphoreType.DMA((len(made),)),
    ]
    n = len(made)
    all_gains = jnp.stack([gain, extra2[local:].reshape(-1), extra3[local:].reshape(-1)]).astype(F32)
    all_scales = jnp.concatenate([scales, jnp.where(section == 3, scales2, scales)])
    layer_cost = cost(2 * rows * width * width, 2 * width * width, rows * width)
    out1, cross = pl.pallas_call(
        functools.partial(encoder_kernel, n),
        out_shape=(row_shape, jax.ShapeDtypeStruct((rows, 4 * HEAD), BF16)),
        in_specs=[SMEM] * 3 + [VMEM] + [ANY] * (1 + n),
        out_specs=(VMEM, VMEM),
        scratch_shapes=scratch
        + [
            pltpu.VMEM((3, width, 2 * HEAD), BF16),
            pltpu.SemaphoreType.DMA((3,)),
            pltpu.VMEM((rows, HEAD), BF16),
            pltpu.VMEM((rows, HEAD), BF16),
        ],
        compiler_params=params(),
        cost_estimate=layer_cost,
    )(section, seq_lengths, scales, all_gains, full, *passed)
    cross = hop(cross, [(1, 2)]) + hop(cross, [(1, 3)])

    result = pl.pallas_call(
        functools.partial(decoder_kernel, n),
        out_shape=row_shape,
        in_specs=[SMEM] * 3 + [VMEM, ANY, VMEM, ANY, VMEM] + [ANY] * (2 * n),
        out_specs=VMEM,
        scratch_shapes=scratch + [pltpu.VMEM((rows, width), BF16)],
        compiler_params=params(),
        cost_estimate=layer_cost,
    )(section, seq_lengths, all_scales, wide_gain, full, cross, out1, target2, *made, *passed)
    return result.reshape(1, micro, seqs, length, width), next_part[None]


def solution(mesh):
    in_specs = (
        P("section", "fsdp", None),
        P("section", "fsdp", None),
        P("section", None),
        P("section", None),
        P("section", None, "fsdp"),
        P(None, "fsdp", None, None),
        P(None, "fsdp", None, None),
        P(None, "fsdp"),
    )
    out_specs = (P("section", None, "fsdp", None, None), P("section", None, "fsdp"))
    return jax.shard_map(shards, mesh=mesh, in_specs=in_specs, out_specs=out_specs, check_vma=False)
```

time: 412 us -> 272 us (0.66)
  Pallas kernels: 161 us -> 55.2 us
  waiting for transfers between devices: 176 us -> 156 us
  starting transfers between devices: 49.8 us -> 33.4 us
  between operations: 3.73 us -> 16.5 us
  local copies, waits for them, and re-layouts: 13.6 us -> 3.45 us
    pallas_call x14 -> x6, Pallas kernels: 155 us -> 49.2 us  [the longest x4 25 us: layer_part(): pl.pallas_call(part_kernel, grid=(PIECE // BLOCK,), out_shape=jax.ShapeDt...]
    ppermute x32 -> x10, waiting for transfers between devices: 119 us -> 21.5 us  [send(): return lax.ppermute(value, 'fsdp', pairs)]
    all_gather x0 -> x1, waiting for transfers between devices: none -> 77.7 us  [shards(): full = lax.all_gather(full, 'fsdp', axis=0, tiled=True)]
    ppermute x32 -> x10, starting transfers between devices: 37.5 us -> 20.9 us  [send(): return lax.ppermute(value, 'fsdp', pairs)]
    unnamed x73 -> x23, local copies, waits for them, and re-layouts: 11.7 us -> 3.39 us
  transfers between devices with their start and end apart: 41 -> 20, of which waited for: 24 -> 16; matrix products, arithmetic and copies ran while one was open for 2% -> 1% of each run, Pallas kernels for 9% -> 8%
where the time goes in v2:
time: 272 us
  waiting for transfers between devices  156 us (57%)
  Pallas kernels  55.2 us (20%)
  starting transfers between devices  33.4 us (12%)
  between operations  16.5 us (6%)
  other arithmetic  5.89 us (2%)
  local copies, waits for them, and re-layouts  3.45 us (1%)
    all_gather x1, waiting for transfers between devices, shards(): full = lax.all_gather(full, 'fsdp', axis=0, tiled=True)  77.7 us
    ppermute x9, waiting for transfers between devices, shards(): hop = lambda value, pairs: lax.ppermute(value, 'section', pairs)  57 us
    pallas_call x4, Pallas kernels, layer_part(): pl.pallas_call(part_kernel, grid=(PIECE // BLOCK,), out_shape=jax.ShapeDt...  25 us
    pallas_call x1, Pallas kernels, shards(): pl.pallas_call(functools.partial(decoder_kernel, n), out_shape=row_shape,...  23.6 us
    ppermute x10, waiting for transfers between devices, send(): return lax.ppermute(value, 'fsdp', pairs)  21.5 us
    ppermute x10, starting transfers between devices, send(): return lax.ppermute(value, 'fsdp', pairs)  20.9 us
    ppermute x9, starting transfers between devices, shards(): hop = lambda value, pairs: lax.ppermute(value, 'section', pairs)  12.4 us
  transfers between devices with their start and end apart: 20, of which 16 were waited for; matrix products, arithmetic and copies ran while one was open for 1% of the time, Pallas kernels for 8%

profile of v2, /device:TPU:24, one launch (start us, length us, event | category | flops | bytes accessed | tf_op | source)
XLA Modules:
  0.0 271.7 jit_solution(5964535439900718998)
XLA Ops:
  9.1 3.1 %collective-permute-start.12 = (bf16[144,256]{1,0:T(8,128)(2,1)S(1)}, bf16[144,256]{1,0:T(8,128)(2,1)S(1)}, u32[]{:S(2)}, u32[]{:S(2)}) collective-permute-start(bf16[144,256]{1,0:T(8,128)(2,1)S(1)} %pad_maximum_fusion.1), channel_id=1, source_target_pairs={{96,32},{97,33},{98,34},{99,35},{100,36},{101,37},{102,38},{103,39... | collective-permute-start | bytes 221192 | tf_op jit(solution)/shard_map/ppermute | solution.py:332
  14.2 2.4 pad_maximum_fusion
  18.3 1.9 collective-permute-start.1
  20.2 1.9 collective-permute-done.1
  22.1 1.6 collective-permute-start.2
  23.6 2.3 collective-permute-done.2
  25.9 3.9 %collective-permute-start.3 = (f32[34,128]{1,0:T(8,128)S(1)}, f32[34,128]{1,0:T(8,128)S(1)}, u32[]{:S(2)}, u32[]{:S(2)}) collective-permute-start(f32[34,128]{1,0:T(8,128)S(1)} %add.50), channel_id=1, source_target_pairs={{0,4},{1,5},{2,6},{3,7},{4,0},{5,1},{6,2},{7,3},{8,12},{9,13},{10,... | collective-permute-start | bytes 52232 | tf_op jit(solution)/shard_map/ppermute | solution.py:49
  29.8 1.8 collective-permute-done.3
  31.6 3.0 %collective-permute-start.4 = (f32[34,128]{1,0:T(8,128)S(1)}, f32[34,128]{1,0:T(8,128)S(1)}, u32[]{:S(2)}, u32[]{:S(2)}) collective-permute-start(f32[34,128]{1,0:T(8,128)S(1)} %add.51), channel_id=1, source_target_pairs={{0,16},{1,17},{2,18},{3,19},{4,20},{5,21},{6,22},{7,23},{8,24},{9,... | collective-permute-start | bytes 52232 | tf_op jit(solution)/shard_map/ppermute | solution.py:49
  34.6 2.4 collective-permute-done.4
  42.5 1.6 collective-permute-start.6
  44.1 4.5 %collective-permute-done.6 = f32[3,128]{0,1:T(8,128)S(1)} collective-permute-done((f32[3,128]{0,1:T(8,128)S(1)}, f32[3,128]{0,1:T(8,128)S(1)}, u32[]{:S(2)}, u32[]{:S(2)}) %collective-permute-start.6) | collective-permute-done | bytes 1568 | tf_op jit(solution)/shard_map/ppermute | solution.py:49
  48.6 1.8 collective-permute-start.7
  50.4 4.1 %collective-permute-done.7 = f32[3,128]{0,1:T(8,128)S(1)} collective-permute-done((f32[3,128]{0,1:T(8,128)S(1)}, f32[3,128]{0,1:T(8,128)S(1)}, u32[]{:S(2)}, u32[]{:S(2)}) %collective-permute-start.7) | collective-permute-done | bytes 1568 | tf_op jit(solution)/shard_map/ppermute | solution.py:49
  54.5 3.7 %collective-permute-start.8 = (f32[3,128]{0,1:T(8,128)S(1)}, f32[3,128]{0,1:T(8,128)S(1)}, u32[]{:S(2)}, u32[]{:S(2)}) collective-permute-start(f32[3,128]{0,1:T(8,128)S(1)} %add.58), channel_id=1, source_target_pairs={{0,4},{1,5},{2,6},{3,7},{4,0},{5,1},{6,2},{7,3},{8,12},{9,13},{10,... | collective-permute-start | bytes 4616 | tf_op jit(solution)/shard_map/ppermute | solution.py:49
  58.2 2.2 collective-permute-done.8
  60.5 3.3 %collective-permute-start.9 = (f32[3,128]{0,1:T(8,128)S(1)}, f32[3,128]{0,1:T(8,128)S(1)}, u32[]{:S(2)}, u32[]{:S(2)}) collective-permute-start(f32[3,128]{0,1:T(8,128)S(1)} %add.59), channel_id=1, source_target_pairs={{0,16},{1,17},{2,18},{3,19},{4,20},{5,21},{6,22},{7,23},{8,24},{9,... | collective-permute-start | bytes 4616 | tf_op jit(solution)/shard_map/ppermute | solution.py:49
  63.7 3.5 %shard_map.95 = (bf16[256,4096]{1,0:T(8,128)(2,1)S(1)}, bf16[256,4096]{1,0:T(8,128)(2,1)S(1)}) custom-call(s32[1]{0:T(128)} %bitcast.section_ref.refs_0_, bf16[256,4096]{1,0:T(8,128)(2,1)} %bitcast.91, bf16[256,4096]{1,0:T(8,128)(2,1)} %bitcast.88, f32[1,4096]{1,0:T(1,128)S(1)} %get-tuple-element.23.gain_ref.refs_3_), custom_call_target="tpu_custom_call" | custom-call | flops 131072 | bytes 131072 | tf_op jit(solution)/shard_map/pallas_call | solution.py:349
  67.3 1.4 copy-done
  70.0 4.8 %collective-permute-done.10 = f32[3,128]{0,1:T(8,128)S(1)} collective-permute-done((f32[3,128]{0,1:T(8,128)S(1)}, f32[3,128]{0,1:T(8,128)S(1)}, u32[]{:S(2)}, u32[]{:S(2)}) %collective-permute-start.10) | collective-permute-done | bytes 1568 | tf_op jit(solution)/shard_map/ppermute | solution.py:332
  74.9 77.7 %all-gather.2.cloned.1.call-done.kv_ref.w_ref.refs_4_ = bf16[4096,4864]{1,0:T(8,128)(2,1)} async-done(((bf16[128,4864]{1,0:T(8,128)(2,1)}), bf16[4096,4864]{1,0:T(8,128)(2,1)}) %all-gather.2.cloned.1.call-update) | async-done | bytes 39845904 | tf_op jit(solution)/shard_map/all_gather | solution.py:340
  152.6 2.4 shard_map.96
  155.0 6.2 %shard_map.97.refs_8_ = bf16[256,1024]{1,0:T(8,128)(2,1)S(1)} custom-call(s32[2]{0:T(128)S(1)} %bitcast.81, s32[1]{0:T(128)} %bitcast.section_ref.refs_0_, f32[3]{0:T(128)S(1)} %get-tuple-element.21.scale_ref.refs_2_, bf16[256,4096]{1,0:T(8,128)(2,1)S(1)} %get-tuple-element.8.xn_ref, bf16[4096,4864]{1,0:T(8,128)(2,1)} %all-gather.2.cloned.1.call-done.kv_ref.w_ref.refs_4_, ...), custom_call_target="tpu_custom_call" | custom-call | flops 33554432 | bytes 131072 | tf_op jit(solution)/shard_map/pallas_call | solution.py:128
  162.6 6.2 %shard_map.98.refs_9_ = bf16[256,1024]{1,0:T(8,128)(2,1)S(1)} custom-call(s32[2]{0:T(128)S(1)} %bitcast.82, s32[1]{0:T(128)} %bitcast.section_ref.refs_0_, f32[3]{0:T(128)S(1)} %get-tuple-element.21.scale_ref.refs_2_, bf16[256,4096]{1,0:T(8,128)(2,1)S(1)} %get-tuple-element.8.xn_ref, bf16[4096,4864]{1,0:T(8,128)(2,1)} %all-gather.2.cloned.1.call-done.kv_ref.w_ref.refs_4_, ...), custom_call_target="tpu_custom_call" | custom-call | flops 33554432 | bytes 131072 | tf_op jit(solution)/shard_map/pallas_call | solution.py:128
  170.1 6.2 %shard_map.99.refs_10_ = bf16[256,1024]{1,0:T(8,128)(2,1)S(1)} custom-call(s32[2]{0:T(128)S(1)} %bitcast.83, s32[1]{0:T(128)} %bitcast.section_ref.refs_0_, f32[3]{0:T(128)S(1)} %get-tuple-element.21.scale_ref.refs_2_, bf16[256,4096]{1,0:T(8,128)(2,1)S(1)} %get-tuple-element.8.xn_ref, bf16[4096,4864]{1,0:T(8,128)(2,1)} %all-gather.2.cloned.1.call-done.kv_ref.w_ref.refs_4_, ...), custom_call_target="tpu_custom_call" | custom-call | flops 33554432 | bytes 131072 | tf_op jit(solution)/shard_map/pallas_call | solution.py:128
  176.4 1.5 collective-permute-start.15
  177.9 6.2 %shard_map.100.refs_11_ = bf16[256,1024]{1,0:T(8,128)(2,1)S(1)} custom-call(s32[2]{0:T(128)S(1)} %bitcast.84, s32[1]{0:T(128)} %bitcast.section_ref.refs_0_, f32[3]{0:T(128)S(1)} %get-tuple-element.21.scale_ref.refs_2_, bf16[256,4096]{1,0:T(8,128)(2,1)S(1)} %get-tuple-element.8.xn_ref, bf16[4096,4864]{1,0:T(8,128)(2,1)} %all-gather.2.cloned.1.call-done.kv_ref.w_ref.refs_4_, ...), custom_call_target="tpu_custom_call" | custom-call | flops 33554432 | bytes 131072 | tf_op jit(solution)/shard_map/pallas_call | solution.py:128
  185.6 3.6 %collective-permute-done.14.refs_6_.refs_13_ = bf16[256,1024]{1,0:T(8,128)(2,1)S(1)} collective-permute-done((bf16[256,1024]{1,0:T(8,128)(2,1)S(1)}, bf16[256,1024]{1,0:T(8,128)(2,1)S(1)}, u32[]{:S(2)}, u32[]{:S(2)}) %collective-permute-start.14) | collective-permute-done | bytes 524320 | tf_op jit(solution)/shard_map/ppermute | solution.py:332
  189.2 11.2 %collective-permute-done.15.refs_7_.refs_14_ = bf16[256,1024]{1,0:T(8,128)(2,1)S(1)} collective-permute-done((bf16[256,1024]{1,0:T(8,128)(2,1)S(1)}, bf16[256,1024]{1,0:T(8,128)(2,1)S(1)}, u32[]{:S(2)}, u32[]{:S(2)}) %collective-permute-start.15) | collective-permute-done | bytes 524320 | tf_op jit(solution)/shard_map/ppermute | solution.py:332
  200.4 10.6 %collective-permute-done.16.refs_8_.refs_15_ = bf16[256,1024]{1,0:T(8,128)(2,1)S(1)} collective-permute-done((bf16[256,1024]{1,0:T(8,128)(2,1)S(1)}, bf16[256,1024]{1,0:T(8,128)(2,1)S(1)}, u32[]{:S(2)}, u32[]{:S(2)}) %collective-permute-start.16) | collective-permute-done | bytes 524320 | tf_op jit(solution)/shard_map/ppermute | solution.py:332
  215.7 25.5 %collective-permute-done.18 = bf16[256,512]{1,0:T(8,128)(2,1)S(1)} collective-permute-done((bf16[256,512]{1,0:T(8,128)(2,1)S(1)}, bf16[256,512]{1,0:T(8,128)(2,1)S(1)}, u32[]{:S(2)}, u32[]{:S(2)}) %collective-permute-start.18) | collective-permute-done | bytes 262176 | tf_op jit(solution)/shard_map/ppermute | solution.py:332
  241.2 23.6 %shard_map.102 = bf16[256,4096]{1,0:T(8,128)(2,1)} custom-call(s32[1]{0:T(128)} %bitcast.section_ref.refs_0_, s32[2]{0:T(128)S(1)} %bitcast.86, f32[6]{0:T(128)S(1)} %pad_maximum_fusion.2.refs_2_, f32[1,4096]{1,0:T(1,128)S(1)} %get-tuple-element.23.gain_ref.refs_3_, bf16[4096,4864]{1,0:T(8,128)(2,1)} %all-gather.2.cloned.1.call-done.kv_ref.w_ref.refs_4_, ...), custom_call_target="tpu_custom_call" | custom-call | flops 134217728 | bytes 524288 | tf_op jit(solution)/shard_map/pallas_call | solution.py:404
  (76 shorter events, 19.0 us)
Async XLA Ops:
  7.2 9.4 %copy-start.5 = (bf16[1,128,256]{2,1,0:T(8,128)(2,1)S(1)}, bf16[1,128,256]{2,1,0:T(8,128)(2,1)}, u32[]{:S(2)}) copy-start(bf16[1,128,256]{2,1,0:T(8,128)(2,1)} %param.9) | copy-start | bytes 196612
  7.2 9.4 %copy-start.7 = (bf16[1,3,128]{2,1,0:T(4,128)(2,1)S(1)}, bf16[1,3,128]{2,1,0:T(4,128)(2,1)}, u32[]{:S(2)}) copy-start(bf16[1,3,128]{2,1,0:T(4,128)(2,1)} %param.12) | copy-start | bytes 2308
  7.2 145.4 %all-gather.2.cloned.1.call-start = ((), (), s32[]{:S(2)}) async-start(), calls=%async_computation | async-start | bytes 41091072 | tf_op jit(solution)/shard_map/all_gather | solution.py:340
  8.1 8.6 %copy-start.4 = (bf16[1,128,4096]{2,1,0:T(8,128)(2,1)S(1)}, bf16[1,128,4096]{2,1,0:T(8,128)(2,1)}, u32[]{:S(2)}) copy-start(bf16[1,128,4096]{2,1,0:T(8,128)(2,1)} %param.8) | copy-start | bytes 3145732
  9.1 5.1 %collective-permute-start.12 = (bf16[144,256]{1,0:T(8,128)(2,1)S(1)}, bf16[144,256]{1,0:T(8,128)(2,1)S(1)}, u32[]{:S(2)}, u32[]{:S(2)}) collective-permute-start(bf16[144,256]{1,0:T(8,128)(2,1)S(1)} %pad_maximum_fusion.1), channel_id=1, source_target_pairs={{96,32},{97,33},{98,34},{99,35},{100,36},{101,37},{102,38},{103,39... | collective-permute-start | bytes 221192 | tf_op jit(solution)/shard_map/ppermute | solution.py:332
  12.2 2.0 collective-permute-start.11
  17.0 1.3 collective-permute-start
  18.3 3.8 %collective-permute-start.1 = (f32[34,128]{1,0:T(8,128)S(1)}, f32[34,128]{1,0:T(8,128)S(1)}, u32[]{:S(2)}, u32[]{:S(2)}) collective-permute-start(f32[34,128]{1,0:T(8,128)S(1)} %fusion.27), channel_id=1, source_target_pairs={{0,2},{1,3},{2,0},{3,1},{4,6},{5,7},{6,4},{7,5},{8,10},{9,11},{10,... | collective-permute-start | bytes 52232 | tf_op jit(solution)/shard_map/ppermute | solution.py:49
  22.1 3.9 %collective-permute-start.2 = (f32[34,128]{1,0:T(8,128)S(1)}, f32[34,128]{1,0:T(8,128)S(1)}, u32[]{:S(2)}, u32[]{:S(2)}) collective-permute-start(f32[34,128]{1,0:T(8,128)S(1)} %fusion.32), channel_id=1, source_target_pairs={{0,8},{1,9},{2,10},{3,11},{4,12},{5,13},{6,14},{7,15},{8,0},{9,1},... | collective-permute-start | bytes 52232 | tf_op jit(solution)/shard_map/ppermute | solution.py:49
  25.9 5.6 %collective-permute-start.3 = (f32[34,128]{1,0:T(8,128)S(1)}, f32[34,128]{1,0:T(8,128)S(1)}, u32[]{:S(2)}, u32[]{:S(2)}) collective-permute-start(f32[34,128]{1,0:T(8,128)S(1)} %add.50), channel_id=1, source_target_pairs={{0,4},{1,5},{2,6},{3,7},{4,0},{5,1},{6,2},{7,3},{8,12},{9,13},{10,... | collective-permute-start | bytes 52232 | tf_op jit(solution)/shard_map/ppermute | solution.py:49
  31.6 5.4 %collective-permute-start.4 = (f32[34,128]{1,0:T(8,128)S(1)}, f32[34,128]{1,0:T(8,128)S(1)}, u32[]{:S(2)}, u32[]{:S(2)}) collective-permute-start(f32[34,128]{1,0:T(8,128)S(1)} %add.51), channel_id=1, source_target_pairs={{0,16},{1,17},{2,18},{3,19},{4,20},{5,21},{6,22},{7,23},{8,24},{9,... | collective-permute-start | bytes 52232 | tf_op jit(solution)/shard_map/ppermute | solution.py:49
  41.1 1.3 collective-permute-start.5
  42.5 6.1 %collective-permute-start.6 = (f32[3,128]{0,1:T(8,128)S(1)}, f32[3,128]{0,1:T(8,128)S(1)}, u32[]{:S(2)}, u32[]{:S(2)}) collective-permute-start(f32[3,128]{0,1:T(8,128)S(1)} %broadcast_add_fusion), channel_id=1, source_target_pairs={{0,2},{1,3},{2,0},{3,1},{4,6},{5,7},{6,4},{7,5},{8,10},{9,11},{10,... | collective-permute-start | bytes 4616 | tf_op jit(solution)/shard_map/ppermute | solution.py:49
  48.6 5.9 %collective-permute-start.7 = (f32[3,128]{0,1:T(8,128)S(1)}, f32[3,128]{0,1:T(8,128)S(1)}, u32[]{:S(2)}, u32[]{:S(2)}) collective-permute-start(f32[3,128]{0,1:T(8,128)S(1)} %fusion.31), channel_id=1, source_target_pairs={{0,8},{1,9},{2,10},{3,11},{4,12},{5,13},{6,14},{7,15},{8,0},{9,1},... | collective-permute-start | bytes 4616 | tf_op jit(solution)/shard_map/ppermute | solution.py:49
  54.5 6.0 %collective-permute-start.8 = (f32[3,128]{0,1:T(8,128)S(1)}, f32[3,128]{0,1:T(8,128)S(1)}, u32[]{:S(2)}, u32[]{:S(2)}) collective-permute-start(f32[3,128]{0,1:T(8,128)S(1)} %add.58), channel_id=1, source_target_pairs={{0,4},{1,5},{2,6},{3,7},{4,0},{5,1},{6,2},{7,3},{8,12},{9,13},{10,... | collective-permute-start | bytes 4616 | tf_op jit(solution)/shard_map/ppermute | solution.py:49
  60.5 8.2 %collective-permute-start.9 = (f32[3,128]{0,1:T(8,128)S(1)}, f32[3,128]{0,1:T(8,128)S(1)}, u32[]{:S(2)}, u32[]{:S(2)}) collective-permute-start(f32[3,128]{0,1:T(8,128)S(1)} %add.59), channel_id=1, source_target_pairs={{0,16},{1,17},{2,18},{3,19},{4,20},{5,21},{6,22},{7,23},{8,24},{9,... | collective-permute-start | bytes 4616 | tf_op jit(solution)/shard_map/ppermute | solution.py:49
  63.7 5.0 %copy-start.8 = (f32[1,3]{1,0:T(1,128)S(1)}, f32[1,3]{1,0:T(1,128)}, u32[]{:S(2)}) copy-start(f32[1,3]{1,0:T(1,128)} %param.10) | copy-start | bytes 40
  67.3 1.4 copy-start
  68.7 6.2 %collective-permute-start.10 = (f32[3,128]{0,1:T(8,128)S(1)}, f32[3,128]{0,1:T(8,128)S(1)}, u32[]{:S(2)}, u32[]{:S(2)}) collective-permute-start(f32[3,128]{0,1:T(8,128)S(1)} %broadcast_in_dim.30), channel_id=1, source_target_pairs={{64,96},{65,97},{66,98},{67,99},{68,100},{69,101},{70,102},{71,103... | collective-permute-start | bytes 4616 | tf_op jit(solution)/shard_map/ppermute | solution.py:332
  152.6 2.5 copy-start.1
  152.6 2.5 copy-start.3
  161.3 24.3 %collective-permute-start.13 = (bf16[256,1024]{1,0:T(8,128)(2,1)S(1)}, bf16[256,1024]{1,0:T(8,128)(2,1)S(1)}, u32[]{:S(2)}, u32[]{:S(2)}) collective-permute-start(bf16[256,1024]{1,0:T(8,128)(2,1)S(1)} %shard_map.97.refs_8_), channel_id=1, source_target_pairs={{0,32},{64,96},{1,33},{65,97},{2,34},{66,98},{3,35},{67,99},{4,36}... | collective-permute-start | bytes 1572872 | tf_op jit(solution)/shard_map/ppermute | solution.py:332
  168.8 20.3 %collective-permute-start.14 = (bf16[256,1024]{1,0:T(8,128)(2,1)S(1)}, bf16[256,1024]{1,0:T(8,128)(2,1)S(1)}, u32[]{:S(2)}, u32[]{:S(2)}) collective-permute-start(bf16[256,1024]{1,0:T(8,128)(2,1)S(1)} %shard_map.98.refs_9_), channel_id=1, source_target_pairs={{0,32},{64,96},{1,33},{65,97},{2,34},{66,98},{3,35},{67,99},{4,36}... | collective-permute-start | bytes 1572872 | tf_op jit(solution)/shard_map/ppermute | solution.py:332
  176.4 9.1 %copy-start.6 = (bf16[1,4096]{1,0:T(2,128)(2,1)S(1)}, bf16[1,4096]{1,0:T(2,128)(2,1)}, u32[]{:S(2)}) copy-start(bf16[1,4096]{1,0:T(2,128)(2,1)} %param.11) | copy-start | bytes 24580
  176.4 24.0 %collective-permute-start.15 = (bf16[256,1024]{1,0:T(8,128)(2,1)S(1)}, bf16[256,1024]{1,0:T(8,128)(2,1)S(1)}, u32[]{:S(2)}, u32[]{:S(2)}) collective-permute-start(bf16[256,1024]{1,0:T(8,128)(2,1)S(1)} %shard_map.99.refs_10_), channel_id=1, source_target_pairs={{0,32},{64,96},{1,33},{65,97},{2,34},{66,98},{3,35},{67,99},{4,36}... | collective-permute-start | bytes 1572872 | tf_op jit(solution)/shard_map/ppermute | solution.py:332
  184.1 26.8 %collective-permute-start.16 = (bf16[256,1024]{1,0:T(8,128)(2,1)S(1)}, bf16[256,1024]{1,0:T(8,128)(2,1)S(1)}, u32[]{:S(2)}, u32[]{:S(2)}) collective-permute-start(bf16[256,1024]{1,0:T(8,128)(2,1)S(1)} %shard_map.100.refs_11_), channel_id=1, source_target_pairs={{0,32},{64,96},{1,33},{65,97},{2,34},{66,98},{3,35},{67,99},{4,36}... | collective-permute-start | bytes 1572872 | tf_op jit(solution)/shard_map/ppermute | solution.py:332
  211.6 1.4 copy-start.2
  213.0 28.2 %collective-permute-start.18 = (bf16[256,512]{1,0:T(8,128)(2,1)S(1)}, bf16[256,512]{1,0:T(8,128)(2,1)S(1)}, u32[]{:S(2)}, u32[]{:S(2)}) collective-permute-start(bf16[256,512]{1,0:T(8,128)(2,1)S(1)} %get-tuple-element.12), channel_id=1, source_target_pairs={{32,96},{33,97},{34,98},{35,99},{36,100},{37,101},{38,102},{39,103... | collective-permute-start | bytes 786440 | tf_op jit(solution)/shard_map/ppermute | solution.py:332
  214.3 26.9 %collective-permute-start.17 = (bf16[256,512]{1,0:T(8,128)(2,1)S(1)}, bf16[256,512]{1,0:T(8,128)(2,1)S(1)}, u32[]{:S(2)}, u32[]{:S(2)}) collective-permute-start(bf16[256,512]{1,0:T(8,128)(2,1)S(1)} %get-tuple-element.12), channel_id=1, source_target_pairs={{32,64},{33,65},{34,66},{35,67},{36,68},{37,69},{38,70},{39,71},{4... | collective-permute-start | bytes 786440 | tf_op jit(solution)/shard_map/ppermute | solution.py:332
Sparse Core Ops, SparseCore 0:
  16.7 135.8 all-gather.1

commit v3 on v2

--- a/solution.py
+++ b/solution.py
@@ -14,7 +14,7 @@
 BF16 = jnp.bfloat16
 VMEM_LIMIT = 48 * 1024 * 1024
 BLOCK = 512
-PIECE = 1024
+PIECES = (512, 1024, 1024, 1024, 512)
 SLOTS = 3
 LOG2E_SCALED = math.log2(math.e) / math.sqrt(HEAD)
 ANY = pl.BlockSpec(memory_space=pl.ANY)
@@ -62,6 +62,42 @@
 def cost(flops, size, exps=0):
     share = 64
     return pl.CostEstimate(flops=int(flops) // share, bytes_accessed=int(size) // share, transcendentals=int(exps) // share)
+
+
+def half_kernel(core_ref, full_ref, *refs):
+    out_ref, sem = refs[-2:]
+    rows, width = out_ref.shape
+    at = pl.ds(pl.multiple_of(core_ref[0] * rows, rows), rows)
+    copy = pltpu.make_async_copy(full_ref.at[at, pl.ds(full_ref.shape[1] - width, width)], out_ref, sem)
+    copy.start()
+    copy.wait()
+
+
+def half_rows(full, width, core, *late):
+    return pl.pallas_call(
+        half_kernel,
+        out_shape=jax.ShapeDtypeStruct((full.shape[0] // 2, width), full.dtype),
+        in_specs=[SMEM] + [ANY] * (1 + len(late)),
+        out_specs=VMEM,
+        scratch_shapes=[pltpu.SemaphoreType.DMA],
+        compiler_params=params(),
+        cost_estimate=cost(0, 0),
+    )(core, full, *late)
+
+
+def copy_kernel(x_ref, *refs):
+    refs[-1][...] = x_ref[...]
+
+
+def copied(x, *late):
+    return pl.pallas_call(
+        copy_kernel,
+        out_shape=jax.ShapeDtypeStruct(x.shape, x.dtype),
+        in_specs=[VMEM] + [ANY] * len(late),
+        out_specs=VMEM,
+        compiler_params=params(),
+        cost_estimate=cost(0, 0),
+    )(x, *late)
 
 
 def norm_into(xn_ref, x_ref, gain_ref, row):
@@ -105,11 +141,12 @@
     norm_into(xn_ref, x_ref, gain_ref, 0)
 
 
-def project_kernel(xn_ref, kv_ref, keys_ref, values_ref):
+def project_kernel(xn_ref, kv_ref, late_ref, keys_ref, values_ref):
     project_into(keys_ref, values_ref, xn_ref[...], kv_ref[...])
 
 
-def part_kernel(lengths_ref, section_ref, scale_ref, xn_ref, w_ref, k_ref, v_ref, x_ref, out_ref):
+def part_kernel(lengths_ref, section_ref, scale_ref, xn_ref, w_ref, k_ref, v_ref, x_ref, *refs):
+    out_ref = refs[-1]
     q = (dot(xn_ref[...], w_ref[...]) * scale_ref[0]).astype(BF16)
 
     @pl.when(section_ref[0] != 2)
@@ -121,14 +158,14 @@
         out_ref[...] = q
 
 
-def layer_part(xn, full, keys, values, x, at, lengths, section, scales):
+def layer_part(xn, full, keys, values, x, at, piece, lengths, section, scales, late):
     rows, width = xn.shape
     first = at // BLOCK
     whole = lambda a: pl.BlockSpec(a.shape, lambda j: (0, 0))
     return pl.pallas_call(
         part_kernel,
-        grid=(PIECE // BLOCK,),
-        out_shape=jax.ShapeDtypeStruct((rows, PIECE), BF16),
+        grid=(piece // BLOCK,),
+        out_shape=jax.ShapeDtypeStruct((rows, piece), BF16),
         in_specs=[
             SMEM,
             SMEM,
@@ -138,11 +175,12 @@
             whole(keys),
             whole(values),
             pl.BlockSpec((rows, BLOCK), lambda j: (0, first + j)),
-        ],
+        ]
+        + [ANY] * len(late),
         out_specs=pl.BlockSpec((rows, BLOCK), lambda j: (0, j)),
         compiler_params=params(),
-        cost_estimate=cost(2 * rows * width * PIECE, 2 * width * PIECE, rows * PIECE),
-    )(lengths, section, scales, xn, full, keys, values, x)
+        cost_estimate=cost(2 * rows * width * piece, 2 * width * piece, rows * piece),
+    )(lengths, section, scales, xn, full, keys, values, x, *late)
 
 
 def stream_layer(full, buf, sems, xn_ref, q_ref, k_ref, v_ref, x_ref, lengths_ref, scale_ref, out_ref):
@@ -195,10 +233,10 @@
 
 
 def encoder_kernel(count, *refs):
-    section_ref, lengths_ref, scale_ref, gain_ref, full = refs[:5]
-    pieces = refs[5 : 5 + count]
-    out_ref, cross_ref = refs[5 + count : 7 + count]
-    buf, sems, xn_ref, q_ref, x_ref, x_sems, kv_buf, kv_sems, k_ref, v_ref = refs[7 + count :]
+    section_ref, core_ref, lengths_ref, scale_ref, gain_ref, full = refs[:6]
+    kv_refs, pieces = refs[6:10], refs[10 : 10 + count]
+    out_ref, cross_ref = refs[10 + count : 12 + count]
+    buf, sems, xn_ref, q_ref, x_ref, x_sems, kv_buf, kv_sems, k_ref, v_ref = refs[12 + count :]
     width = x_ref.shape[1]
 
     @pl.when(section_ref[0] == 1)
@@ -206,12 +244,16 @@
         arrive = bring(pieces, x_ref, x_sems)
         for copy in arrive:
             copy.start()
+        half = width // 2
         kv_copies = [
-            pltpu.make_async_copy(
-                full.at[:, pl.ds(width + i * 2 * HEAD, 2 * HEAD)], kv_buf.at[i], kv_sems.at[i]
+            pltpu.make_async_copy(full.at[:, pl.ds(width, 2 * HEAD)], kv_buf.at[0], kv_sems.at[0])
+        ]
+        for i, ref in enumerate(kv_refs):
+            kind = core_ref[0] if i % 2 == 0 else 1 - core_ref[0]
+            rows = pl.ds(pl.multiple_of(kind * half, half), half)
+            kv_copies.append(
+                pltpu.make_async_copy(ref, kv_buf.at[1 + i // 2, rows], kv_sems.at[1 + i])
             )
-            for i in range(3)
-        ]
         for copy in kv_copies[:1]:
             copy.start()
         start, run = stream_layer(
@@ -331,14 +373,11 @@
 
     hop = lambda value, pairs: lax.ppermute(value, "section", pairs)
 
-    extra = jnp.concatenate([kv_part, gain.reshape(-1, 2 * HEAD)], 0)
-    extra2 = hop(extra, [(2, 1)])
-    extra3 = hop(extra, [(3, 1)])
-    local = kv_part.shape[0]
-
-    full = jnp.concatenate([weight, kv_part, extra2[:local], extra3[:local]], 1)
-    full = lax.all_gather(full, "fsdp", axis=0, tiled=True)
-
+    full = lax.all_gather(jnp.concatenate([weight, kv_part], 1), "fsdp", axis=0, tiled=True)
+
+    gain_rows = gain.reshape(-1, 128)
+    gain2 = hop(gain_rows, [(2, 1)])
+    gain3 = hop(gain_rows, [(3, 1)])
     along = spectral_along(weight, kv_part, start_rows).reshape(-1)
     images = spectral_images(weight, kv_part, along)
     squares = jnp.broadcast_to(jnp.sum(images * images, axis=1)[:, None], (3, 128))
@@ -355,22 +394,34 @@
         cost_estimate=cost(8 * rows * width, 8 * rows * width),
     )(section, source2, target2, wide_gain)
 
+    core = lax.rem(lax.axis_index("fsdp"), 2).astype(jnp.int32).reshape(1)
+    kv_half = half_rows(full, 2 * HEAD, core, scales, scales2, gain2, gain3, xn0)
+    kv2 = hop(kv_half, [(3, 2), (2, 1)])
+
     kv_block = pl.BlockSpec((width, 2 * HEAD), lambda j: (0, width // (2 * HEAD)))
     whole = lambda shape: pl.BlockSpec(shape, lambda j: (0, 0))
     keys, values = pl.pallas_call(
         project_kernel,
         grid=(1,),
         out_shape=(head_shape, head_shape),
-        in_specs=[whole((rows, width)), kv_block],
+        in_specs=[whole((rows, width)), kv_block, ANY],
         out_specs=(whole((rows, HEAD)), whole((rows, HEAD))),
         compiler_params=params(),
         cost_estimate=cost(4 * rows * width * HEAD, 4 * width * HEAD),
-    )(xn0, full)
+    )(xn0, full, kv_half)
 
     made, passed = [], []
-    for at in range(0, width, PIECE):
-        made.append(layer_part(xn0, full, keys, values, x0, at, seq_lengths, section, scales))
+    at = 0
+    for i, piece in enumerate(PIECES):
+        late = made[-1:] + (passed[i - 2 : i - 1] if i >= 2 else [])
+        made.append(layer_part(xn0, full, keys, values, x0, at, piece, seq_lengths, section, scales, late))
         passed.append(hop(made[-1], [(0, 1), (2, 3)]))
+        at += piece
+        if i == 2:
+            kv2 = copied(kv2, made[-1], passed[1])
+            kv3 = hop(kv2, [(2, 1)])
+    kv3 = copied(kv3, made[-1], passed[3])
+    kv_halves = [kv2, send(kv2, CORE_SWAP), kv3, send(kv3, CORE_SWAP)]
 
     scratch = [
         pltpu.VMEM((SLOTS, width, BLOCK), BF16),
@@ -381,24 +432,24 @@
         pltpu.SemaphoreType.DMA((len(made),)),
     ]
     n = len(made)
-    all_gains = jnp.stack([gain, extra2[local:].reshape(-1), extra3[local:].reshape(-1)]).astype(F32)
+    all_gains = jnp.concatenate([gain[None], gain2.reshape(1, width), gain3.reshape(1, width)], 0).astype(F32)
     all_scales = jnp.concatenate([scales, jnp.where(section == 3, scales2, scales)])
     layer_cost = cost(2 * rows * width * width, 2 * width * width, rows * width)
     out1, cross = pl.pallas_call(
         functools.partial(encoder_kernel, n),
         out_shape=(row_shape, jax.ShapeDtypeStruct((rows, 4 * HEAD), BF16)),
-        in_specs=[SMEM] * 3 + [VMEM] + [ANY] * (1 + n),
+        in_specs=[SMEM] * 4 + [VMEM] + [ANY] * (5 + n),
         out_specs=(VMEM, VMEM),
         scratch_shapes=scratch
         + [
             pltpu.VMEM((3, width, 2 * HEAD), BF16),
-            pltpu.SemaphoreType.DMA((3,)),
+            pltpu.SemaphoreType.DMA((5,)),
             pltpu.VMEM((rows, HEAD), BF16),
             pltpu.VMEM((rows, HEAD), BF16),
         ],
         compiler_params=params(),
         cost_estimate=layer_cost,
-    )(section, seq_lengths, scales, all_gains, full, *passed)
+    )(section, core, seq_lengths, scales, all_gains, full, *kv_halves, *passed)
     cross = hop(cross, [(1, 2)]) + hop(cross, [(1, 3)])
 
     result = pl.pallas_call(

time: 272 us -> 278 us (1.022)
  Pallas kernels: 55.2 us -> 60.1 us
  starting transfers between devices: 33.4 us -> 37.3 us
    all_gather x1, waiting for transfers between devices: 77.7 us -> 65.6 us  [shards(): lax.all_gather(jnp.concatenate([weight, kv_part], 1), 'fsdp', axis=0, til...]
    ppermute x9 -> x12, waiting for transfers between devices: 57 us -> 66.2 us  [shards(): hop = lambda value, pairs: lax.ppermute(value, 'section', pairs)]
    ppermute x9 -> x12, starting transfers between devices: 12.4 us -> 16.5 us  [shards(): hop = lambda value, pairs: lax.ppermute(value, 'section', pairs)]
    pallas_call x4 -> x8, Pallas kernels: 25 us -> 28.5 us  [the longest x5 27.1 us: layer_part(): pl.pallas_call(part_kernel, grid=(piece // BLOCK,), out_shape=jax.ShapeDt...]
    ppermute x10 -> x12, waiting for transfers between devices: 21.5 us -> 23.5 us  [send(): return lax.ppermute(value, 'fsdp', pairs)]
    ppermute x10 -> x12, starting transfers between devices: 20.9 us -> 20.8 us  [send(): return lax.ppermute(value, 'fsdp', pairs)]
  transfers between devices with their start and end apart: 20 -> 25, of which waited for: 16 -> 16; matrix products, arithmetic and copies ran while one was open for 1% -> 1% of each run, Pallas kernels for 8% -> 12%
where the time goes in v3:
time: 278 us; the launch traced here: 277 us
  waiting for transfers between devices  155 us (56%)
  Pallas kernels  60.1 us (22%)
  starting transfers between devices  37.3 us (13%)
  between operations  16.6 us (6%)
  other arithmetic  4.21 us (2%)
  local copies, waits for them, and re-layouts  2.95 us (1%)
    ppermute x12, waiting for transfers between devices, shards(): hop = lambda value, pairs: lax.ppermute(value, 'section', pairs)  66.2 us
    all_gather x1, waiting for transfers between devices, shards(): lax.all_gather(jnp.concatenate([weight, kv_part], 1), 'fsdp', axis=0, til...  65.6 us
    pallas_call x5, Pallas kernels, layer_part(): pl.pallas_call(part_kernel, grid=(piece // BLOCK,), out_shape=jax.ShapeDt...  27.1 us
    pallas_call x1, Pallas kernels, shards(): pl.pallas_call(functools.partial(decoder_kernel, n), out_shape=row_shape,...  23.8 us
    ppermute x12, waiting for transfers between devices, send(): return lax.ppermute(value, 'fsdp', pairs)  23.5 us
    ppermute x12, starting transfers between devices, send(): return lax.ppermute(value, 'fsdp', pairs)  20.8 us
    ppermute x12, starting transfers between devices, shards(): hop = lambda value, pairs: lax.ppermute(value, 'section', pairs)  16.5 us
  transfers between devices with their start and end apart: 25, of which 16 were waited for; matrix products, arithmetic and copies ran while one was open for 1% of the time, Pallas kernels for 12%

profile of v3, /device:TPU:24, one launch (start us, length us, event | category | flops | bytes accessed | tf_op | source)
XLA Modules:
  0.0 277.5 jit_solution(13288640726739265201)
XLA Ops:
  7.2 2.4 pad_maximum_fusion
  11.4 1.9 collective-permute-start.1
  13.3 1.9 collective-permute-done.1
  16.7 2.3 collective-permute-done.2
  19.0 3.9 %collective-permute-start.3 = (f32[34,128]{1,0:T(8,128)S(1)}, f32[34,128]{1,0:T(8,128)S(1)}, u32[]{:S(2)}, u32[]{:S(2)}) collective-permute-start(f32[34,128]{1,0:T(8,128)S(1)} %add.50), channel_id=1, source_target_pairs={{0,4},{1,5},{2,6},{3,7},{4,0},{5,1},{6,2},{7,3},{8,12},{9,13},{10,... | collective-permute-start | bytes 52232 | tf_op jit(solution)/shard_map/ppermute | solution.py:49
  22.9 1.8 collective-permute-done.3
  24.7 3.0 %collective-permute-start.4 = (f32[34,128]{1,0:T(8,128)S(1)}, f32[34,128]{1,0:T(8,128)S(1)}, u32[]{:S(2)}, u32[]{:S(2)}) collective-permute-start(f32[34,128]{1,0:T(8,128)S(1)} %add.51), channel_id=1, source_target_pairs={{0,16},{1,17},{2,18},{3,19},{4,20},{5,21},{6,22},{7,23},{8,24},{9,... | collective-permute-start | bytes 52232 | tf_op jit(solution)/shard_map/ppermute | solution.py:49
  27.7 2.7 collective-permute-done.4
  35.9 1.6 collective-permute-start.6
  37.5 4.5 %collective-permute-done.6 = f32[3,128]{0,1:T(8,128)S(1)} collective-permute-done((f32[3,128]{0,1:T(8,128)S(1)}, f32[3,128]{0,1:T(8,128)S(1)}, u32[]{:S(2)}, u32[]{:S(2)}) %collective-permute-start.6) | collective-permute-done | bytes 1568 | tf_op jit(solution)/shard_map/ppermute | solution.py:49
  43.6 2.8 %collective-permute-done.7 = f32[3,128]{0,1:T(8,128)S(1)} collective-permute-done((f32[3,128]{0,1:T(8,128)S(1)}, f32[3,128]{0,1:T(8,128)S(1)}, u32[]{:S(2)}, u32[]{:S(2)}) %collective-permute-start.7) | collective-permute-done | bytes 1568 | tf_op jit(solution)/shard_map/ppermute | solution.py:49
  46.3 3.7 %collective-permute-start.8 = (f32[3,128]{0,1:T(8,128)S(1)}, f32[3,128]{0,1:T(8,128)S(1)}, u32[]{:S(2)}, u32[]{:S(2)}) collective-permute-start(f32[3,128]{0,1:T(8,128)S(1)} %add.58), channel_id=1, source_target_pairs={{0,4},{1,5},{2,6},{3,7},{4,0},{5,1},{6,2},{7,3},{8,12},{9,13},{10,... | collective-permute-start | bytes 4616 | tf_op jit(solution)/shard_map/ppermute | solution.py:49
  50.1 2.2 collective-permute-done.8
  52.3 3.1 %collective-permute-start.9 = (f32[3,128]{0,1:T(8,128)S(1)}, f32[3,128]{0,1:T(8,128)S(1)}, u32[]{:S(2)}, u32[]{:S(2)}) collective-permute-start(f32[3,128]{0,1:T(8,128)S(1)} %add.59), channel_id=1, source_target_pairs={{0,16},{1,17},{2,18},{3,19},{4,20},{5,21},{6,22},{7,23},{8,24},{9,... | collective-permute-start | bytes 4616 | tf_op jit(solution)/shard_map/ppermute | solution.py:49
  55.5 3.0 %collective-permute-done.9 = f32[3,128]{0,1:T(8,128)S(1)} collective-permute-done((f32[3,128]{0,1:T(8,128)S(1)}, f32[3,128]{0,1:T(8,128)S(1)}, u32[]{:S(2)}, u32[]{:S(2)}) %collective-permute-start.9) | collective-permute-done | bytes 1568 | tf_op jit(solution)/shard_map/ppermute | solution.py:49
  59.9 2.3 collective-permute-start.12
  62.8 3.5 %shard_map.95 = (bf16[256,4096]{1,0:T(8,128)(2,1)S(1)}, bf16[256,4096]{1,0:T(8,128)(2,1)S(1)}) custom-call(s32[1]{0:T(128)} %bitcast.section_ref.refs_0_, bf16[256,4096]{1,0:T(8,128)(2,1)} %bitcast.98, bf16[256,4096]{1,0:T(8,128)(2,1)} %bitcast.95, f32[1,4096]{1,0:T(1,128)S(1)} %get-tuple-element.23.gain_ref.refs_3_), custom_call_target="tpu_custom_call" | custom-call | flops 131072 | bytes 131072 | tf_op jit(solution)/shard_map/pallas_call | solution.py:388
  67.7 65.6 %all-gather.2.cloned.1.call-done.full_ref.kv_ref.w_ref.refs_5_.refs_4_ = bf16[4096,4352]{1,0:T(8,128)(2,1)} async-done(((bf16[128,4352]{1,0:T(8,128)(2,1)}), bf16[4096,4352]{1,0:T(8,128)(2,1)}) %all-gather.2.cloned.1.call-update) | async-done | bytes 35651600 | tf_op jit(solution)/shard_map/all_gather | solution.py:376
  134.5 2.9 %collective-permute-start.13 = (bf16[2048,256]{1,0:T(8,128)(2,1)S(1)}, bf16[2048,256]{1,0:T(8,128)(2,1)S(1)}, u32[]{:S(2)}, u32[]{:S(2)}) collective-permute-start(bf16[2048,256]{1,0:T(8,128)(2,1)S(1)} %shard_map.96.late_ref), channel_id=1, source_target_pairs={{96,64},{64,32},{97,65},{65,33},{98,66},{66,34},{99,67},{67,35},{1... | collective-permute-start | bytes 3145736 | tf_op jit(solution)/shard_map/ppermute | solution.py:374
  137.4 2.3 shard_map.97
  139.8 4.2 %shard_map.98.refs_0_.refs_8_ = bf16[256,512]{1,0:T(8,128)(2,1)S(1)} custom-call(s32[2]{0:T(128)S(1)} %bitcast.87, s32[1]{0:T(128)} %bitcast.section_ref.refs_0_, f32[3]{0:T(128)S(1)} %get-tuple-element.21.refs_0_.scale_ref.refs_3_, bf16[256,4096]{1,0:T(8,128)(2,1)S(1)} %get-tuple-element.8.refs_4_.xn_ref, ...), custom_call_target="tpu_custom_call" | custom-call | flops 16777216 | bytes 65536 | tf_op jit(solution)/shard_map/pallas_call | solution.py:165
  143.9 6.2 %shard_map.99.refs_0_.refs_9_ = bf16[256,1024]{1,0:T(8,128)(2,1)S(1)} custom-call(s32[2]{0:T(128)S(1)} %bitcast.88, s32[1]{0:T(128)} %bitcast.section_ref.refs_0_, f32[3]{0:T(128)S(1)} %get-tuple-element.21.refs_0_.scale_ref.refs_3_, bf16[256,4096]{1,0:T(8,128)(2,1)S(1)} %get-tuple-element.8.refs_4_.xn_ref, ...), custom_call_target="tpu_custom_call" | custom-call | flops 33554432 | bytes 131072 | tf_op jit(solution)/shard_map/pallas_call | solution.py:165
  152.8 18.7 %collective-permute-done.14.refs_1_.refs_10_.refs_13_ = bf16[256,512]{1,0:T(8,128)(2,1)S(1)} collective-permute-done((bf16[256,512]{1,0:T(8,128)(2,1)S(1)}, bf16[256,512]{1,0:T(8,128)(2,1)S(1)}, u32[]{:S(2)}, u32[]{:S(2)}) %collective-permute-start.14) | collective-permute-done | bytes 262176 | tf_op jit(solution)/shard_map/ppermute | solution.py:374
  171.5 6.3 %shard_map.100.refs_0_.refs_10_ = bf16[256,1024]{1,0:T(8,128)(2,1)S(1)} custom-call(s32[2]{0:T(128)S(1)} %bitcast.89, s32[1]{0:T(128)} %bitcast.section_ref.refs_0_, f32[3]{0:T(128)S(1)} %get-tuple-element.21.refs_0_.scale_ref.refs_3_, bf16[256,4096]{1,0:T(8,128)(2,1)S(1)} %get-tuple-element.8.refs_4_.xn_ref, ...), custom_call_target="tpu_custom_call" | custom-call | flops 33554432 | bytes 131072 | tf_op jit(solution)/shard_map/pallas_call | solution.py:165
  180.1 6.2 %shard_map.102.refs_0_.refs_11_ = bf16[256,1024]{1,0:T(8,128)(2,1)S(1)} custom-call(s32[2]{0:T(128)S(1)} %bitcast.90, s32[1]{0:T(128)} %bitcast.section_ref.refs_0_, f32[3]{0:T(128)S(1)} %get-tuple-element.21.refs_0_.scale_ref.refs_3_, bf16[256,4096]{1,0:T(8,128)(2,1)S(1)} %get-tuple-element.8.refs_4_.xn_ref, ...), custom_call_target="tpu_custom_call" | custom-call | flops 33554432 | bytes 131072 | tf_op jit(solution)/shard_map/pallas_call | solution.py:165
  187.7 7.7 %collective-permute-done.18.refs_1_.refs_12_.refs_15_ = bf16[256,1024]{1,0:T(8,128)(2,1)S(1)} collective-permute-done((bf16[256,1024]{1,0:T(8,128)(2,1)S(1)}, bf16[256,1024]{1,0:T(8,128)(2,1)S(1)}, u32[]{:S(2)}, u32[]{:S(2)}) %collective-permute-start.18) | collective-permute-done | bytes 524320 | tf_op jit(solution)/shard_map/ppermute | solution.py:374
  195.4 4.2 %shard_map.103.refs_0_.refs_12_ = bf16[256,512]{1,0:T(8,128)(2,1)S(1)} custom-call(s32[2]{0:T(128)S(1)} %bitcast.91, s32[1]{0:T(128)} %bitcast.section_ref.refs_0_, f32[3]{0:T(128)S(1)} %get-tuple-element.21.refs_0_.scale_ref.refs_3_, bf16[256,4096]{1,0:T(8,128)(2,1)S(1)} %get-tuple-element.8.refs_4_.xn_ref, ...), custom_call_target="tpu_custom_call" | custom-call | flops 16777216 | bytes 65536 | tf_op jit(solution)/shard_map/pallas_call | solution.py:165
  199.7 5.1 %collective-permute-done.19.refs_1_.refs_13_.refs_16_ = bf16[256,1024]{1,0:T(8,128)(2,1)S(1)} collective-permute-done((bf16[256,1024]{1,0:T(8,128)(2,1)S(1)}, bf16[256,1024]{1,0:T(8,128)(2,1)S(1)}, u32[]{:S(2)}, u32[]{:S(2)}) %collective-permute-start.19) | collective-permute-done | bytes 524320 | tf_op jit(solution)/shard_map/ppermute | solution.py:374
  206.3 9.2 %collective-permute-done.21.refs_14_.refs_17_ = bf16[256,512]{1,0:T(8,128)(2,1)S(1)} collective-permute-done((bf16[256,512]{1,0:T(8,128)(2,1)S(1)}, bf16[256,512]{1,0:T(8,128)(2,1)S(1)}, u32[]{:S(2)}, u32[]{:S(2)}) %collective-permute-start.21) | collective-permute-done | bytes 262176 | tf_op jit(solution)/shard_map/ppermute | solution.py:374
  216.5 2.0 shard_map.105
  221.3 25.4 %collective-permute-done.23 = bf16[256,512]{1,0:T(8,128)(2,1)S(1)} collective-permute-done((bf16[256,512]{1,0:T(8,128)(2,1)S(1)}, bf16[256,512]{1,0:T(8,128)(2,1)S(1)}, u32[]{:S(2)}, u32[]{:S(2)}) %collective-permute-start.23) | collective-permute-done | bytes 262176 | tf_op jit(solution)/shard_map/ppermute | solution.py:374
  246.8 23.8 %shard_map.106 = bf16[256,4096]{1,0:T(8,128)(2,1)} custom-call(s32[1]{0:T(128)} %bitcast.section_ref.refs_0_, s32[2]{0:T(128)S(1)} %bitcast.93, f32[6]{0:T(128)S(1)} %pad_maximum_fusion.1.refs_2_, f32[1,4096]{1,0:T(1,128)S(1)} %get-tuple-element.23.gain_ref.refs_3_, bf16[4096,4352]{1,0:T(8,128)(2,1)} %all-gather.2.cloned.1.call-done.full_ref.kv_ref.w_ref.refs_5_.refs_4_, ...), custom_call_target="tpu_custom_call" | custom-call | flops 134217728 | bytes 524288 | tf_op jit(solution)/shard_map/pallas_call | solution.py:455
  (85 shorter events, 24.4 us)
Async XLA Ops:
  7.2 2.5 copy-start.5
  7.2 2.7 copy-start.3
  7.2 2.5 copy-start.7
  7.2 126.0 %all-gather.2.cloned.1.call-start = ((), (), s32[]{:S(2)}) async-start(), calls=%async_computation | async-start | bytes 36765696 | tf_op jit(solution)/shard_map/all_gather | solution.py:376
  9.7 48.8 %copy-start.8 = (f32[1,3]{1,0:T(1,128)S(1)}, f32[1,3]{1,0:T(1,128)}, u32[]{:S(2)}) copy-start(f32[1,3]{1,0:T(1,128)} %param.10) | copy-start | bytes 40
  9.7 50.1 %copy-start.6 = (bf16[1,4096]{1,0:T(2,128)(2,1)S(1)}, bf16[1,4096]{1,0:T(2,128)(2,1)}, u32[]{:S(2)}) copy-start(bf16[1,4096]{1,0:T(2,128)(2,1)} %param.11) | copy-start | bytes 24580
  10.1 1.3 collective-permute-start
  11.4 3.8 %collective-permute-start.1 = (f32[34,128]{1,0:T(8,128)S(1)}, f32[34,128]{1,0:T(8,128)S(1)}, u32[]{:S(2)}, u32[]{:S(2)}) collective-permute-start(f32[34,128]{1,0:T(8,128)S(1)} %fusion.27), channel_id=1, source_target_pairs={{0,2},{1,3},{2,0},{3,1},{4,6},{5,7},{6,4},{7,5},{8,10},{9,11},{10,... | collective-permute-start | bytes 52232 | tf_op jit(solution)/shard_map/ppermute | solution.py:49
  15.2 3.9 %collective-permute-start.2 = (f32[34,128]{1,0:T(8,128)S(1)}, f32[34,128]{1,0:T(8,128)S(1)}, u32[]{:S(2)}, u32[]{:S(2)}) collective-permute-start(f32[34,128]{1,0:T(8,128)S(1)} %fusion.32), channel_id=1, source_target_pairs={{0,8},{1,9},{2,10},{3,11},{4,12},{5,13},{6,14},{7,15},{8,0},{9,1},... | collective-permute-start | bytes 52232 | tf_op jit(solution)/shard_map/ppermute | solution.py:49
  19.0 5.6 %collective-permute-start.3 = (f32[34,128]{1,0:T(8,128)S(1)}, f32[34,128]{1,0:T(8,128)S(1)}, u32[]{:S(2)}, u32[]{:S(2)}) collective-permute-start(f32[34,128]{1,0:T(8,128)S(1)} %add.50), channel_id=1, source_target_pairs={{0,4},{1,5},{2,6},{3,7},{4,0},{5,1},{6,2},{7,3},{8,12},{9,13},{10,... | collective-permute-start | bytes 52232 | tf_op jit(solution)/shard_map/ppermute | solution.py:49
  24.7 5.7 %collective-permute-start.4 = (f32[34,128]{1,0:T(8,128)S(1)}, f32[34,128]{1,0:T(8,128)S(1)}, u32[]{:S(2)}, u32[]{:S(2)}) collective-permute-start(f32[34,128]{1,0:T(8,128)S(1)} %add.51), channel_id=1, source_target_pairs={{0,16},{1,17},{2,18},{3,19},{4,20},{5,21},{6,22},{7,23},{8,24},{9,... | collective-permute-start | bytes 52232 | tf_op jit(solution)/shard_map/ppermute | solution.py:49
  34.5 1.3 collective-permute-start.5
  35.9 6.1 %collective-permute-start.6 = (f32[3,128]{0,1:T(8,128)S(1)}, f32[3,128]{0,1:T(8,128)S(1)}, u32[]{:S(2)}, u32[]{:S(2)}) collective-permute-start(f32[3,128]{0,1:T(8,128)S(1)} %broadcast_add_fusion), channel_id=1, source_target_pairs={{0,2},{1,3},{2,0},{3,1},{4,6},{5,7},{6,4},{7,5},{8,10},{9,11},{10,... | collective-permute-start | bytes 4616 | tf_op jit(solution)/shard_map/ppermute | solution.py:49
  42.0 4.3 %collective-permute-start.7 = (f32[3,128]{0,1:T(8,128)S(1)}, f32[3,128]{0,1:T(8,128)S(1)}, u32[]{:S(2)}, u32[]{:S(2)}) collective-permute-start(f32[3,128]{0,1:T(8,128)S(1)} %fusion.31), channel_id=1, source_target_pairs={{0,8},{1,9},{2,10},{3,11},{4,12},{5,13},{6,14},{7,15},{8,0},{9,1},... | collective-permute-start | bytes 4616 | tf_op jit(solution)/shard_map/ppermute | solution.py:49
  46.3 6.0 %collective-permute-start.8 = (f32[3,128]{0,1:T(8,128)S(1)}, f32[3,128]{0,1:T(8,128)S(1)}, u32[]{:S(2)}, u32[]{:S(2)}) collective-permute-start(f32[3,128]{0,1:T(8,128)S(1)} %add.58), channel_id=1, source_target_pairs={{0,4},{1,5},{2,6},{3,7},{4,0},{5,1},{6,2},{7,3},{8,12},{9,13},{10,... | collective-permute-start | bytes 4616 | tf_op jit(solution)/shard_map/ppermute | solution.py:49
  52.3 6.1 %collective-permute-start.9 = (f32[3,128]{0,1:T(8,128)S(1)}, f32[3,128]{0,1:T(8,128)S(1)}, u32[]{:S(2)}, u32[]{:S(2)}) collective-permute-start(f32[3,128]{0,1:T(8,128)S(1)} %add.59), channel_id=1, source_target_pairs={{0,16},{1,17},{2,18},{3,19},{4,20},{5,21},{6,22},{7,23},{8,24},{9,... | collective-permute-start | bytes 4616 | tf_op jit(solution)/shard_map/ppermute | solution.py:49
  58.5 9.2 %collective-permute-start.10 = (f32[3,128]{0,1:T(8,128)S(1)}, f32[3,128]{0,1:T(8,128)S(1)}, u32[]{:S(2)}, u32[]{:S(2)}) collective-permute-start(f32[3,128]{0,1:T(8,128)S(1)} %broadcast_in_dim.30), channel_id=1, source_target_pairs={{64,96},{65,97},{66,98},{67,99},{68,100},{69,101},{70,102},{71,103... | collective-permute-start | bytes 4616 | tf_op jit(solution)/shard_map/ppermute | solution.py:374
  59.9 7.8 %collective-permute-start.12 = (bf16[32,128]{1,0:T(8,128)(2,1)S(1)}, bf16[32,128]{1,0:T(8,128)(2,1)S(1)}, u32[]{:S(2)}, u32[]{:S(2)}) collective-permute-start(bf16[32,128]{1,0:T(8,128)(2,1)S(1)} %bitcast.107), channel_id=1, source_target_pairs={{96,32},{97,33},{98,34},{99,35},{100,36},{101,37},{102,38},{103,39... | collective-permute-start | bytes 24584 | tf_op jit(solution)/shard_map/ppermute | solution.py:374
  62.1 5.6 %collective-permute-start.11 = (bf16[32,128]{1,0:T(8,128)(2,1)S(1)}, bf16[32,128]{1,0:T(8,128)(2,1)S(1)}, u32[]{:S(2)}, u32[]{:S(2)}) collective-permute-start(bf16[32,128]{1,0:T(8,128)(2,1)S(1)} %bitcast.108), channel_id=1, source_target_pairs={{64,32},{65,33},{66,34},{67,35},{68,36},{69,37},{70,38},{71,39},{7... | collective-permute-start | bytes 24584 | tf_op jit(solution)/shard_map/ppermute | solution.py:374
  134.5 5.3 %copy-start.1 = (bf16[256,4096]{1,0:T(8,128)(2,1)S(1)}, bf16[256,4096]{1,0:T(8,128)(2,1)}, u32[]{:S(2)}) copy-start(bf16[256,4096]{1,0:T(8,128)(2,1)} %copy-done) | copy-start | bytes 6291460
  134.5 5.3 %copy-start.2 = (s32[2,1]{0,1:T(1,128)S(1)}, s32[2,1]{0,1:T(1,128)}, u32[]{:S(2)}) copy-start(s32[2,1]{0,1:T(1,128)} %param.15) | copy-start | bytes 28
  134.5 43.3 %collective-permute-start.13 = (bf16[2048,256]{1,0:T(8,128)(2,1)S(1)}, bf16[2048,256]{1,0:T(8,128)(2,1)S(1)}, u32[]{:S(2)}, u32[]{:S(2)}) collective-permute-start(bf16[2048,256]{1,0:T(8,128)(2,1)S(1)} %shard_map.96.late_ref), channel_id=1, source_target_pairs={{96,64},{64,32},{97,65},{65,33},{98,66},{66,34},{99,67},{67,35},{1... | collective-permute-start | bytes 3145736 | tf_op jit(solution)/shard_map/ppermute | solution.py:374
  150.2 27.6 %collective-permute-start.15 = (bf16[256,1024]{1,0:T(8,128)(2,1)S(1)}, bf16[256,1024]{1,0:T(8,128)(2,1)S(1)}, u32[]{:S(2)}, u32[]{:S(2)}) collective-permute-start(bf16[256,1024]{1,0:T(8,128)(2,1)S(1)} %shard_map.99.refs_0_.refs_9_), channel_id=1, source_target_pairs={{0,32},{64,96},{1,33},{65,97},{2,34},{66,98},{3,35},{67,99},{4,36}... | collective-permute-start | bytes 1572872 | tf_op jit(solution)/shard_map/ppermute | solution.py:374
  151.5 20.0 %collective-permute-start.14 = (bf16[256,512]{1,0:T(8,128)(2,1)S(1)}, bf16[256,512]{1,0:T(8,128)(2,1)S(1)}, u32[]{:S(2)}, u32[]{:S(2)}) collective-permute-start(bf16[256,512]{1,0:T(8,128)(2,1)S(1)} %shard_map.98.refs_0_.refs_8_), channel_id=1, source_target_pairs={{0,32},{64,96},{1,33},{65,97},{2,34},{66,98},{3,35},{67,99},{4,36}... | collective-permute-start | bytes 786440 | tf_op jit(solution)/shard_map/ppermute | solution.py:374
  177.9 26.8 %collective-permute-start.17 = (bf16[2048,256]{1,0:T(8,128)(2,1)S(1)}, bf16[2048,256]{1,0:T(8,128)(2,1)S(1)}, u32[]{:S(2)}, u32[]{:S(2)}) collective-permute-start(bf16[2048,256]{1,0:T(8,128)(2,1)S(1)} %shard_map.101.refs_6_), channel_id=1, source_target_pairs={{64,32},{65,33},{66,34},{67,35},{68,36},{69,37},{70,38},{71,39},{7... | collective-permute-start | bytes 3145736 | tf_op jit(solution)/shard_map/ppermute | solution.py:374
  178.7 16.8 %collective-permute-start.18 = (bf16[256,1024]{1,0:T(8,128)(2,1)S(1)}, bf16[256,1024]{1,0:T(8,128)(2,1)S(1)}, u32[]{:S(2)}, u32[]{:S(2)}) collective-permute-start(bf16[256,1024]{1,0:T(8,128)(2,1)S(1)} %shard_map.100.refs_0_.refs_10_), channel_id=1, source_target_pairs={{0,32},{64,96},{1,33},{65,97},{2,34},{66,98},{3,35},{67,99},{4,36}... | collective-permute-start | bytes 1572872 | tf_op jit(solution)/shard_map/ppermute | solution.py:374
  186.4 18.4 %collective-permute-start.19 = (bf16[256,1024]{1,0:T(8,128)(2,1)S(1)}, bf16[256,1024]{1,0:T(8,128)(2,1)S(1)}, u32[]{:S(2)}, u32[]{:S(2)}) collective-permute-start(bf16[256,1024]{1,0:T(8,128)(2,1)S(1)} %shard_map.102.refs_0_.refs_11_), channel_id=1, source_target_pairs={{0,32},{64,96},{1,33},{65,97},{2,34},{66,98},{3,35},{67,99},{4,36}... | collective-permute-start | bytes 1572872 | tf_op jit(solution)/shard_map/ppermute | solution.py:374
  199.6 16.0 %collective-permute-start.16 = (bf16[2048,256]{1,0:T(8,128)(2,1)S(1)}, bf16[2048,256]{1,0:T(8,128)(2,1)S(1)}, u32[]{:S(2)}, u32[]{:S(2)}) collective-permute-start(bf16[2048,256]{1,0:T(8,128)(2,1)S(1)} %shard_map.101.refs_6_), channel_id=1, source_target_pairs={{0,1},{1,0},{2,3},{3,2},{4,5},{5,4},{6,7},{7,6},{8,9},{9,8},{10,11... | collective-permute-start | bytes 3145736 | tf_op jit(solution)/shard_map/ppermute | solution.py:49
  204.8 10.7 %collective-permute-start.20 = (bf16[2048,256]{1,0:T(8,128)(2,1)S(1)}, bf16[2048,256]{1,0:T(8,128)(2,1)S(1)}, u32[]{:S(2)}, u32[]{:S(2)}) collective-permute-start(bf16[2048,256]{1,0:T(8,128)(2,1)S(1)} %shard_map.104.refs_8_), channel_id=1, source_target_pairs={{0,1},{1,0},{2,3},{3,2},{4,5},{5,4},{6,7},{7,6},{8,9},{9,8},{10,11... | collective-permute-start | bytes 3145736 | tf_op jit(solution)/shard_map/ppermute | solution.py:49
  205.0 10.6 %collective-permute-start.21 = (bf16[256,512]{1,0:T(8,128)(2,1)S(1)}, bf16[256,512]{1,0:T(8,128)(2,1)S(1)}, u32[]{:S(2)}, u32[]{:S(2)}) collective-permute-start(bf16[256,512]{1,0:T(8,128)(2,1)S(1)} %shard_map.103.refs_0_.refs_12_), channel_id=1, source_target_pairs={{0,32},{64,96},{1,33},{65,97},{2,34},{66,98},{3,35},{67,99},{4,36}... | collective-permute-start | bytes 786440 | tf_op jit(solution)/shard_map/ppermute | solution.py:374
  218.6 28.1 %collective-permute-start.23 = (bf16[256,512]{1,0:T(8,128)(2,1)S(1)}, bf16[256,512]{1,0:T(8,128)(2,1)S(1)}, u32[]{:S(2)}, u32[]{:S(2)}) collective-permute-start(bf16[256,512]{1,0:T(8,128)(2,1)S(1)} %get-tuple-element.12), channel_id=1, source_target_pairs={{32,96},{33,97},{34,98},{35,99},{36,100},{37,101},{38,102},{39,103... | collective-permute-start | bytes 786440 | tf_op jit(solution)/shard_map/ppermute | solution.py:374
  219.9 26.8 %collective-permute-start.22 = (bf16[256,512]{1,0:T(8,128)(2,1)S(1)}, bf16[256,512]{1,0:T(8,128)(2,1)S(1)}, u32[]{:S(2)}, u32[]{:S(2)}) collective-permute-start(bf16[256,512]{1,0:T(8,128)(2,1)S(1)} %get-tuple-element.12), channel_id=1, source_target_pairs={{32,64},{33,65},{34,66},{35,67},{36,68},{37,69},{38,70},{39,71},{4... | collective-permute-start | bytes 786440 | tf_op jit(solution)/shard_map/ppermute | solution.py:374
  (2 other events, 2.3 us)
Sparse Core Ops, SparseCore 0:
  10.3 122.9 all-gather.1

commit v4 on v2

--- a/solution.py
+++ b/solution.py
@@ -35,6 +35,7 @@
     return pairs
 
 
+ROUTE = (0, -1, 1, 2)
 CORE_SWAP = moves(lambda x, z, c: (x, z, 1 - c))
 DOUBLING = (
     CORE_SWAP,
@@ -49,6 +50,37 @@
     return lax.ppermute(value, "fsdp", pairs)
 
 
+def along_first(step):
+    return moves(lambda x, z, c: (x, z + step, c) if c == 0 else (x + step, z, c))
+
+
+def along_second(step):
+    return moves(lambda x, z, c: (x + step, z, c) if c == 0 else (x, z + step, c))
+
+
+def send_one(value, pairs):
+    return lax.ppermute(value, ("section", "fsdp"), [(32 + a, 32 + b) for a, b in pairs])
+
+
+def ring(block, move):
+    before, after = send_one(block, move(1)), send_one(block, move(-1))
+    return [block, before, after, send_one(before, move(1))]
+
+
+def row_order():
+    index = lax.axis_index("fsdp")
+    x, z, core = index // 8, (index // 2) % 4, index % 2
+    first = jnp.array(ROUTE, jnp.int32)
+    line, plane = jnp.tile(first, 4), jnp.repeat(first, 4)
+
+    def order(kind):
+        zs = z + jnp.where(kind == 0, line, plane)
+        xs = x + jnp.where(kind == 0, plane, line)
+        return ((xs + 8) % 4) * 8 + ((zs + 8) % 4) * 2 + kind
+
+    return jnp.concatenate([order(core), order(1 - core)]).astype(jnp.int32)
+
+
 def total(value):
     for pairs in DOUBLING:
         value = value + send(value, pairs)
@@ -62,6 +94,36 @@
 def cost(flops, size, exps=0):
     share = 64
     return pl.CostEstimate(flops=int(flops) // share, bytes_accessed=int(size) // share, transcendentals=int(exps) // share)
+
+
+def stack_kernel(count, *refs):
+    sources, out, held, sems = refs[:count], refs[count], refs[count + 1], refs[count + 2]
+    rows = sources[0].shape[0]
+    reads = [pltpu.make_async_copy(source, held.at[i], sems.at[0, i]) for i, source in enumerate(sources)]
+    writes = [
+        pltpu.make_async_copy(held.at[i], out.at[pl.ds(i * rows, rows)], sems.at[1, i]) for i in range(count)
+    ]
+    for read in reads:
+        read.start()
+    for read, write in zip(reads, writes):
+        read.wait()
+        write.start()
+    for write in writes:
+        write.wait()
+
+
+def stack(blocks):
+    count = len(blocks)
+    rows, width = blocks[0].shape
+    return pl.pallas_call(
+        functools.partial(stack_kernel, count),
+        out_shape=jax.ShapeDtypeStruct((count * rows, width), blocks[0].dtype),
+        in_specs=[ANY] * count,
+        out_specs=ANY,
+        scratch_shapes=[pltpu.VMEM((count, rows, width), blocks[0].dtype), pltpu.SemaphoreType.DMA((2, count))],
+        compiler_params=pltpu.CompilerParams(vmem_limit_bytes=12 * 1024 * 1024),
+        cost_estimate=cost(0, 4 * count * rows * width),
+    )(*blocks)
 
 
 def norm_into(xn_ref, x_ref, gain_ref, row):
@@ -105,20 +167,25 @@
     norm_into(xn_ref, x_ref, gain_ref, 0)
 
 
-def project_kernel(xn_ref, kv_ref, keys_ref, values_ref):
+def project_kernel(xn_ref, kv_ref, *refs):
+    keys_ref, values_ref = refs[-2:]
     project_into(keys_ref, values_ref, xn_ref[...], kv_ref[...])
 
 
 def part_kernel(lengths_ref, section_ref, scale_ref, xn_ref, w_ref, k_ref, v_ref, x_ref, out_ref):
-    q = (dot(xn_ref[...], w_ref[...]) * scale_ref[0]).astype(BF16)
-
-    @pl.when(section_ref[0] != 2)
-    def _():
-        out_ref[...] = attend(q, k_ref, v_ref, x_ref[...], lengths_ref, scale_ref[1], scale_ref[2])
+    query = lambda: (dot(xn_ref[...], w_ref[...]) * scale_ref[0]).astype(BF16)
+
+    @pl.when(section_ref[0] == 0)
+    def _():
+        out_ref[...] = attend(query(), k_ref, v_ref, x_ref[...], lengths_ref, scale_ref[1], scale_ref[2])
 
     @pl.when(section_ref[0] == 2)
     def _():
-        out_ref[...] = q
+        out_ref[...] = query()
+
+    @pl.when(lax.rem(section_ref[0], 2) == 1)
+    def _():
+        out_ref[...] = jnp.zeros_like(out_ref)
 
 
 def layer_part(xn, full, keys, values, x, at, lengths, section, scales):
@@ -195,10 +262,10 @@
 
 
 def encoder_kernel(count, *refs):
-    section_ref, lengths_ref, scale_ref, gain_ref, full = refs[:5]
-    pieces = refs[5 : 5 + count]
-    out_ref, cross_ref = refs[5 + count : 7 + count]
-    buf, sems, xn_ref, q_ref, x_ref, x_sems, kv_buf, kv_sems, k_ref, v_ref = refs[7 + count :]
+    section_ref, order_ref, lengths_ref, scale_ref, gain_ref, full = refs[:6]
+    kv_refs, pieces = refs[6:8], refs[8 : 8 + count]
+    out_ref, cross_ref = refs[8 + count : 10 + count]
+    buf, sems, xn_ref, q_ref, x_ref, x_sems, kv_buf, kv_sems, k_ref, v_ref = refs[10 + count :]
     width = x_ref.shape[1]
 
     @pl.when(section_ref[0] == 1)
@@ -206,29 +273,32 @@
         arrive = bring(pieces, x_ref, x_sems)
         for copy in arrive:
             copy.start()
-        kv_copies = [
-            pltpu.make_async_copy(
-                full.at[:, pl.ds(width + i * 2 * HEAD, 2 * HEAD)], kv_buf.at[i], kv_sems.at[i]
-            )
-            for i in range(3)
-        ]
-        for copy in kv_copies[:1]:
-            copy.start()
+        of_layer = lambda i: pltpu.make_async_copy(
+            full.at[:, pl.ds(width, 2 * HEAD)], kv_buf.at[i], kv_sems.at[i]
+        )
+
+        def begin_later():
+            for k in range(32):
+                ref, row = kv_refs[k // 16], k % 16 * 128
+                rows = pl.ds(pl.multiple_of(order_ref[k] * 128, 128), 128)
+                for i in (1, 2):
+                    block = ref.at[pl.ds(row, 128), pl.ds((i - 1) * 2 * HEAD, 2 * HEAD)]
+                    pltpu.make_async_copy(block, kv_buf.at[i, rows], kv_sems.at[i]).start()
+
+        of_layer(0).start()
         start, run = stream_layer(
             full, buf, sems, xn_ref, q_ref, k_ref, v_ref, x_ref, lengths_ref, scale_ref, out_ref
         )
         start()
-        for copy in kv_copies[1:]:
-            copy.start()
+        begin_later()
         for copy in arrive:
             copy.wait()
         norm_into(xn_ref, x_ref, gain_ref, 0)
-        for copy in kv_copies[:1]:
-            copy.wait()
+        of_layer(0).wait()
         project_into(k_ref, v_ref, xn_ref[...], kv_buf[0])
         run()
-        for copy in kv_copies[1:]:
-            copy.wait()
+        for i in (1, 2):
+            of_layer(i).wait()
         for i in (1, 2):
             norm_into(xn_ref, out_ref, gain_ref, i)
             at = (i - 1) * 2 * HEAD
@@ -336,8 +406,10 @@
     extra3 = hop(extra, [(3, 1)])
     local = kv_part.shape[0]
 
-    full = jnp.concatenate([weight, kv_part, extra2[:local], extra3[:local]], 1)
-    full = lax.all_gather(full, "fsdp", axis=0, tiled=True)
+    line = stack(ring(jnp.concatenate([extra2[:local], extra3[:local]], 1), along_first))
+    kv_own = stack(ring(line, along_second))
+    kv_other = send_one(kv_own, CORE_SWAP)
+    full = lax.all_gather(jnp.concatenate([weight, kv_part], 1), "fsdp", axis=0, tiled=True)
 
     along = spectral_along(weight, kv_part, start_rows).reshape(-1)
     images = spectral_images(weight, kv_part, along)
@@ -361,11 +433,11 @@
         project_kernel,
         grid=(1,),
         out_shape=(head_shape, head_shape),
-        in_specs=[whole((rows, width)), kv_block],
+        in_specs=[whole((rows, width)), kv_block, ANY, ANY],
         out_specs=(whole((rows, HEAD)), whole((rows, HEAD))),
         compiler_params=params(),
         cost_estimate=cost(4 * rows * width * HEAD, 4 * width * HEAD),
-    )(xn0, full)
+    )(xn0, full, kv_own, kv_other)
 
     made, passed = [], []
     for at in range(0, width, PIECE):
@@ -387,7 +459,7 @@
     out1, cross = pl.pallas_call(
         functools.partial(encoder_kernel, n),
         out_shape=(row_shape, jax.ShapeDtypeStruct((rows, 4 * HEAD), BF16)),
-        in_specs=[SMEM] * 3 + [VMEM] + [ANY] * (1 + n),
+        in_specs=[SMEM] * 4 + [VMEM] + [ANY] * (3 + n),
         out_specs=(VMEM, VMEM),
         scratch_shapes=scratch
         + [
@@ -398,7 +470,7 @@
         ],
         compiler_params=params(),
         cost_estimate=layer_cost,
-    )(section, seq_lengths, scales, all_gains, full, *passed)
+    )(section, row_order(), seq_lengths, scales, all_gains, full, kv_own, kv_other, *passed)
     cross = hop(cross, [(1, 2)]) + hop(cross, [(1, 3)])
 
     result = pl.pallas_call(

time: 272 us -> 259 us (0.952)
  waiting for transfers between devices: 156 us -> 145 us
  Pallas kernels: 55.2 us -> 48.5 us
  starting transfers between devices: 33.4 us -> 39.9 us
    all_gather x1, waiting for transfers between devices: 77.7 us -> 57.4 us  [shards(): lax.all_gather(jnp.concatenate([weight, kv_part], 1), 'fsdp', axis=0, til...]
    ppermute x9, waiting for transfers between devices: 57 us -> 71.2 us  [shards(): hop = lambda value, pairs: lax.ppermute(value, 'section', pairs)]
    pallas_call x4, Pallas kernels: 25 us -> 14.6 us  [layer_part(): pl.pallas_call(part_kernel, grid=(PIECE // BLOCK,), out_shape=jax.ShapeDt...]
    ppermute x0 -> x7, starting transfers between devices: none -> 6.1 us  [send_one(): lax.ppermute(value, ('section', 'fsdp'), [(32 + a, 32 + b) for a, b in pa...]
    ppermute x10, waiting for transfers between devices: 21.5 us -> 16.1 us  [send(): return lax.ppermute(value, 'fsdp', pairs)]
    pallas_call x0 -> x2, Pallas kernels: none -> 2.95 us  [stack(): pl.pallas_call(functools.partial(stack_kernel, count), out_shape=jax.Shap...]
  transfers between devices with their start and end apart: 20 -> 27, of which waited for: 16 -> 15; matrix products, arithmetic and copies ran while one was open for 1% -> 2% of each run, Pallas kernels for 8% -> 7%
where the time goes in v4:
time: 259 us
  waiting for transfers between devices  145 us (56%)
  Pallas kernels  48.5 us (19%)
  starting transfers between devices  39.9 us (15%)
  between operations  16.7 us (6%)
  other arithmetic  4.38 us (2%)
  local copies, waits for them, and re-layouts  3.65 us (1%)
    ppermute x9, waiting for transfers between devices, shards(): hop = lambda value, pairs: lax.ppermute(value, 'section', pairs)  71.2 us
    all_gather x1, waiting for transfers between devices, shards(): lax.all_gather(jnp.concatenate([weight, kv_part], 1), 'fsdp', axis=0, til...  57.4 us
    pallas_call x1, Pallas kernels, shards(): pl.pallas_call(functools.partial(decoder_kernel, n), out_shape=row_shape,...  23.8 us
    ppermute x10, starting transfers between devices, send(): return lax.ppermute(value, 'fsdp', pairs)  21.4 us
    ppermute x10, waiting for transfers between devices, send(): return lax.ppermute(value, 'fsdp', pairs)  16.1 us
    pallas_call x4, Pallas kernels, layer_part(): pl.pallas_call(part_kernel, grid=(PIECE // BLOCK,), out_shape=jax.ShapeDt...  14.6 us
    ppermute x9, starting transfers between devices, shards(): hop = lambda value, pairs: lax.ppermute(value, 'section', pairs)  12.4 us
    ppermute x7, starting transfers between devices, send_one(): lax.ppermute(value, ('section', 'fsdp'), [(32 + a, 32 + b) for a, b in pa...  6.1 us
  transfers between devices with their start and end apart: 27, of which 15 were waited for; matrix products, arithmetic and copies ran while one was open for 2% of the time, Pallas kernels for 7%

profile of v4, /device:TPU:24, one launch (start us, length us, event | category | flops | bytes accessed | tf_op | source)
XLA Modules:
  0.0 258.8 jit_solution(8198573892726449546)
XLA Ops:
  7.2 2.4 pad_maximum_fusion
  9.8 3.1 %collective-permute-start.12 = (bf16[144,256]{1,0:T(8,128)(2,1)S(1)}, bf16[144,256]{1,0:T(8,128)(2,1)S(1)}, u32[]{:S(2)}, u32[]{:S(2)}) collective-permute-start(bf16[144,256]{1,0:T(8,128)(2,1)S(1)} %pad_maximum_fusion.2), channel_id=1, source_target_pairs={{96,32},{97,33},{98,34},{99,35},{100,36},{101,37},{102,38},{103,39... | collective-permute-start | bytes 221192 | tf_op jit(solution)/shard_map/ppermute | solution.py:402
  17.1 2.0 collective-permute-start.1
  21.3 1.6 collective-permute-start.2
  22.9 2.3 collective-permute-done.2
  25.2 3.6 %collective-permute-start.3 = (f32[34,128]{1,0:T(8,128)S(1)}, f32[34,128]{1,0:T(8,128)S(1)}, u32[]{:S(2)}, u32[]{:S(2)}) collective-permute-start(f32[34,128]{1,0:T(8,128)S(1)} %add.143), channel_id=1, source_target_pairs={{0,4},{1,5},{2,6},{3,7},{4,0},{5,1},{6,2},{7,3},{8,12},{9,13},{10,... | collective-permute-start | bytes 52232 | tf_op jit(solution)/shard_map/ppermute | solution.py:50
  28.8 2.2 collective-permute-done.3
  30.9 3.4 %collective-permute-start.4 = (f32[34,128]{1,0:T(8,128)S(1)}, f32[34,128]{1,0:T(8,128)S(1)}, u32[]{:S(2)}, u32[]{:S(2)}) collective-permute-start(f32[34,128]{1,0:T(8,128)S(1)} %add.144), channel_id=1, source_target_pairs={{0,16},{1,17},{2,18},{3,19},{4,20},{5,21},{6,22},{7,23},{8,24},{9,... | collective-permute-start | bytes 52232 | tf_op jit(solution)/shard_map/ppermute | solution.py:50
  34.4 2.3 collective-permute-done.4
  41.9 1.5 shard_map.105.refs_0_.refs_6_
  43.5 2.0 collective-permute-start.19
  47.1 1.6 collective-permute-start.6
  48.7 2.7 %collective-permute-done.6 = f32[3,128]{0,1:T(8,128)S(1)} collective-permute-done((f32[3,128]{0,1:T(8,128)S(1)}, f32[3,128]{0,1:T(8,128)S(1)}, u32[]{:S(2)}, u32[]{:S(2)}) %collective-permute-start.6) | collective-permute-done | bytes 1568 | tf_op jit(solution)/shard_map/ppermute | solution.py:50
  51.4 1.8 collective-permute-start.7
  53.6 2.2 collective-permute-done.7
  55.8 3.7 %collective-permute-start.8 = (f32[3,128]{0,1:T(8,128)S(1)}, f32[3,128]{0,1:T(8,128)S(1)}, u32[]{:S(2)}, u32[]{:S(2)}) collective-permute-start(f32[3,128]{0,1:T(8,128)S(1)} %add.151), channel_id=1, source_target_pairs={{0,4},{1,5},{2,6},{3,7},{4,0},{5,1},{6,2},{7,3},{8,12},{9,13},{10,... | collective-permute-start | bytes 4616 | tf_op jit(solution)/shard_map/ppermute | solution.py:50
  59.5 3.3 %collective-permute-done.8 = f32[3,128]{0,1:T(8,128)S(1)} collective-permute-done((f32[3,128]{0,1:T(8,128)S(1)}, f32[3,128]{0,1:T(8,128)S(1)}, u32[]{:S(2)}, u32[]{:S(2)}) %collective-permute-start.8) | collective-permute-done | bytes 1568 | tf_op jit(solution)/shard_map/ppermute | solution.py:50
  62.8 3.5 %collective-permute-start.9 = (f32[3,128]{0,1:T(8,128)S(1)}, f32[3,128]{0,1:T(8,128)S(1)}, u32[]{:S(2)}, u32[]{:S(2)}) collective-permute-start(f32[3,128]{0,1:T(8,128)S(1)} %add.152), channel_id=1, source_target_pairs={{0,16},{1,17},{2,18},{3,19},{4,20},{5,21},{6,22},{7,23},{8,24},{9,... | collective-permute-start | bytes 4616 | tf_op jit(solution)/shard_map/ppermute | solution.py:50
  66.4 4.0 %shard_map.106 = (bf16[256,4096]{1,0:T(8,128)(2,1)S(1)}, bf16[256,4096]{1,0:T(8,128)(2,1)S(1)}) custom-call(s32[1]{0:T(128)} %bitcast.section_ref.refs_0_, bf16[256,4096]{1,0:T(8,128)(2,1)} %bitcast.91, bf16[256,4096]{1,0:T(8,128)(2,1)} %bitcast.88, f32[1,4096]{1,0:T(1,128)S(1)} %get-tuple-element.23.gain_ref.refs_3_), custom_call_target="tpu_custom_call" | custom-call | flops 131072 | bytes 131072 | tf_op jit(solution)/shard_map/pallas_call | solution.py:421
  73.1 4.8 %collective-permute-done.10 = f32[3,128]{0,1:T(8,128)S(1)} collective-permute-done((f32[3,128]{0,1:T(8,128)S(1)}, f32[3,128]{0,1:T(8,128)S(1)}, u32[]{:S(2)}, u32[]{:S(2)}) %collective-permute-start.10) | collective-permute-done | bytes 1568 | tf_op jit(solution)/shard_map/ppermute | solution.py:402
  78.0 57.4 %all-gather.2.cloned.1.call-done.kv_ref.w_ref.refs_5_.refs_4_ = bf16[4096,4352]{1,0:T(8,128)(2,1)} async-done(((bf16[128,4352]{1,0:T(8,128)(2,1)}), bf16[4096,4352]{1,0:T(8,128)(2,1)}) %all-gather.2.cloned.1.call-update) | async-done | bytes 35651600 | tf_op jit(solution)/shard_map/all_gather | solution.py:412
  135.3 2.4 shard_map.107
  137.8 3.6 %shard_map.108.refs_8_ = bf16[256,1024]{1,0:T(8,128)(2,1)S(1)} custom-call(s32[2]{0:T(128)S(1)} %bitcast.81, s32[1]{0:T(128)} %bitcast.section_ref.refs_0_, f32[3]{0:T(128)S(1)} %get-tuple-element.21.scale_ref.refs_3_, bf16[256,4096]{1,0:T(8,128)(2,1)S(1)} %get-tuple-element.8.xn_ref, ...), custom_call_target="tpu_custom_call" | custom-call | flops 33554432 | bytes 131072 | tf_op jit(solution)/shard_map/pallas_call | solution.py:195
  142.7 3.7 %shard_map.109.refs_9_ = bf16[256,1024]{1,0:T(8,128)(2,1)S(1)} custom-call(s32[2]{0:T(128)S(1)} %bitcast.82, s32[1]{0:T(128)} %bitcast.section_ref.refs_0_, f32[3]{0:T(128)S(1)} %get-tuple-element.21.scale_ref.refs_3_, bf16[256,4096]{1,0:T(8,128)(2,1)S(1)} %get-tuple-element.8.xn_ref, ...), custom_call_target="tpu_custom_call" | custom-call | flops 33554432 | bytes 131072 | tf_op jit(solution)/shard_map/pallas_call | solution.py:195
  146.4 1.5 collective-permute-start.21
  147.9 3.7 %shard_map.110.refs_10_ = bf16[256,1024]{1,0:T(8,128)(2,1)S(1)} custom-call(s32[2]{0:T(128)S(1)} %bitcast.83, s32[1]{0:T(128)} %bitcast.section_ref.refs_0_, f32[3]{0:T(128)S(1)} %get-tuple-element.21.scale_ref.refs_3_, bf16[256,4096]{1,0:T(8,128)(2,1)S(1)} %get-tuple-element.8.xn_ref, ...), custom_call_target="tpu_custom_call" | custom-call | flops 33554432 | bytes 131072 | tf_op jit(solution)/shard_map/pallas_call | solution.py:195
  152.9 3.6 %shard_map.111.refs_11_ = bf16[256,1024]{1,0:T(8,128)(2,1)S(1)} custom-call(s32[2]{0:T(128)S(1)} %bitcast.84, s32[1]{0:T(128)} %bitcast.section_ref.refs_0_, f32[3]{0:T(128)S(1)} %get-tuple-element.21.scale_ref.refs_3_, bf16[256,4096]{1,0:T(8,128)(2,1)S(1)} %get-tuple-element.8.xn_ref, ...), custom_call_target="tpu_custom_call" | custom-call | flops 33554432 | bytes 131072 | tf_op jit(solution)/shard_map/pallas_call | solution.py:195
  158.1 11.2 %collective-permute-done.21.refs_9_.refs_13_ = bf16[256,1024]{1,0:T(8,128)(2,1)S(1)} collective-permute-done((bf16[256,1024]{1,0:T(8,128)(2,1)S(1)}, bf16[256,1024]{1,0:T(8,128)(2,1)S(1)}, u32[]{:S(2)}, u32[]{:S(2)}) %collective-permute-start.21) | collective-permute-done | bytes 524320 | tf_op jit(solution)/shard_map/ppermute | solution.py:402
  169.3 11.2 %collective-permute-done.22.refs_10_.refs_14_ = bf16[256,1024]{1,0:T(8,128)(2,1)S(1)} collective-permute-done((bf16[256,1024]{1,0:T(8,128)(2,1)S(1)}, bf16[256,1024]{1,0:T(8,128)(2,1)S(1)}, u32[]{:S(2)}, u32[]{:S(2)}) %collective-permute-start.22) | collective-permute-done | bytes 524320 | tf_op jit(solution)/shard_map/ppermute | solution.py:402
  180.5 10.9 %collective-permute-done.23.refs_11_.refs_15_ = bf16[256,1024]{1,0:T(8,128)(2,1)S(1)} collective-permute-done((bf16[256,1024]{1,0:T(8,128)(2,1)S(1)}, bf16[256,1024]{1,0:T(8,128)(2,1)S(1)}, u32[]{:S(2)}, u32[]{:S(2)}) %collective-permute-start.23) | collective-permute-done | bytes 524320 | tf_op jit(solution)/shard_map/ppermute | solution.py:402
  196.1 32.0 %collective-permute-done.25 = bf16[256,512]{1,0:T(8,128)(2,1)S(1)} collective-permute-done((bf16[256,512]{1,0:T(8,128)(2,1)S(1)}, bf16[256,512]{1,0:T(8,128)(2,1)S(1)}, u32[]{:S(2)}, u32[]{:S(2)}) %collective-permute-start.25) | collective-permute-done | bytes 262176 | tf_op jit(solution)/shard_map/ppermute | solution.py:402
  228.1 23.8 %shard_map.113 = bf16[256,4096]{1,0:T(8,128)(2,1)} custom-call(s32[1]{0:T(128)} %bitcast.section_ref.refs_0_, s32[2]{0:T(128)S(1)} %bitcast.86, f32[6]{0:T(128)S(1)} %pad_maximum_fusion.3.refs_2_, f32[1,4096]{1,0:T(1,128)S(1)} %get-tuple-element.23.gain_ref.refs_3_, bf16[4096,4352]{1,0:T(8,128)(2,1)} %all-gather.2.cloned.1.call-done.kv_ref.w_ref.refs_5_.refs_4_, ...), custom_call_target="tpu_custom_call" | custom-call | flops 134217728 | bytes 524288 | tf_op jit(solution)/shard_map/pallas_call | solution.py:476
  (102 shorter events, 23.1 us)
Async XLA Ops:
  7.2 2.6 %copy-start.5 = (bf16[1,128,256]{2,1,0:T(8,128)(2,1)S(1)}, bf16[1,128,256]{2,1,0:T(8,128)(2,1)}, u32[]{:S(2)}) copy-start(bf16[1,128,256]{2,1,0:T(8,128)(2,1)} %param.10) | copy-start | bytes 196612
  7.2 6.5 %copy-start.4 = (bf16[1,128,4096]{2,1,0:T(8,128)(2,1)S(1)}, bf16[1,128,4096]{2,1,0:T(8,128)(2,1)}, u32[]{:S(2)}) copy-start(bf16[1,128,4096]{2,1,0:T(8,128)(2,1)} %param.9) | copy-start | bytes 3145732
  7.2 6.4 %copy-start.7 = (bf16[1,3,128]{2,1,0:T(4,128)(2,1)S(1)}, bf16[1,3,128]{2,1,0:T(4,128)(2,1)}, u32[]{:S(2)}) copy-start(bf16[1,3,128]{2,1,0:T(4,128)(2,1)} %param.13) | copy-start | bytes 2308
  7.2 128.1 %all-gather.2.cloned.1.call-start = ((), (), s32[]{:S(2)}) async-start(), calls=%async_computation | async-start | bytes 36765696 | tf_op jit(solution)/shard_map/all_gather | solution.py:412
  9.8 5.1 %collective-permute-start.12 = (bf16[144,256]{1,0:T(8,128)(2,1)S(1)}, bf16[144,256]{1,0:T(8,128)(2,1)S(1)}, u32[]{:S(2)}, u32[]{:S(2)}) collective-permute-start(bf16[144,256]{1,0:T(8,128)(2,1)S(1)} %pad_maximum_fusion.2), channel_id=1, source_target_pairs={{96,32},{97,33},{98,34},{99,35},{100,36},{101,37},{102,38},{103,39... | collective-permute-start | bytes 221192 | tf_op jit(solution)/shard_map/ppermute | solution.py:402
  13.0 2.0 collective-permute-start.11
  15.0 1.5 collective-permute-start.13
  15.7 1.5 collective-permute-start
  15.8 3.4 %collective-permute-start.14 = (bf16[128,512]{1,0:T(8,128)(2,1)S(1)}, bf16[128,512]{1,0:T(8,128)(2,1)S(1)}, u32[]{:S(2)}, u32[]{:S(2)}) collective-permute-start(bf16[128,512]{1,0:T(8,128)(2,1)S(1)} %pad_maximum_fusion.1.refs_0_), channel_id=1, source_target_pairs={{32,38},{33,57},{34,32},{35,59},{36,34},{37,61},{38,36},{39,63},{4... | collective-permute-start | bytes 393224 | tf_op jit(solution)/shard_map/ppermute | solution.py:62
  16.4 2.7 %collective-permute-start.15 = (bf16[128,512]{1,0:T(8,128)(2,1)S(1)}, bf16[128,512]{1,0:T(8,128)(2,1)S(1)}, u32[]{:S(2)}, u32[]{:S(2)}) collective-permute-start(bf16[128,512]{1,0:T(8,128)(2,1)S(1)} %collective-permute-done.13.refs_1_), channel_id=1, source_target_pairs={{32,34},{33,41},{34,36},{35,43},{36,38},{37,45},{38,32},{39,47},{4... | collective-permute-start | bytes 393224 | tf_op jit(solution)/shard_map/ppermute | solution.py:62
  17.1 4.1 %collective-permute-start.1 = (f32[34,128]{1,0:T(8,128)S(1)}, f32[34,128]{1,0:T(8,128)S(1)}, u32[]{:S(2)}, u32[]{:S(2)}) collective-permute-start(f32[34,128]{1,0:T(8,128)S(1)} %fusion.39), channel_id=1, source_target_pairs={{0,2},{1,3},{2,0},{3,1},{4,6},{5,7},{6,4},{7,5},{8,10},{9,11},{10,... | collective-permute-start | bytes 52232 | tf_op jit(solution)/shard_map/ppermute | solution.py:50
  20.6 18.1 %collective-permute-start.16 = (bf16[512,512]{1,0:T(8,128)(2,1)S(1)}, bf16[512,512]{1,0:T(8,128)(2,1)S(1)}, u32[]{:S(2)}, u32[]{:S(2)}) collective-permute-start(bf16[512,512]{1,0:T(8,128)(2,1)S(1)} %shard_map.104.refs_0_), channel_id=1, source_target_pairs={{32,40},{33,35},{34,42},{35,37},{36,44},{37,39},{38,46},{39,33},{4... | collective-permute-start | bytes 1572872 | tf_op jit(solution)/shard_map/ppermute | solution.py:62
  21.3 3.9 %collective-permute-start.2 = (f32[34,128]{1,0:T(8,128)S(1)}, f32[34,128]{1,0:T(8,128)S(1)}, u32[]{:S(2)}, u32[]{:S(2)}) collective-permute-start(f32[34,128]{1,0:T(8,128)S(1)} %fusion.44), channel_id=1, source_target_pairs={{0,8},{1,9},{2,10},{3,11},{4,12},{5,13},{6,14},{7,15},{8,0},{9,1},... | collective-permute-start | bytes 52232 | tf_op jit(solution)/shard_map/ppermute | solution.py:50
  25.2 5.8 %collective-permute-start.3 = (f32[34,128]{1,0:T(8,128)S(1)}, f32[34,128]{1,0:T(8,128)S(1)}, u32[]{:S(2)}, u32[]{:S(2)}) collective-permute-start(f32[34,128]{1,0:T(8,128)S(1)} %add.143), channel_id=1, source_target_pairs={{0,4},{1,5},{2,6},{3,7},{4,0},{5,1},{6,2},{7,3},{8,12},{9,13},{10,... | collective-permute-start | bytes 52232 | tf_op jit(solution)/shard_map/ppermute | solution.py:50
  30.9 5.7 %collective-permute-start.4 = (f32[34,128]{1,0:T(8,128)S(1)}, f32[34,128]{1,0:T(8,128)S(1)}, u32[]{:S(2)}, u32[]{:S(2)}) collective-permute-start(f32[34,128]{1,0:T(8,128)S(1)} %add.144), channel_id=1, source_target_pairs={{0,16},{1,17},{2,18},{3,19},{4,20},{5,21},{6,22},{7,23},{8,24},{9,... | collective-permute-start | bytes 52232 | tf_op jit(solution)/shard_map/ppermute | solution.py:50
  38.0 3.9 %collective-permute-start.17 = (bf16[512,512]{1,0:T(8,128)(2,1)S(1)}, bf16[512,512]{1,0:T(8,128)(2,1)S(1)}, u32[]{:S(2)}, u32[]{:S(2)}) collective-permute-start(bf16[512,512]{1,0:T(8,128)(2,1)S(1)} %shard_map.104.refs_0_), channel_id=1, source_target_pairs={{32,56},{33,39},{34,58},{35,33},{36,60},{37,35},{38,62},{39,37},{4... | collective-permute-start | bytes 1572872 | tf_op jit(solution)/shard_map/ppermute | solution.py:62
  38.7 3.2 %collective-permute-start.18 = (bf16[512,512]{1,0:T(8,128)(2,1)S(1)}, bf16[512,512]{1,0:T(8,128)(2,1)S(1)}, u32[]{:S(2)}, u32[]{:S(2)}) collective-permute-start(bf16[512,512]{1,0:T(8,128)(2,1)S(1)} %collective-permute-done.16.refs_1_), channel_id=1, source_target_pairs={{32,40},{33,35},{34,42},{35,37},{36,44},{37,39},{38,46},{39,33},{4... | collective-permute-start | bytes 1572872 | tf_op jit(solution)/shard_map/ppermute | solution.py:62
  41.9 11.3 %copy-start.8 = (s32[4]{0:T(128)S(1)}, s32[4]{0:T(128)}, u32[]{:S(2)}) copy-start(s32[4]{0:T(128)} %constant.90.clone) | copy-start | bytes 52
  43.5 34.5 %collective-permute-start.19 = (bf16[2048,512]{1,0:T(8,128)(2,1)}, bf16[2048,512]{1,0:T(8,128)(2,1)}, u32[]{:S(2)}, u32[]{:S(2)}) collective-permute-start(bf16[2048,512]{1,0:T(8,128)(2,1)} %shard_map.105.refs_0_.refs_6_), channel_id=1, source_target_pairs={{32,33},{33,32},{34,35},{35,34},{36,37},{37,36},{38,39},{39,38},{4... | collective-permute-start | bytes 6291464 | tf_op jit(solution)/shard_map/ppermute | solution.py:62
  45.7 1.3 collective-permute-start.5
  47.1 4.3 %collective-permute-start.6 = (f32[3,128]{0,1:T(8,128)S(1)}, f32[3,128]{0,1:T(8,128)S(1)}, u32[]{:S(2)}, u32[]{:S(2)}) collective-permute-start(f32[3,128]{0,1:T(8,128)S(1)} %broadcast_add_fusion), channel_id=1, source_target_pairs={{0,2},{1,3},{2,0},{3,1},{4,6},{5,7},{6,4},{7,5},{8,10},{9,11},{10,... | collective-permute-start | bytes 4616 | tf_op jit(solution)/shard_map/ppermute | solution.py:50
  51.4 4.3 %collective-permute-start.7 = (f32[3,128]{0,1:T(8,128)S(1)}, f32[3,128]{0,1:T(8,128)S(1)}, u32[]{:S(2)}, u32[]{:S(2)}) collective-permute-start(f32[3,128]{0,1:T(8,128)S(1)} %fusion.43), channel_id=1, source_target_pairs={{0,8},{1,9},{2,10},{3,11},{4,12},{5,13},{6,14},{7,15},{8,0},{9,1},... | collective-permute-start | bytes 4616 | tf_op jit(solution)/shard_map/ppermute | solution.py:50
  55.8 7.0 %collective-permute-start.8 = (f32[3,128]{0,1:T(8,128)S(1)}, f32[3,128]{0,1:T(8,128)S(1)}, u32[]{:S(2)}, u32[]{:S(2)}) collective-permute-start(f32[3,128]{0,1:T(8,128)S(1)} %add.151), channel_id=1, source_target_pairs={{0,4},{1,5},{2,6},{3,7},{4,0},{5,1},{6,2},{7,3},{8,12},{9,13},{10,... | collective-permute-start | bytes 4616 | tf_op jit(solution)/shard_map/ppermute | solution.py:50
  62.8 8.9 %collective-permute-start.9 = (f32[3,128]{0,1:T(8,128)S(1)}, f32[3,128]{0,1:T(8,128)S(1)}, u32[]{:S(2)}, u32[]{:S(2)}) collective-permute-start(f32[3,128]{0,1:T(8,128)S(1)} %add.152), channel_id=1, source_target_pairs={{0,16},{1,17},{2,18},{3,19},{4,20},{5,21},{6,22},{7,23},{8,24},{9,... | collective-permute-start | bytes 4616 | tf_op jit(solution)/shard_map/ppermute | solution.py:50
  66.4 5.3 %copy-start.9 = (f32[1,3]{1,0:T(1,128)S(1)}, f32[1,3]{1,0:T(1,128)}, u32[]{:S(2)}) copy-start(f32[1,3]{1,0:T(1,128)} %param.11) | copy-start | bytes 40
  71.8 6.2 %collective-permute-start.10 = (f32[3,128]{0,1:T(8,128)S(1)}, f32[3,128]{0,1:T(8,128)S(1)}, u32[]{:S(2)}, u32[]{:S(2)}) collective-permute-start(f32[3,128]{0,1:T(8,128)S(1)} %broadcast_in_dim.33), channel_id=1, source_target_pairs={{64,96},{65,97},{66,98},{67,99},{68,100},{69,101},{70,102},{71,103... | collective-permute-start | bytes 4616 | tf_op jit(solution)/shard_map/ppermute | solution.py:402
  141.4 16.6 %collective-permute-start.20 = (bf16[256,1024]{1,0:T(8,128)(2,1)S(1)}, bf16[256,1024]{1,0:T(8,128)(2,1)S(1)}, u32[]{:S(2)}, u32[]{:S(2)}) collective-permute-start(bf16[256,1024]{1,0:T(8,128)(2,1)S(1)} %shard_map.108.refs_8_), channel_id=1, source_target_pairs={{0,32},{64,96},{1,33},{65,97},{2,34},{66,98},{3,35},{67,99},{4,36}... | collective-permute-start | bytes 1572872 | tf_op jit(solution)/shard_map/ppermute | solution.py:402
  146.4 22.9 %collective-permute-start.21 = (bf16[256,1024]{1,0:T(8,128)(2,1)S(1)}, bf16[256,1024]{1,0:T(8,128)(2,1)S(1)}, u32[]{:S(2)}, u32[]{:S(2)}) collective-permute-start(bf16[256,1024]{1,0:T(8,128)(2,1)S(1)} %shard_map.109.refs_9_), channel_id=1, source_target_pairs={{0,32},{64,96},{1,33},{65,97},{2,34},{66,98},{3,35},{67,99},{4,36}... | collective-permute-start | bytes 1572872 | tf_op jit(solution)/shard_map/ppermute | solution.py:402
  151.6 29.0 %collective-permute-start.22 = (bf16[256,1024]{1,0:T(8,128)(2,1)S(1)}, bf16[256,1024]{1,0:T(8,128)(2,1)S(1)}, u32[]{:S(2)}, u32[]{:S(2)}) collective-permute-start(bf16[256,1024]{1,0:T(8,128)(2,1)S(1)} %shard_map.110.refs_10_), channel_id=1, source_target_pairs={{0,32},{64,96},{1,33},{65,97},{2,34},{66,98},{3,35},{67,99},{4,36}... | collective-permute-start | bytes 1572872 | tf_op jit(solution)/shard_map/ppermute | solution.py:402
  156.5 34.9 %collective-permute-start.23 = (bf16[256,1024]{1,0:T(8,128)(2,1)S(1)}, bf16[256,1024]{1,0:T(8,128)(2,1)S(1)}, u32[]{:S(2)}, u32[]{:S(2)}) collective-permute-start(bf16[256,1024]{1,0:T(8,128)(2,1)S(1)} %shard_map.111.refs_11_), channel_id=1, source_target_pairs={{0,32},{64,96},{1,33},{65,97},{2,34},{66,98},{3,35},{67,99},{4,36}... | collective-permute-start | bytes 1572872 | tf_op jit(solution)/shard_map/ppermute | solution.py:402
  193.4 34.7 %collective-permute-start.25 = (bf16[256,512]{1,0:T(8,128)(2,1)S(1)}, bf16[256,512]{1,0:T(8,128)(2,1)S(1)}, u32[]{:S(2)}, u32[]{:S(2)}) collective-permute-start(bf16[256,512]{1,0:T(8,128)(2,1)S(1)} %get-tuple-element.12), channel_id=1, source_target_pairs={{32,96},{33,97},{34,98},{35,99},{36,100},{37,101},{38,102},{39,103... | collective-permute-start | bytes 786440 | tf_op jit(solution)/shard_map/ppermute | solution.py:402
  194.7 33.4 %collective-permute-start.24 = (bf16[256,512]{1,0:T(8,128)(2,1)S(1)}, bf16[256,512]{1,0:T(8,128)(2,1)S(1)}, u32[]{:S(2)}, u32[]{:S(2)}) collective-permute-start(bf16[256,512]{1,0:T(8,128)(2,1)S(1)} %get-tuple-element.12), channel_id=1, source_target_pairs={{32,64},{33,65},{34,66},{35,67},{36,68},{37,69},{38,70},{39,71},{4... | collective-permute-start | bytes 786440 | tf_op jit(solution)/shard_map/ppermute | solution.py:402
  (5 other events, 10.1 us)
Sparse Core Ops, SparseCore 0:
  10.3 124.9 all-gather.1

commit v5 on v4

--- a/solution.py
+++ b/solution.py
@@ -126,10 +126,13 @@
     )(*blocks)
 
 
+def inverse_norm(wide):
+    return lax.rsqrt(jnp.mean(wide * wide, axis=-1, keepdims=True) + EPS)
+
+
 def norm_into(xn_ref, x_ref, gain_ref, row):
     wide = x_ref[...].astype(F32)
-    inv = lax.rsqrt(jnp.mean(wide * wide, axis=-1, keepdims=True) + EPS)
-    xn_ref[...] = (wide * inv * gain_ref[row : row + 1, :]).astype(BF16)
+    xn_ref[...] = (wide * inverse_norm(wide) * gain_ref[row : row + 1, :]).astype(BF16)
 
 
 def attend(q, keys_ref, values_ref, resid, lengths_ref, key_scale, value_scale):
@@ -297,10 +300,11 @@
         of_layer(0).wait()
         project_into(k_ref, v_ref, xn_ref[...], kv_buf[0])
         run()
+        inv = inverse_norm(out_ref[...].astype(F32))
         for i in (1, 2):
             of_layer(i).wait()
         for i in (1, 2):
-            norm_into(xn_ref, out_ref, gain_ref, i)
+            xn_ref[...] = (out_ref[...].astype(F32) * inv * gain_ref[i : i + 1, :]).astype(BF16)
             at = (i - 1) * 2 * HEAD
             project_into(
                 cross_ref.at[:, pl.ds(at, HEAD)],
@@ -311,13 +315,13 @@
 
 
 def decoder_kernel(count, *refs):
-    section_ref, lengths_ref, scale_ref, gain_ref, full, cross_ref, first_out, target = refs[:8]
-    made, passed = refs[8 : 8 + count], refs[8 + count : 8 + 2 * count]
-    out_ref = refs[8 + 2 * count]
-    buf, sems, xn_ref, q_ref, x_ref, x_sems, mid_ref = refs[9 + 2 * count :]
+    section_ref, lengths_ref, scale_ref, gain_ref, full, cross2_ref, cross3_ref, first_out, target = refs[:9]
+    made, passed = refs[9 : 9 + count], refs[9 + count : 9 + 2 * count]
+    out_ref = refs[9 + 2 * count]
+    buf, sems, xn_ref, q_ref, x_ref, x_sems, mid_ref = refs[10 + 2 * count :]
     section = section_ref[0]
     blocks = x_ref.shape[1] // BLOCK
-    cols = lambda i: cross_ref.at[:, pl.ds(i * HEAD, HEAD)]
+    cols = lambda ref, i: ref.at[:, pl.ds(i * HEAD, HEAD)]
 
     def fetch(pieces, into):
         copies = bring(pieces, into, x_sems)
@@ -326,11 +330,11 @@
         for copy in copies:
             copy.wait()
 
-    def attend_all(resid_ref, into):
+    def attend_all(cross_ref, into):
         def step(b, carry):
             columns = pl.ds(pl.multiple_of(b * BLOCK, BLOCK), BLOCK)
             into[:, columns] = attend(
-                x_ref[:, columns], cols(0), cols(1), resid_ref[:, columns], lengths_ref, scale_ref[4], scale_ref[5]
+                x_ref[:, columns], cols(cross_ref, 0), cols(cross_ref, 1), target[:, columns], lengths_ref, scale_ref[4], scale_ref[5]
             )
             return carry
 
@@ -347,12 +351,12 @@
     @pl.when(section == 2)
     def _():
         fetch(made, x_ref)
-        attend_all(target, out_ref)
+        attend_all(cross2_ref, out_ref)
 
     @pl.when(section == 3)
     def _():
         start, run = stream_layer(
-            full, buf, sems, xn_ref, q_ref, cols(2), cols(3), mid_ref, lengths_ref, scale_ref, out_ref
+            full, buf, sems, xn_ref, q_ref, cols(cross3_ref, 2), cols(cross3_ref, 3), mid_ref, lengths_ref, scale_ref, out_ref
         )
         copies = bring(passed, x_ref, x_sems)
         for copy in copies:
@@ -360,7 +364,7 @@
         start()
         for copy in copies:
             copy.wait()
-        attend_all(target, mid_ref)
+        attend_all(cross3_ref, mid_ref)
         norm_into(xn_ref, mid_ref, gain_ref, 0)
         run()
 
@@ -471,17 +475,17 @@
         compiler_params=params(),
         cost_estimate=layer_cost,
     )(section, row_order(), seq_lengths, scales, all_gains, full, kv_own, kv_other, *passed)
-    cross = hop(cross, [(1, 2)]) + hop(cross, [(1, 3)])
+    cross2, cross3 = hop(cross[:, : 2 * HEAD], [(1, 2)]), hop(cross, [(1, 3)])
 
     result = pl.pallas_call(
         functools.partial(decoder_kernel, n),
         out_shape=row_shape,
-        in_specs=[SMEM] * 3 + [VMEM, ANY, VMEM, ANY, VMEM] + [ANY] * (2 * n),
+        in_specs=[SMEM] * 3 + [VMEM, ANY, VMEM, VMEM, ANY, VMEM] + [ANY] * (2 * n),
         out_specs=VMEM,
         scratch_shapes=scratch + [pltpu.VMEM((rows, width), BF16)],
         compiler_params=params(),
         cost_estimate=layer_cost,
-    )(section, seq_lengths, all_scales, wide_gain, full, cross, out1, target2, *made, *passed)
+    )(section, seq_lengths, all_scales, wide_gain, full, cross2, cross3, out1, target2, *made, *passed)
     return result.reshape(1, micro, seqs, length, width), next_part[None]
 
 

time: 259 us -> 259 us (level)
  no operation moved by 1% of the time
where the time goes in v5:
time: 259 us; the launch traced here: 258 us
  waiting for transfers between devices  144 us (56%)
  Pallas kernels  48.5 us (19%)
  starting transfers between devices  39.9 us (15%)
  between operations  16.7 us (6%)
  other arithmetic  4.32 us (2%)
  local copies, waits for them, and re-layouts  3.66 us (1%)
    ppermute x9, waiting for transfers between devices, shards(): hop = lambda value, pairs: lax.ppermute(value, 'section', pairs)  70.5 us
    all_gather x1, waiting for transfers between devices, shards(): lax.all_gather(jnp.concatenate([weight, kv_part], 1), 'fsdp', axis=0, til...  57.4 us
    pallas_call x1, Pallas kernels, shards(): pl.pallas_call(functools.partial(decoder_kernel, n), out_shape=row_shape,...  23.9 us
    ppermute x10, starting transfers between devices, send(): return lax.ppermute(value, 'fsdp', pairs)  21.4 us
    ppermute x10, waiting for transfers between devices, send(): return lax.ppermute(value, 'fsdp', pairs)  16.1 us
    pallas_call x4, Pallas kernels, layer_part(): pl.pallas_call(part_kernel, grid=(PIECE // BLOCK,), out_shape=jax.ShapeDt...  14.6 us
    ppermute x9, starting transfers between devices, shards(): hop = lambda value, pairs: lax.ppermute(value, 'section', pairs)  12.4 us
    ppermute x7, starting transfers between devices, send_one(): lax.ppermute(value, ('section', 'fsdp'), [(32 + a, 32 + b) for a, b in pa...  6.1 us
  transfers between devices with their start and end apart: 27, of which 15 were waited for; matrix products, arithmetic and copies ran while one was open for 2% of the time, Pallas kernels for 7%

profile of v5, /device:TPU:24, one launch (start us, length us, event | category | flops | bytes accessed | tf_op | source)
XLA Modules:
  0.0 258.1 jit_solution(14436697576822238763)
XLA Ops:
  7.2 2.4 pad_maximum_fusion
  9.8 3.1 %collective-permute-start.12 = (bf16[144,256]{1,0:T(8,128)(2,1)S(1)}, bf16[144,256]{1,0:T(8,128)(2,1)S(1)}, u32[]{:S(2)}, u32[]{:S(2)}) collective-permute-start(bf16[144,256]{1,0:T(8,128)(2,1)S(1)} %pad_maximum_fusion.2), channel_id=1, source_target_pairs={{96,32},{97,33},{98,34},{99,35},{100,36},{101,37},{102,38},{103,39... | collective-permute-start | bytes 221192 | tf_op jit(solution)/shard_map/ppermute | solution.py:406
  17.1 2.0 collective-permute-start.1
  21.3 1.6 collective-permute-start.2
  22.9 2.3 collective-permute-done.2
  25.2 3.6 %collective-permute-start.3 = (f32[34,128]{1,0:T(8,128)S(1)}, f32[34,128]{1,0:T(8,128)S(1)}, u32[]{:S(2)}, u32[]{:S(2)}) collective-permute-start(f32[34,128]{1,0:T(8,128)S(1)} %add.140), channel_id=1, source_target_pairs={{0,4},{1,5},{2,6},{3,7},{4,0},{5,1},{6,2},{7,3},{8,12},{9,13},{10,... | collective-permute-start | bytes 52232 | tf_op jit(solution)/shard_map/ppermute | solution.py:50
  28.8 2.2 collective-permute-done.3
  30.9 3.4 %collective-permute-start.4 = (f32[34,128]{1,0:T(8,128)S(1)}, f32[34,128]{1,0:T(8,128)S(1)}, u32[]{:S(2)}, u32[]{:S(2)}) collective-permute-start(f32[34,128]{1,0:T(8,128)S(1)} %add.141), channel_id=1, source_target_pairs={{0,16},{1,17},{2,18},{3,19},{4,20},{5,21},{6,22},{7,23},{8,24},{9,... | collective-permute-start | bytes 52232 | tf_op jit(solution)/shard_map/ppermute | solution.py:50
  34.4 2.3 collective-permute-done.4
  41.9 1.5 shard_map.105.refs_0_.refs_6_
  43.5 2.0 collective-permute-start.19
  47.1 1.6 collective-permute-start.6
  48.7 2.7 %collective-permute-done.6 = f32[3,128]{0,1:T(8,128)S(1)} collective-permute-done((f32[3,128]{0,1:T(8,128)S(1)}, f32[3,128]{0,1:T(8,128)S(1)}, u32[]{:S(2)}, u32[]{:S(2)}) %collective-permute-start.6) | collective-permute-done | bytes 1568 | tf_op jit(solution)/shard_map/ppermute | solution.py:50
  51.4 1.8 collective-permute-start.7
  53.6 2.2 collective-permute-done.7
  55.8 3.7 %collective-permute-start.8 = (f32[3,128]{0,1:T(8,128)S(1)}, f32[3,128]{0,1:T(8,128)S(1)}, u32[]{:S(2)}, u32[]{:S(2)}) collective-permute-start(f32[3,128]{0,1:T(8,128)S(1)} %add.148), channel_id=1, source_target_pairs={{0,4},{1,5},{2,6},{3,7},{4,0},{5,1},{6,2},{7,3},{8,12},{9,13},{10,... | collective-permute-start | bytes 4616 | tf_op jit(solution)/shard_map/ppermute | solution.py:50
  59.5 3.3 %collective-permute-done.8 = f32[3,128]{0,1:T(8,128)S(1)} collective-permute-done((f32[3,128]{0,1:T(8,128)S(1)}, f32[3,128]{0,1:T(8,128)S(1)}, u32[]{:S(2)}, u32[]{:S(2)}) %collective-permute-start.8) | collective-permute-done | bytes 1568 | tf_op jit(solution)/shard_map/ppermute | solution.py:50
  62.8 3.5 %collective-permute-start.9 = (f32[3,128]{0,1:T(8,128)S(1)}, f32[3,128]{0,1:T(8,128)S(1)}, u32[]{:S(2)}, u32[]{:S(2)}) collective-permute-start(f32[3,128]{0,1:T(8,128)S(1)} %add.149), channel_id=1, source_target_pairs={{0,16},{1,17},{2,18},{3,19},{4,20},{5,21},{6,22},{7,23},{8,24},{9,... | collective-permute-start | bytes 4616 | tf_op jit(solution)/shard_map/ppermute | solution.py:50
  66.4 4.0 %shard_map.106 = (bf16[256,4096]{1,0:T(8,128)(2,1)S(1)}, bf16[256,4096]{1,0:T(8,128)(2,1)S(1)}) custom-call(s32[1]{0:T(128)} %bitcast.section_ref.refs_0_, bf16[256,4096]{1,0:T(8,128)(2,1)} %bitcast.91, bf16[256,4096]{1,0:T(8,128)(2,1)} %bitcast.88, f32[1,4096]{1,0:T(1,128)S(1)} %get-tuple-element.23.gain_ref.refs_3_), custom_call_target="tpu_custom_call" | custom-call | flops 131072 | bytes 131072 | tf_op jit(solution)/shard_map/pallas_call | solution.py:425
  73.1 4.8 %collective-permute-done.10 = f32[3,128]{0,1:T(8,128)S(1)} collective-permute-done((f32[3,128]{0,1:T(8,128)S(1)}, f32[3,128]{0,1:T(8,128)S(1)}, u32[]{:S(2)}, u32[]{:S(2)}) %collective-permute-start.10) | collective-permute-done | bytes 1568 | tf_op jit(solution)/shard_map/ppermute | solution.py:406
  78.0 57.4 %all-gather.2.cloned.1.call-done.kv_ref.w_ref.refs_5_.refs_4_ = bf16[4096,4352]{1,0:T(8,128)(2,1)} async-done(((bf16[128,4352]{1,0:T(8,128)(2,1)}), bf16[4096,4352]{1,0:T(8,128)(2,1)}) %all-gather.2.cloned.1.call-update) | async-done | bytes 35651600 | tf_op jit(solution)/shard_map/all_gather | solution.py:416
  135.3 2.4 shard_map.107
  137.8 3.6 %shard_map.108.refs_9_ = bf16[256,1024]{1,0:T(8,128)(2,1)S(1)} custom-call(s32[2]{0:T(128)S(1)} %bitcast.81, s32[1]{0:T(128)} %bitcast.section_ref.refs_0_, f32[3]{0:T(128)S(1)} %get-tuple-element.21.scale_ref.refs_3_, bf16[256,4096]{1,0:T(8,128)(2,1)S(1)} %get-tuple-element.8.xn_ref, ...), custom_call_target="tpu_custom_call" | custom-call | flops 33554432 | bytes 131072 | tf_op jit(solution)/shard_map/pallas_call | solution.py:198
  142.7 3.7 %shard_map.109.refs_10_ = bf16[256,1024]{1,0:T(8,128)(2,1)S(1)} custom-call(s32[2]{0:T(128)S(1)} %bitcast.82, s32[1]{0:T(128)} %bitcast.section_ref.refs_0_, f32[3]{0:T(128)S(1)} %get-tuple-element.21.scale_ref.refs_3_, bf16[256,4096]{1,0:T(8,128)(2,1)S(1)} %get-tuple-element.8.xn_ref, ...), custom_call_target="tpu_custom_call" | custom-call | flops 33554432 | bytes 131072 | tf_op jit(solution)/shard_map/pallas_call | solution.py:198
  146.4 1.5 collective-permute-start.21
  147.9 3.7 %shard_map.110.refs_11_ = bf16[256,1024]{1,0:T(8,128)(2,1)S(1)} custom-call(s32[2]{0:T(128)S(1)} %bitcast.83, s32[1]{0:T(128)} %bitcast.section_ref.refs_0_, f32[3]{0:T(128)S(1)} %get-tuple-element.21.scale_ref.refs_3_, bf16[256,4096]{1,0:T(8,128)(2,1)S(1)} %get-tuple-element.8.xn_ref, ...), custom_call_target="tpu_custom_call" | custom-call | flops 33554432 | bytes 131072 | tf_op jit(solution)/shard_map/pallas_call | solution.py:198
  152.9 3.6 %shard_map.111.refs_12_ = bf16[256,1024]{1,0:T(8,128)(2,1)S(1)} custom-call(s32[2]{0:T(128)S(1)} %bitcast.84, s32[1]{0:T(128)} %bitcast.section_ref.refs_0_, f32[3]{0:T(128)S(1)} %get-tuple-element.21.scale_ref.refs_3_, bf16[256,4096]{1,0:T(8,128)(2,1)S(1)} %get-tuple-element.8.xn_ref, ...), custom_call_target="tpu_custom_call" | custom-call | flops 33554432 | bytes 131072 | tf_op jit(solution)/shard_map/pallas_call | solution.py:198
  158.1 11.2 %collective-permute-done.21.refs_9_.refs_14_ = bf16[256,1024]{1,0:T(8,128)(2,1)S(1)} collective-permute-done((bf16[256,1024]{1,0:T(8,128)(2,1)S(1)}, bf16[256,1024]{1,0:T(8,128)(2,1)S(1)}, u32[]{:S(2)}, u32[]{:S(2)}) %collective-permute-start.21) | collective-permute-done | bytes 524320 | tf_op jit(solution)/shard_map/ppermute | solution.py:406
  169.3 11.2 %collective-permute-done.22.refs_10_.refs_15_ = bf16[256,1024]{1,0:T(8,128)(2,1)S(1)} collective-permute-done((bf16[256,1024]{1,0:T(8,128)(2,1)S(1)}, bf16[256,1024]{1,0:T(8,128)(2,1)S(1)}, u32[]{:S(2)}, u32[]{:S(2)}) %collective-permute-start.22) | collective-permute-done | bytes 524320 | tf_op jit(solution)/shard_map/ppermute | solution.py:406
  180.5 10.9 %collective-permute-done.23.refs_11_.refs_16_ = bf16[256,1024]{1,0:T(8,128)(2,1)S(1)} collective-permute-done((bf16[256,1024]{1,0:T(8,128)(2,1)S(1)}, bf16[256,1024]{1,0:T(8,128)(2,1)S(1)}, u32[]{:S(2)}, u32[]{:S(2)}) %collective-permute-start.23) | collective-permute-done | bytes 524320 | tf_op jit(solution)/shard_map/ppermute | solution.py:406
  196.1 31.3 %collective-permute-done.25.refs_6_ = bf16[256,512]{1,0:T(8,128)(2,1)S(1)} collective-permute-done((bf16[256,512]{1,0:T(8,128)(2,1)S(1)}, bf16[256,512]{1,0:T(8,128)(2,1)S(1)}, u32[]{:S(2)}, u32[]{:S(2)}) %collective-permute-start.25) | collective-permute-done | bytes 262176 | tf_op jit(solution)/shard_map/ppermute | solution.py:406
  227.3 23.9 %shard_map.113 = bf16[256,4096]{1,0:T(8,128)(2,1)} custom-call(s32[1]{0:T(128)} %bitcast.section_ref.refs_0_, s32[2]{0:T(128)S(1)} %bitcast.86, f32[6]{0:T(128)S(1)} %pad_maximum_fusion.3.refs_2_, f32[1,4096]{1,0:T(1,128)S(1)} %get-tuple-element.23.gain_ref.refs_3_, bf16[4096,4352]{1,0:T(8,128)(2,1)} %all-gather.2.cloned.1.call-done.kv_ref.w_ref.refs_5_.refs_4_, ...), custom_call_target="tpu_custom_call" | custom-call | flops 134217728 | bytes 524288 | tf_op jit(solution)/shard_map/pallas_call | solution.py:480
  (102 shorter events, 23.0 us)
Async XLA Ops:
  7.2 2.6 %copy-start.5 = (bf16[1,128,256]{2,1,0:T(8,128)(2,1)S(1)}, bf16[1,128,256]{2,1,0:T(8,128)(2,1)}, u32[]{:S(2)}) copy-start(bf16[1,128,256]{2,1,0:T(8,128)(2,1)} %param.10) | copy-start | bytes 196612
  7.2 6.5 %copy-start.4 = (bf16[1,128,4096]{2,1,0:T(8,128)(2,1)S(1)}, bf16[1,128,4096]{2,1,0:T(8,128)(2,1)}, u32[]{:S(2)}) copy-start(bf16[1,128,4096]{2,1,0:T(8,128)(2,1)} %param.9) | copy-start | bytes 3145732
  7.2 6.4 %copy-start.7 = (bf16[1,3,128]{2,1,0:T(4,128)(2,1)S(1)}, bf16[1,3,128]{2,1,0:T(4,128)(2,1)}, u32[]{:S(2)}) copy-start(bf16[1,3,128]{2,1,0:T(4,128)(2,1)} %param.13) | copy-start | bytes 2308
  7.2 128.1 %all-gather.2.cloned.1.call-start = ((), (), s32[]{:S(2)}) async-start(), calls=%async_computation | async-start | bytes 36765696 | tf_op jit(solution)/shard_map/all_gather | solution.py:416
  9.8 5.1 %collective-permute-start.12 = (bf16[144,256]{1,0:T(8,128)(2,1)S(1)}, bf16[144,256]{1,0:T(8,128)(2,1)S(1)}, u32[]{:S(2)}, u32[]{:S(2)}) collective-permute-start(bf16[144,256]{1,0:T(8,128)(2,1)S(1)} %pad_maximum_fusion.2), channel_id=1, source_target_pairs={{96,32},{97,33},{98,34},{99,35},{100,36},{101,37},{102,38},{103,39... | collective-permute-start | bytes 221192 | tf_op jit(solution)/shard_map/ppermute | solution.py:406
  13.0 2.0 collective-permute-start.11
  15.0 1.5 collective-permute-start.13
  15.7 1.5 collective-permute-start
  15.8 3.4 %collective-permute-start.14 = (bf16[128,512]{1,0:T(8,128)(2,1)S(1)}, bf16[128,512]{1,0:T(8,128)(2,1)S(1)}, u32[]{:S(2)}, u32[]{:S(2)}) collective-permute-start(bf16[128,512]{1,0:T(8,128)(2,1)S(1)} %pad_maximum_fusion.1.refs_0_), channel_id=1, source_target_pairs={{32,38},{33,57},{34,32},{35,59},{36,34},{37,61},{38,36},{39,63},{4... | collective-permute-start | bytes 393224 | tf_op jit(solution)/shard_map/ppermute | solution.py:62
  16.4 2.7 %collective-permute-start.15 = (bf16[128,512]{1,0:T(8,128)(2,1)S(1)}, bf16[128,512]{1,0:T(8,128)(2,1)S(1)}, u32[]{:S(2)}, u32[]{:S(2)}) collective-permute-start(bf16[128,512]{1,0:T(8,128)(2,1)S(1)} %collective-permute-done.13.refs_1_), channel_id=1, source_target_pairs={{32,34},{33,41},{34,36},{35,43},{36,38},{37,45},{38,32},{39,47},{4... | collective-permute-start | bytes 393224 | tf_op jit(solution)/shard_map/ppermute | solution.py:62
  17.1 4.1 %collective-permute-start.1 = (f32[34,128]{1,0:T(8,128)S(1)}, f32[34,128]{1,0:T(8,128)S(1)}, u32[]{:S(2)}, u32[]{:S(2)}) collective-permute-start(f32[34,128]{1,0:T(8,128)S(1)} %fusion.39), channel_id=1, source_target_pairs={{0,2},{1,3},{2,0},{3,1},{4,6},{5,7},{6,4},{7,5},{8,10},{9,11},{10,... | collective-permute-start | bytes 52232 | tf_op jit(solution)/shard_map/ppermute | solution.py:50
  20.6 18.1 %collective-permute-start.16 = (bf16[512,512]{1,0:T(8,128)(2,1)S(1)}, bf16[512,512]{1,0:T(8,128)(2,1)S(1)}, u32[]{:S(2)}, u32[]{:S(2)}) collective-permute-start(bf16[512,512]{1,0:T(8,128)(2,1)S(1)} %shard_map.104.refs_0_), channel_id=1, source_target_pairs={{32,40},{33,35},{34,42},{35,37},{36,44},{37,39},{38,46},{39,33},{4... | collective-permute-start | bytes 1572872 | tf_op jit(solution)/shard_map/ppermute | solution.py:62
  21.3 3.9 %collective-permute-start.2 = (f32[34,128]{1,0:T(8,128)S(1)}, f32[34,128]{1,0:T(8,128)S(1)}, u32[]{:S(2)}, u32[]{:S(2)}) collective-permute-start(f32[34,128]{1,0:T(8,128)S(1)} %fusion.44), channel_id=1, source_target_pairs={{0,8},{1,9},{2,10},{3,11},{4,12},{5,13},{6,14},{7,15},{8,0},{9,1},... | collective-permute-start | bytes 52232 | tf_op jit(solution)/shard_map/ppermute | solution.py:50
  25.2 5.8 %collective-permute-start.3 = (f32[34,128]{1,0:T(8,128)S(1)}, f32[34,128]{1,0:T(8,128)S(1)}, u32[]{:S(2)}, u32[]{:S(2)}) collective-permute-start(f32[34,128]{1,0:T(8,128)S(1)} %add.140), channel_id=1, source_target_pairs={{0,4},{1,5},{2,6},{3,7},{4,0},{5,1},{6,2},{7,3},{8,12},{9,13},{10,... | collective-permute-start | bytes 52232 | tf_op jit(solution)/shard_map/ppermute | solution.py:50
  30.9 5.7 %collective-permute-start.4 = (f32[34,128]{1,0:T(8,128)S(1)}, f32[34,128]{1,0:T(8,128)S(1)}, u32[]{:S(2)}, u32[]{:S(2)}) collective-permute-start(f32[34,128]{1,0:T(8,128)S(1)} %add.141), channel_id=1, source_target_pairs={{0,16},{1,17},{2,18},{3,19},{4,20},{5,21},{6,22},{7,23},{8,24},{9,... | collective-permute-start | bytes 52232 | tf_op jit(solution)/shard_map/ppermute | solution.py:50
  38.0 3.9 %collective-permute-start.17 = (bf16[512,512]{1,0:T(8,128)(2,1)S(1)}, bf16[512,512]{1,0:T(8,128)(2,1)S(1)}, u32[]{:S(2)}, u32[]{:S(2)}) collective-permute-start(bf16[512,512]{1,0:T(8,128)(2,1)S(1)} %shard_map.104.refs_0_), channel_id=1, source_target_pairs={{32,56},{33,39},{34,58},{35,33},{36,60},{37,35},{38,62},{39,37},{4... | collective-permute-start | bytes 1572872 | tf_op jit(solution)/shard_map/ppermute | solution.py:62
  38.7 3.2 %collective-permute-start.18 = (bf16[512,512]{1,0:T(8,128)(2,1)S(1)}, bf16[512,512]{1,0:T(8,128)(2,1)S(1)}, u32[]{:S(2)}, u32[]{:S(2)}) collective-permute-start(bf16[512,512]{1,0:T(8,128)(2,1)S(1)} %collective-permute-done.16.refs_1_), channel_id=1, source_target_pairs={{32,40},{33,35},{34,42},{35,37},{36,44},{37,39},{38,46},{39,33},{4... | collective-permute-start | bytes 1572872 | tf_op jit(solution)/shard_map/ppermute | solution.py:62
  41.9 11.3 %copy-start.8 = (s32[4]{0:T(128)S(1)}, s32[4]{0:T(128)}, u32[]{:S(2)}) copy-start(s32[4]{0:T(128)} %constant.90.clone) | copy-start | bytes 52
  43.5 34.5 %collective-permute-start.19 = (bf16[2048,512]{1,0:T(8,128)(2,1)}, bf16[2048,512]{1,0:T(8,128)(2,1)}, u32[]{:S(2)}, u32[]{:S(2)}) collective-permute-start(bf16[2048,512]{1,0:T(8,128)(2,1)} %shard_map.105.refs_0_.refs_6_), channel_id=1, source_target_pairs={{32,33},{33,32},{34,35},{35,34},{36,37},{37,36},{38,39},{39,38},{4... | collective-permute-start | bytes 6291464 | tf_op jit(solution)/shard_map/ppermute | solution.py:62
  45.7 1.3 collective-permute-start.5
  47.1 4.3 %collective-permute-start.6 = (f32[3,128]{0,1:T(8,128)S(1)}, f32[3,128]{0,1:T(8,128)S(1)}, u32[]{:S(2)}, u32[]{:S(2)}) collective-permute-start(f32[3,128]{0,1:T(8,128)S(1)} %broadcast_add_fusion), channel_id=1, source_target_pairs={{0,2},{1,3},{2,0},{3,1},{4,6},{5,7},{6,4},{7,5},{8,10},{9,11},{10,... | collective-permute-start | bytes 4616 | tf_op jit(solution)/shard_map/ppermute | solution.py:50
  51.4 4.3 %collective-permute-start.7 = (f32[3,128]{0,1:T(8,128)S(1)}, f32[3,128]{0,1:T(8,128)S(1)}, u32[]{:S(2)}, u32[]{:S(2)}) collective-permute-start(f32[3,128]{0,1:T(8,128)S(1)} %fusion.43), channel_id=1, source_target_pairs={{0,8},{1,9},{2,10},{3,11},{4,12},{5,13},{6,14},{7,15},{8,0},{9,1},... | collective-permute-start | bytes 4616 | tf_op jit(solution)/shard_map/ppermute | solution.py:50
  55.8 7.0 %collective-permute-start.8 = (f32[3,128]{0,1:T(8,128)S(1)}, f32[3,128]{0,1:T(8,128)S(1)}, u32[]{:S(2)}, u32[]{:S(2)}) collective-permute-start(f32[3,128]{0,1:T(8,128)S(1)} %add.148), channel_id=1, source_target_pairs={{0,4},{1,5},{2,6},{3,7},{4,0},{5,1},{6,2},{7,3},{8,12},{9,13},{10,... | collective-permute-start | bytes 4616 | tf_op jit(solution)/shard_map/ppermute | solution.py:50
  62.8 8.9 %collective-permute-start.9 = (f32[3,128]{0,1:T(8,128)S(1)}, f32[3,128]{0,1:T(8,128)S(1)}, u32[]{:S(2)}, u32[]{:S(2)}) collective-permute-start(f32[3,128]{0,1:T(8,128)S(1)} %add.149), channel_id=1, source_target_pairs={{0,16},{1,17},{2,18},{3,19},{4,20},{5,21},{6,22},{7,23},{8,24},{9,... | collective-permute-start | bytes 4616 | tf_op jit(solution)/shard_map/ppermute | solution.py:50
  66.4 5.3 %copy-start.9 = (f32[1,3]{1,0:T(1,128)S(1)}, f32[1,3]{1,0:T(1,128)}, u32[]{:S(2)}) copy-start(f32[1,3]{1,0:T(1,128)} %param.11) | copy-start | bytes 40
  71.8 6.2 %collective-permute-start.10 = (f32[3,128]{0,1:T(8,128)S(1)}, f32[3,128]{0,1:T(8,128)S(1)}, u32[]{:S(2)}, u32[]{:S(2)}) collective-permute-start(f32[3,128]{0,1:T(8,128)S(1)} %broadcast_in_dim.33), channel_id=1, source_target_pairs={{64,96},{65,97},{66,98},{67,99},{68,100},{69,101},{70,102},{71,103... | collective-permute-start | bytes 4616 | tf_op jit(solution)/shard_map/ppermute | solution.py:406
  141.4 16.6 %collective-permute-start.20 = (bf16[256,1024]{1,0:T(8,128)(2,1)S(1)}, bf16[256,1024]{1,0:T(8,128)(2,1)S(1)}, u32[]{:S(2)}, u32[]{:S(2)}) collective-permute-start(bf16[256,1024]{1,0:T(8,128)(2,1)S(1)} %shard_map.108.refs_9_), channel_id=1, source_target_pairs={{0,32},{64,96},{1,33},{65,97},{2,34},{66,98},{3,35},{67,99},{4,36}... | collective-permute-start | bytes 1572872 | tf_op jit(solution)/shard_map/ppermute | solution.py:406
  146.4 22.9 %collective-permute-start.21 = (bf16[256,1024]{1,0:T(8,128)(2,1)S(1)}, bf16[256,1024]{1,0:T(8,128)(2,1)S(1)}, u32[]{:S(2)}, u32[]{:S(2)}) collective-permute-start(bf16[256,1024]{1,0:T(8,128)(2,1)S(1)} %shard_map.109.refs_10_), channel_id=1, source_target_pairs={{0,32},{64,96},{1,33},{65,97},{2,34},{66,98},{3,35},{67,99},{4,36}... | collective-permute-start | bytes 1572872 | tf_op jit(solution)/shard_map/ppermute | solution.py:406
  151.6 29.0 %collective-permute-start.22 = (bf16[256,1024]{1,0:T(8,128)(2,1)S(1)}, bf16[256,1024]{1,0:T(8,128)(2,1)S(1)}, u32[]{:S(2)}, u32[]{:S(2)}) collective-permute-start(bf16[256,1024]{1,0:T(8,128)(2,1)S(1)} %shard_map.110.refs_11_), channel_id=1, source_target_pairs={{0,32},{64,96},{1,33},{65,97},{2,34},{66,98},{3,35},{67,99},{4,36}... | collective-permute-start | bytes 1572872 | tf_op jit(solution)/shard_map/ppermute | solution.py:406
  156.5 34.9 %collective-permute-start.23 = (bf16[256,1024]{1,0:T(8,128)(2,1)S(1)}, bf16[256,1024]{1,0:T(8,128)(2,1)S(1)}, u32[]{:S(2)}, u32[]{:S(2)}) collective-permute-start(bf16[256,1024]{1,0:T(8,128)(2,1)S(1)} %shard_map.111.refs_12_), channel_id=1, source_target_pairs={{0,32},{64,96},{1,33},{65,97},{2,34},{66,98},{3,35},{67,99},{4,36}... | collective-permute-start | bytes 1572872 | tf_op jit(solution)/shard_map/ppermute | solution.py:406
  193.4 34.0 %collective-permute-start.25 = (bf16[256,512]{1,0:T(8,128)(2,1)S(1)}, bf16[256,512]{1,0:T(8,128)(2,1)S(1)}, u32[]{:S(2)}, u32[]{:S(2)}) collective-permute-start(bf16[256,512]{1,0:T(8,128)(2,1)S(1)} %get-tuple-element.12), channel_id=1, source_target_pairs={{32,96},{33,97},{34,98},{35,99},{36,100},{37,101},{38,102},{39,103... | collective-permute-start | bytes 786440 | tf_op jit(solution)/shard_map/ppermute | solution.py:406
  194.7 1.4 collective-permute-start.24
  (5 other events, 10.1 us)
Sparse Core Ops, SparseCore 0:
  10.3 124.9 all-gather.1

commit v6 on v5

--- a/solution.py
+++ b/solution.py
@@ -14,7 +14,7 @@
 BF16 = jnp.bfloat16
 VMEM_LIMIT = 48 * 1024 * 1024
 BLOCK = 512
-PIECE = 1024
+PIECES = (512, 512, 1024, 1024, 1024)
 SLOTS = 3
 LOG2E_SCALED = math.log2(math.e) / math.sqrt(HEAD)
 ANY = pl.BlockSpec(memory_space=pl.ANY)
@@ -124,6 +124,21 @@
         compiler_params=pltpu.CompilerParams(vmem_limit_bytes=12 * 1024 * 1024),
         cost_estimate=cost(0, 4 * count * rows * width),
     )(*blocks)
+
+
+def copy_kernel(x_ref, *refs):
+    refs[-1][...] = x_ref[...]
+
+
+def copied(x, late):
+    return pl.pallas_call(
+        copy_kernel,
+        out_shape=jax.ShapeDtypeStruct(x.shape, x.dtype),
+        in_specs=[VMEM, ANY],
+        out_specs=VMEM,
+        compiler_params=params(),
+        cost_estimate=cost(0, 0),
+    )(x, late)
 
 
 def inverse_norm(wide):
@@ -191,14 +206,14 @@
         out_ref[...] = jnp.zeros_like(out_ref)
 
 
-def layer_part(xn, full, keys, values, x, at, lengths, section, scales):
+def layer_part(xn, full, keys, values, x, at, piece, lengths, section, scales):
     rows, width = xn.shape
     first = at // BLOCK
     whole = lambda a: pl.BlockSpec(a.shape, lambda j: (0, 0))
     return pl.pallas_call(
         part_kernel,
-        grid=(PIECE // BLOCK,),
-        out_shape=jax.ShapeDtypeStruct((rows, PIECE), BF16),
+        grid=(piece // BLOCK,),
+        out_shape=jax.ShapeDtypeStruct((rows, piece), BF16),
         in_specs=[
             SMEM,
             SMEM,
@@ -211,7 +226,7 @@
         ],
         out_specs=pl.BlockSpec((rows, BLOCK), lambda j: (0, j)),
         compiler_params=params(),
-        cost_estimate=cost(2 * rows * width * PIECE, 2 * width * PIECE, rows * PIECE),
+        cost_estimate=cost(2 * rows * width * piece, 2 * width * piece, rows * piece),
     )(lengths, section, scales, xn, full, keys, values, x)
 
 
@@ -444,9 +459,19 @@
     )(xn0, full, kv_own, kv_other)
 
     made, passed = [], []
-    for at in range(0, width, PIECE):
-        made.append(layer_part(xn0, full, keys, values, x0, at, seq_lengths, section, scales))
-        passed.append(hop(made[-1], [(0, 1), (2, 3)]))
+    at = 0
+    for i, piece in enumerate(PIECES):
+        made.append(layer_part(xn0, full, keys, values, x0, at, piece, seq_lengths, section, scales))
+        at += piece
+        if i == 0:
+            relay = hop(made[0], [(0, 3), (2, 1)])
+        else:
+            passed.append(hop(made[-1], [(0, 1), (2, 3)]))
+        if i == 2:
+            relay = hop(copied(relay, made[-1]), [(3, 2), (1, 0)])
+        if i == 3:
+            relay = hop(copied(relay, made[-1]), [(2, 1), (0, 3)])
+    passed = [relay] + passed
 
     scratch = [
         pltpu.VMEM((SLOTS, width, BLOCK), BF16),

time: 259 us -> 261 us (level)
  starting transfers between devices: 39.9 us -> 46.9 us
  waiting for transfers between devices: 144 us -> 139 us
    ppermute x9 -> x12, waiting for transfers between devices: 70.5 us -> 59.5 us  [shards(): hop = lambda value, pairs: lax.ppermute(value, 'section', pairs)]
    ppermute x10, waiting for transfers between devices: 16.1 us -> 24.3 us  [send(): return lax.ppermute(value, 'fsdp', pairs)]
    ppermute x9 -> x12, starting transfers between devices: 12.4 us -> 19.7 us  [shards(): hop = lambda value, pairs: lax.ppermute(value, 'section', pairs)]
    all_gather x1, waiting for transfers between devices: 57.4 us -> 54.6 us  [shards(): lax.all_gather(jnp.concatenate([weight, kv_part], 1), 'fsdp', axis=0, til...]
    pallas_call x4 -> x7, Pallas kernels: 14.6 us -> 15.4 us  [the longest x5 15.4 us: layer_part(): pl.pallas_call(part_kernel, grid=(piece // BLOCK,), out_shape=jax.ShapeDt...]
  transfers between devices with their start and end apart: 27 -> 30, of which waited for: 15 -> 15; matrix products, arithmetic and copies ran while one was open for 2% -> 2% of each run, Pallas kernels for 7% -> 8%
where the time goes in v6:
time: 261 us; the launch traced here: 260 us
  waiting for transfers between devices  139 us (53%)
  Pallas kernels  48.9 us (19%)
  starting transfers between devices  46.9 us (18%)
  between operations  16.7 us (6%)
  other arithmetic  4.33 us (2%)
  local copies, waits for them, and re-layouts  3.64 us (1%)
    ppermute x12, waiting for transfers between devices, shards(): hop = lambda value, pairs: lax.ppermute(value, 'section', pairs)  59.5 us
    all_gather x1, waiting for transfers between devices, shards(): lax.all_gather(jnp.concatenate([weight, kv_part], 1), 'fsdp', axis=0, til...  54.6 us
    ppermute x10, waiting for transfers between devices, send(): return lax.ppermute(value, 'fsdp', pairs)  24.3 us
    pallas_call x1, Pallas kernels, shards(): pl.pallas_call(functools.partial(decoder_kernel, n), out_shape=row_shape,...  23.8 us
    ppermute x10, starting transfers between devices, send(): return lax.ppermute(value, 'fsdp', pairs)  21.1 us
    ppermute x12, starting transfers between devices, shards(): hop = lambda value, pairs: lax.ppermute(value, 'section', pairs)  19.7 us
    pallas_call x5, Pallas kernels, layer_part(): pl.pallas_call(part_kernel, grid=(piece // BLOCK,), out_shape=jax.ShapeDt...  15.4 us
    ppermute x7, starting transfers between devices, send_one(): lax.ppermute(value, ('section', 'fsdp'), [(32 + a, 32 + b) for a, b in pa...  6.07 us
  transfers between devices with their start and end apart: 30, of which 15 were waited for; matrix products, arithmetic and copies ran while one was open for 2% of the time, Pallas kernels for 8%

profile of v6, /device:TPU:24, one launch (start us, length us, event | category | flops | bytes accessed | tf_op | source)
XLA Modules:
  0.0 260.1 jit_solution(1340113232102252053)
XLA Ops:
  7.2 2.4 pad_maximum_fusion
  9.8 3.1 %collective-permute-start.12 = (bf16[144,256]{1,0:T(8,128)(2,1)S(1)}, bf16[144,256]{1,0:T(8,128)(2,1)S(1)}, u32[]{:S(2)}, u32[]{:S(2)}) collective-permute-start(bf16[144,256]{1,0:T(8,128)(2,1)S(1)} %pad_maximum_fusion.2), channel_id=1, source_target_pairs={{96,32},{97,33},{98,34},{99,35},{100,36},{101,37},{102,38},{103,39... | collective-permute-start | bytes 221192 | tf_op jit(solution)/shard_map/ppermute | solution.py:421
  20.8 1.9 collective-permute-start.1
  24.6 1.6 collective-permute-start.2
  26.2 2.7 %collective-permute-done.2 = f32[34,128]{1,0:T(8,128)S(1)} collective-permute-done((f32[34,128]{1,0:T(8,128)S(1)}, f32[34,128]{1,0:T(8,128)S(1)}, u32[]{:S(2)}, u32[]{:S(2)}) %collective-permute-start.2) | collective-permute-done | bytes 17440 | tf_op jit(solution)/shard_map/ppermute | solution.py:50
  28.9 3.9 %collective-permute-start.3 = (f32[34,128]{1,0:T(8,128)S(1)}, f32[34,128]{1,0:T(8,128)S(1)}, u32[]{:S(2)}, u32[]{:S(2)}) collective-permute-start(f32[34,128]{1,0:T(8,128)S(1)} %add.140), channel_id=1, source_target_pairs={{0,4},{1,5},{2,6},{3,7},{4,0},{5,1},{6,2},{7,3},{8,12},{9,13},{10,... | collective-permute-start | bytes 52232 | tf_op jit(solution)/shard_map/ppermute | solution.py:50
  32.8 2.2 collective-permute-done.3
  35.0 3.0 %collective-permute-start.4 = (f32[34,128]{1,0:T(8,128)S(1)}, f32[34,128]{1,0:T(8,128)S(1)}, u32[]{:S(2)}, u32[]{:S(2)}) collective-permute-start(f32[34,128]{1,0:T(8,128)S(1)} %add.141), channel_id=1, source_target_pairs={{0,16},{1,17},{2,18},{3,19},{4,20},{5,21},{6,22},{7,23},{8,24},{9,... | collective-permute-start | bytes 52232 | tf_op jit(solution)/shard_map/ppermute | solution.py:50
  38.0 2.7 %collective-permute-done.4 = f32[34,128]{1,0:T(8,128)S(1)} collective-permute-done((f32[34,128]{1,0:T(8,128)S(1)}, f32[34,128]{1,0:T(8,128)S(1)}, u32[]{:S(2)}, u32[]{:S(2)}) %collective-permute-start.4) | collective-permute-done | bytes 17440 | tf_op jit(solution)/shard_map/ppermute | solution.py:50
  42.0 1.5 shard_map.105.refs_0_.refs_6_
  43.5 2.0 collective-permute-start.19
  49.7 1.6 collective-permute-start.6
  51.4 2.7 %collective-permute-done.6 = f32[3,128]{0,1:T(8,128)S(1)} collective-permute-done((f32[3,128]{0,1:T(8,128)S(1)}, f32[3,128]{0,1:T(8,128)S(1)}, u32[]{:S(2)}, u32[]{:S(2)}) %collective-permute-start.6) | collective-permute-done | bytes 1568 | tf_op jit(solution)/shard_map/ppermute | solution.py:50
  54.1 1.6 collective-permute-start.7
  55.6 3.5 %collective-permute-done.7 = f32[3,128]{0,1:T(8,128)S(1)} collective-permute-done((f32[3,128]{0,1:T(8,128)S(1)}, f32[3,128]{0,1:T(8,128)S(1)}, u32[]{:S(2)}, u32[]{:S(2)}) %collective-permute-start.7) | collective-permute-done | bytes 1568 | tf_op jit(solution)/shard_map/ppermute | solution.py:50
  59.1 4.2 %collective-permute-start.8 = (f32[3,128]{0,1:T(8,128)S(1)}, f32[3,128]{0,1:T(8,128)S(1)}, u32[]{:S(2)}, u32[]{:S(2)}) collective-permute-start(f32[3,128]{0,1:T(8,128)S(1)} %add.148), channel_id=1, source_target_pairs={{0,4},{1,5},{2,6},{3,7},{4,0},{5,1},{6,2},{7,3},{8,12},{9,13},{10,... | collective-permute-start | bytes 4616 | tf_op jit(solution)/shard_map/ppermute | solution.py:50
  63.4 3.6 %collective-permute-done.8 = f32[3,128]{0,1:T(8,128)S(1)} collective-permute-done((f32[3,128]{0,1:T(8,128)S(1)}, f32[3,128]{0,1:T(8,128)S(1)}, u32[]{:S(2)}, u32[]{:S(2)}) %collective-permute-start.8) | collective-permute-done | bytes 1568 | tf_op jit(solution)/shard_map/ppermute | solution.py:50
  67.0 3.1 %collective-permute-start.9 = (f32[3,128]{0,1:T(8,128)S(1)}, f32[3,128]{0,1:T(8,128)S(1)}, u32[]{:S(2)}, u32[]{:S(2)}) collective-permute-start(f32[3,128]{0,1:T(8,128)S(1)} %add.149), channel_id=1, source_target_pairs={{0,16},{1,17},{2,18},{3,19},{4,20},{5,21},{6,22},{7,23},{8,24},{9,... | collective-permute-start | bytes 4616 | tf_op jit(solution)/shard_map/ppermute | solution.py:50
  70.1 4.1 %collective-permute-done.9 = f32[3,128]{0,1:T(8,128)S(1)} collective-permute-done((f32[3,128]{0,1:T(8,128)S(1)}, f32[3,128]{0,1:T(8,128)S(1)}, u32[]{:S(2)}, u32[]{:S(2)}) %collective-permute-start.9) | collective-permute-done | bytes 1568 | tf_op jit(solution)/shard_map/ppermute | solution.py:50
  75.7 3.6 %shard_map.106 = (bf16[256,4096]{1,0:T(8,128)(2,1)S(1)}, bf16[256,4096]{1,0:T(8,128)(2,1)S(1)}) custom-call(s32[1]{0:T(128)} %bitcast.section_ref.refs_0_, bf16[256,4096]{1,0:T(8,128)(2,1)} %bitcast.92, bf16[256,4096]{1,0:T(8,128)(2,1)} %bitcast.89, f32[1,4096]{1,0:T(1,128)S(1)} %get-tuple-element.23.gain_ref.refs_3_), custom_call_target="tpu_custom_call" | custom-call | flops 131072 | bytes 131072 | tf_op jit(solution)/shard_map/pallas_call | solution.py:440
  80.9 54.6 %all-gather.2.cloned.1.call-done.kv_ref.w_ref.refs_5_.refs_4_ = bf16[4096,4352]{1,0:T(8,128)(2,1)} async-done(((bf16[128,4352]{1,0:T(8,128)(2,1)}), bf16[4096,4352]{1,0:T(8,128)(2,1)}) %all-gather.2.cloned.1.call-update) | async-done | bytes 35651600 | tf_op jit(solution)/shard_map/all_gather | solution.py:431
  135.6 2.4 shard_map.107
  138.1 2.2 shard_map.108.refs_9_
  141.7 3.6 %shard_map.109.refs_0_.refs_11_ = bf16[256,1024]{1,0:T(8,128)(2,1)S(1)} custom-call(s32[2]{0:T(128)S(1)} %bitcast.82, s32[1]{0:T(128)} %bitcast.section_ref.refs_0_, f32[3]{0:T(128)S(1)} %get-tuple-element.21.scale_ref.refs_3_, bf16[256,4096]{1,0:T(8,128)(2,1)S(1)} %get-tuple-element.8.xn_ref, ...), custom_call_target="tpu_custom_call" | custom-call | flops 33554432 | bytes 131072 | tf_op jit(solution)/shard_map/pallas_call | solution.py:213
  145.3 6.6 %collective-permute-done.20.x_ref = bf16[256,512]{1,0:T(8,128)(2,1)S(1)} collective-permute-done((bf16[256,512]{1,0:T(8,128)(2,1)S(1)}, bf16[256,512]{1,0:T(8,128)(2,1)S(1)}, u32[]{:S(2)}, u32[]{:S(2)}) %collective-permute-start.20) | collective-permute-done | bytes 262176 | tf_op jit(solution)/shard_map/ppermute | solution.py:421
  151.9 4.7 %collective-permute-start.21 = (bf16[256,512]{1,0:T(8,128)(2,1)S(1)}, bf16[256,512]{1,0:T(8,128)(2,1)S(1)}, u32[]{:S(2)}, u32[]{:S(2)}) collective-permute-start(bf16[256,512]{1,0:T(8,128)(2,1)S(1)} %shard_map.110), channel_id=1, source_target_pairs={{96,64},{32,0},{97,65},{33,1},{98,66},{34,2},{99,67},{35,3},{100,6... | collective-permute-start | bytes 786440 | tf_op jit(solution)/shard_map/ppermute | solution.py:421
  158.1 3.7 %shard_map.114.refs_13_ = bf16[256,1024]{1,0:T(8,128)(2,1)S(1)} custom-call(s32[2]{0:T(128)S(1)} %bitcast.83, s32[1]{0:T(128)} %bitcast.section_ref.refs_0_, f32[3]{0:T(128)S(1)} %get-tuple-element.21.scale_ref.refs_3_, bf16[256,4096]{1,0:T(8,128)(2,1)S(1)} %get-tuple-element.8.xn_ref, ...), custom_call_target="tpu_custom_call" | custom-call | flops 33554432 | bytes 131072 | tf_op jit(solution)/shard_map/pallas_call | solution.py:213
  163.1 3.6 %shard_map.111.refs_0_.refs_12_ = bf16[256,1024]{1,0:T(8,128)(2,1)S(1)} custom-call(s32[2]{0:T(128)S(1)} %bitcast.84, s32[1]{0:T(128)} %bitcast.section_ref.refs_0_, f32[3]{0:T(128)S(1)} %get-tuple-element.21.scale_ref.refs_3_, bf16[256,4096]{1,0:T(8,128)(2,1)S(1)} %get-tuple-element.8.xn_ref, ...), custom_call_target="tpu_custom_call" | custom-call | flops 33554432 | bytes 131072 | tf_op jit(solution)/shard_map/pallas_call | solution.py:213
  168.0 2.2 shard_map.113.refs_10_
  173.0 26.5 %collective-permute-done.23.refs_9_.refs_15_ = bf16[256,512]{1,0:T(8,128)(2,1)S(1)} collective-permute-done((bf16[256,512]{1,0:T(8,128)(2,1)S(1)}, bf16[256,512]{1,0:T(8,128)(2,1)S(1)}, u32[]{:S(2)}, u32[]{:S(2)}) %collective-permute-start.23) | collective-permute-done | bytes 262176 | tf_op jit(solution)/shard_map/ppermute | solution.py:421
  204.3 25.1 %collective-permute-done.28.refs_6_ = bf16[256,512]{1,0:T(8,128)(2,1)S(1)} collective-permute-done((bf16[256,512]{1,0:T(8,128)(2,1)S(1)}, bf16[256,512]{1,0:T(8,128)(2,1)S(1)}, u32[]{:S(2)}, u32[]{:S(2)}) %collective-permute-start.28) | collective-permute-done | bytes 262176 | tf_op jit(solution)/shard_map/ppermute | solution.py:421
  229.4 23.8 %shard_map.116 = bf16[256,4096]{1,0:T(8,128)(2,1)} custom-call(s32[1]{0:T(128)} %bitcast.section_ref.refs_0_, s32[2]{0:T(128)S(1)} %bitcast.87, f32[6]{0:T(128)S(1)} %pad_maximum_fusion.3.refs_2_, f32[1,4096]{1,0:T(1,128)S(1)} %get-tuple-element.23.gain_ref.refs_3_, bf16[4096,4352]{1,0:T(8,128)(2,1)} %all-gather.2.cloned.1.call-done.kv_ref.w_ref.refs_5_.refs_4_, ...), custom_call_target="tpu_custom_call" | custom-call | flops 134217728 | bytes 524288 | tf_op jit(solution)/shard_map/pallas_call | solution.py:505
  (111 shorter events, 29.1 us)
Async XLA Ops:
  7.2 128.4 %all-gather.2.cloned.1.call-start = ((), (), s32[]{:S(2)}) async-start(), calls=%async_computation | async-start | bytes 36765696 | tf_op jit(solution)/shard_map/all_gather | solution.py:431
  9.8 5.1 %collective-permute-start.12 = (bf16[144,256]{1,0:T(8,128)(2,1)S(1)}, bf16[144,256]{1,0:T(8,128)(2,1)S(1)}, u32[]{:S(2)}, u32[]{:S(2)}) collective-permute-start(bf16[144,256]{1,0:T(8,128)(2,1)S(1)} %pad_maximum_fusion.2), channel_id=1, source_target_pairs={{96,32},{97,33},{98,34},{99,35},{100,36},{101,37},{102,38},{103,39... | collective-permute-start | bytes 221192 | tf_op jit(solution)/shard_map/ppermute | solution.py:421
  12.9 2.0 collective-permute-start.11
  14.9 1.6 collective-permute-start.13
  15.9 1.5 collective-permute-start.14
  16.6 0.8 collective-permute-start.15
  18.8 4.6 %collective-permute-start.16 = (bf16[512,512]{1,0:T(8,128)(2,1)S(1)}, bf16[512,512]{1,0:T(8,128)(2,1)S(1)}, u32[]{:S(2)}, u32[]{:S(2)}) collective-permute-start(bf16[512,512]{1,0:T(8,128)(2,1)S(1)} %shard_map.104.refs_0_), channel_id=1, source_target_pairs={{32,40},{33,35},{34,42},{35,37},{36,44},{37,39},{38,46},{39,33},{4... | collective-permute-start | bytes 1572872 | tf_op jit(solution)/shard_map/ppermute | solution.py:62
  19.5 1.3 collective-permute-start
  20.8 3.8 %collective-permute-start.1 = (f32[34,128]{1,0:T(8,128)S(1)}, f32[34,128]{1,0:T(8,128)S(1)}, u32[]{:S(2)}, u32[]{:S(2)}) collective-permute-start(f32[34,128]{1,0:T(8,128)S(1)} %fusion.39), channel_id=1, source_target_pairs={{0,2},{1,3},{2,0},{3,1},{4,6},{5,7},{6,4},{7,5},{8,10},{9,11},{10,... | collective-permute-start | bytes 52232 | tf_op jit(solution)/shard_map/ppermute | solution.py:50
  22.7 19.2 %collective-permute-start.17 = (bf16[512,512]{1,0:T(8,128)(2,1)S(1)}, bf16[512,512]{1,0:T(8,128)(2,1)S(1)}, u32[]{:S(2)}, u32[]{:S(2)}) collective-permute-start(bf16[512,512]{1,0:T(8,128)(2,1)S(1)} %shard_map.104.refs_0_), channel_id=1, source_target_pairs={{32,56},{33,39},{34,58},{35,33},{36,60},{37,35},{38,62},{39,37},{4... | collective-permute-start | bytes 1572872 | tf_op jit(solution)/shard_map/ppermute | solution.py:62
  23.4 18.5 %collective-permute-start.18 = (bf16[512,512]{1,0:T(8,128)(2,1)S(1)}, bf16[512,512]{1,0:T(8,128)(2,1)S(1)}, u32[]{:S(2)}, u32[]{:S(2)}) collective-permute-start(bf16[512,512]{1,0:T(8,128)(2,1)S(1)} %collective-permute-done.16.refs_1_), channel_id=1, source_target_pairs={{32,40},{33,35},{34,42},{35,37},{36,44},{37,39},{38,46},{39,33},{4... | collective-permute-start | bytes 1572872 | tf_op jit(solution)/shard_map/ppermute | solution.py:62
  24.6 4.3 %collective-permute-start.2 = (f32[34,128]{1,0:T(8,128)S(1)}, f32[34,128]{1,0:T(8,128)S(1)}, u32[]{:S(2)}, u32[]{:S(2)}) collective-permute-start(f32[34,128]{1,0:T(8,128)S(1)} %fusion.44), channel_id=1, source_target_pairs={{0,8},{1,9},{2,10},{3,11},{4,12},{5,13},{6,14},{7,15},{8,0},{9,1},... | collective-permute-start | bytes 52232 | tf_op jit(solution)/shard_map/ppermute | solution.py:50
  28.9 6.0 %collective-permute-start.3 = (f32[34,128]{1,0:T(8,128)S(1)}, f32[34,128]{1,0:T(8,128)S(1)}, u32[]{:S(2)}, u32[]{:S(2)}) collective-permute-start(f32[34,128]{1,0:T(8,128)S(1)} %add.140), channel_id=1, source_target_pairs={{0,4},{1,5},{2,6},{3,7},{4,0},{5,1},{6,2},{7,3},{8,12},{9,13},{10,... | collective-permute-start | bytes 52232 | tf_op jit(solution)/shard_map/ppermute | solution.py:50
  35.0 5.7 %collective-permute-start.4 = (f32[34,128]{1,0:T(8,128)S(1)}, f32[34,128]{1,0:T(8,128)S(1)}, u32[]{:S(2)}, u32[]{:S(2)}) collective-permute-start(f32[34,128]{1,0:T(8,128)S(1)} %add.141), channel_id=1, source_target_pairs={{0,16},{1,17},{2,18},{3,19},{4,20},{5,21},{6,22},{7,23},{8,24},{9,... | collective-permute-start | bytes 52232 | tf_op jit(solution)/shard_map/ppermute | solution.py:50
  42.0 32.3 %copy-start.9 = (f32[1,3]{1,0:T(1,128)S(1)}, f32[1,3]{1,0:T(1,128)}, u32[]{:S(2)}) copy-start(f32[1,3]{1,0:T(1,128)} %param.11) | copy-start | bytes 40
  43.5 32.0 %copy-start.8 = (s32[4]{0:T(128)S(1)}, s32[4]{0:T(128)}, u32[]{:S(2)}) copy-start(s32[4]{0:T(128)} %constant.90.clone) | copy-start | bytes 52
  43.5 37.4 %collective-permute-start.19 = (bf16[2048,512]{1,0:T(8,128)(2,1)}, bf16[2048,512]{1,0:T(8,128)(2,1)}, u32[]{:S(2)}, u32[]{:S(2)}) collective-permute-start(bf16[2048,512]{1,0:T(8,128)(2,1)} %shard_map.105.refs_0_.refs_6_), channel_id=1, source_target_pairs={{32,33},{33,32},{34,35},{35,34},{36,37},{37,36},{38,39},{39,38},{4... | collective-permute-start | bytes 6291464 | tf_op jit(solution)/shard_map/ppermute | solution.py:62
  48.4 1.3 collective-permute-start.5
  49.7 4.3 %collective-permute-start.6 = (f32[3,128]{0,1:T(8,128)S(1)}, f32[3,128]{0,1:T(8,128)S(1)}, u32[]{:S(2)}, u32[]{:S(2)}) collective-permute-start(f32[3,128]{0,1:T(8,128)S(1)} %broadcast_add_fusion), channel_id=1, source_target_pairs={{0,2},{1,3},{2,0},{3,1},{4,6},{5,7},{6,4},{7,5},{8,10},{9,11},{10,... | collective-permute-start | bytes 4616 | tf_op jit(solution)/shard_map/ppermute | solution.py:50
  54.1 5.1 %collective-permute-start.7 = (f32[3,128]{0,1:T(8,128)S(1)}, f32[3,128]{0,1:T(8,128)S(1)}, u32[]{:S(2)}, u32[]{:S(2)}) collective-permute-start(f32[3,128]{0,1:T(8,128)S(1)} %fusion.43), channel_id=1, source_target_pairs={{0,8},{1,9},{2,10},{3,11},{4,12},{5,13},{6,14},{7,15},{8,0},{9,1},... | collective-permute-start | bytes 4616 | tf_op jit(solution)/shard_map/ppermute | solution.py:50
  59.1 7.9 %collective-permute-start.8 = (f32[3,128]{0,1:T(8,128)S(1)}, f32[3,128]{0,1:T(8,128)S(1)}, u32[]{:S(2)}, u32[]{:S(2)}) collective-permute-start(f32[3,128]{0,1:T(8,128)S(1)} %add.148), channel_id=1, source_target_pairs={{0,4},{1,5},{2,6},{3,7},{4,0},{5,1},{6,2},{7,3},{8,12},{9,13},{10,... | collective-permute-start | bytes 4616 | tf_op jit(solution)/shard_map/ppermute | solution.py:50
  67.0 7.2 %collective-permute-start.9 = (f32[3,128]{0,1:T(8,128)S(1)}, f32[3,128]{0,1:T(8,128)S(1)}, u32[]{:S(2)}, u32[]{:S(2)}) collective-permute-start(f32[3,128]{0,1:T(8,128)S(1)} %add.149), channel_id=1, source_target_pairs={{0,16},{1,17},{2,18},{3,19},{4,20},{5,21},{6,22},{7,23},{8,24},{9,... | collective-permute-start | bytes 4616 | tf_op jit(solution)/shard_map/ppermute | solution.py:50
  74.3 6.6 %collective-permute-start.10 = (f32[3,128]{0,1:T(8,128)S(1)}, f32[3,128]{0,1:T(8,128)S(1)}, u32[]{:S(2)}, u32[]{:S(2)}) collective-permute-start(f32[3,128]{0,1:T(8,128)S(1)} %broadcast_in_dim.33), channel_id=1, source_target_pairs={{64,96},{65,97},{66,98},{67,99},{68,100},{69,101},{70,102},{71,103... | collective-permute-start | bytes 4616 | tf_op jit(solution)/shard_map/ppermute | solution.py:421
  140.3 11.6 %collective-permute-start.20 = (bf16[256,512]{1,0:T(8,128)(2,1)S(1)}, bf16[256,512]{1,0:T(8,128)(2,1)S(1)}, u32[]{:S(2)}, u32[]{:S(2)}) collective-permute-start(bf16[256,512]{1,0:T(8,128)(2,1)S(1)} %shard_map.108.refs_9_), channel_id=1, source_target_pairs={{0,96},{64,32},{1,97},{65,33},{2,98},{66,34},{3,99},{67,35},{4,100... | collective-permute-start | bytes 786440 | tf_op jit(solution)/shard_map/ppermute | solution.py:421
  151.9 19.7 %collective-permute-start.21 = (bf16[256,512]{1,0:T(8,128)(2,1)S(1)}, bf16[256,512]{1,0:T(8,128)(2,1)S(1)}, u32[]{:S(2)}, u32[]{:S(2)}) collective-permute-start(bf16[256,512]{1,0:T(8,128)(2,1)S(1)} %shard_map.110), channel_id=1, source_target_pairs={{96,64},{32,0},{97,65},{33,1},{98,66},{34,2},{99,67},{35,3},{100,6... | collective-permute-start | bytes 786440 | tf_op jit(solution)/shard_map/ppermute | solution.py:421
  156.6 43.0 %collective-permute-start.24 = (bf16[256,1024]{1,0:T(8,128)(2,1)S(1)}, bf16[256,1024]{1,0:T(8,128)(2,1)S(1)}, u32[]{:S(2)}, u32[]{:S(2)}) collective-permute-start(bf16[256,1024]{1,0:T(8,128)(2,1)S(1)} %shard_map.109.refs_0_.refs_11_), channel_id=1, source_target_pairs={{0,32},{64,96},{1,33},{65,97},{2,34},{66,98},{3,35},{67,99},{4,36}... | collective-permute-start | bytes 1572872 | tf_op jit(solution)/shard_map/ppermute | solution.py:421
  161.8 37.8 %collective-permute-start.26 = (bf16[256,1024]{1,0:T(8,128)(2,1)S(1)}, bf16[256,1024]{1,0:T(8,128)(2,1)S(1)}, u32[]{:S(2)}, u32[]{:S(2)}) collective-permute-start(bf16[256,1024]{1,0:T(8,128)(2,1)S(1)} %shard_map.114.refs_13_), channel_id=1, source_target_pairs={{0,32},{64,96},{1,33},{65,97},{2,34},{66,98},{3,35},{67,99},{4,36}... | collective-permute-start | bytes 1572872 | tf_op jit(solution)/shard_map/ppermute | solution.py:421
  166.7 32.9 %collective-permute-start.25 = (bf16[256,1024]{1,0:T(8,128)(2,1)S(1)}, bf16[256,1024]{1,0:T(8,128)(2,1)S(1)}, u32[]{:S(2)}, u32[]{:S(2)}) collective-permute-start(bf16[256,1024]{1,0:T(8,128)(2,1)S(1)} %shard_map.111.refs_0_.refs_12_), channel_id=1, source_target_pairs={{0,32},{64,96},{1,33},{65,97},{2,34},{66,98},{3,35},{67,99},{4,36}... | collective-permute-start | bytes 1572872 | tf_op jit(solution)/shard_map/ppermute | solution.py:421
  170.3 29.3 %collective-permute-start.23 = (bf16[256,512]{1,0:T(8,128)(2,1)S(1)}, bf16[256,512]{1,0:T(8,128)(2,1)S(1)}, u32[]{:S(2)}, u32[]{:S(2)}) collective-permute-start(bf16[256,512]{1,0:T(8,128)(2,1)S(1)} %shard_map.113.refs_10_), channel_id=1, source_target_pairs={{0,32},{64,96},{1,33},{65,97},{2,34},{66,98},{3,35},{67,99},{4,36}... | collective-permute-start | bytes 786440 | tf_op jit(solution)/shard_map/ppermute | solution.py:421
  171.6 27.9 %collective-permute-start.22 = (bf16[256,512]{1,0:T(8,128)(2,1)S(1)}, bf16[256,512]{1,0:T(8,128)(2,1)S(1)}, u32[]{:S(2)}, u32[]{:S(2)}) collective-permute-start(bf16[256,512]{1,0:T(8,128)(2,1)S(1)} %shard_map.112), channel_id=1, source_target_pairs={{64,32},{0,96},{65,33},{1,97},{66,34},{2,98},{67,35},{3,99},{68,36... | collective-permute-start | bytes 786440 | tf_op jit(solution)/shard_map/ppermute | solution.py:421
  201.6 27.8 %collective-permute-start.28 = (bf16[256,512]{1,0:T(8,128)(2,1)S(1)}, bf16[256,512]{1,0:T(8,128)(2,1)S(1)}, u32[]{:S(2)}, u32[]{:S(2)}) collective-permute-start(bf16[256,512]{1,0:T(8,128)(2,1)S(1)} %get-tuple-element.12), channel_id=1, source_target_pairs={{32,96},{33,97},{34,98},{35,99},{36,100},{37,101},{38,102},{39,103... | collective-permute-start | bytes 786440 | tf_op jit(solution)/shard_map/ppermute | solution.py:421
  202.9 1.4 collective-permute-start.27
  (8 other events, 29.5 us)
Sparse Core Ops, SparseCore 0:
  10.3 125.2 all-gather.1

commit v7 on v5

--- a/solution.py
+++ b/solution.py
@@ -14,7 +14,7 @@
 BF16 = jnp.bfloat16
 VMEM_LIMIT = 48 * 1024 * 1024
 BLOCK = 512
-PIECE = 1024
+PIECES = (512,) * 8
 SLOTS = 3
 LOG2E_SCALED = math.log2(math.e) / math.sqrt(HEAD)
 ANY = pl.BlockSpec(memory_space=pl.ANY)
@@ -191,14 +191,14 @@
         out_ref[...] = jnp.zeros_like(out_ref)
 
 
-def layer_part(xn, full, keys, values, x, at, lengths, section, scales):
+def layer_part(xn, full, keys, values, x, at, piece, lengths, section, scales):
     rows, width = xn.shape
     first = at // BLOCK
     whole = lambda a: pl.BlockSpec(a.shape, lambda j: (0, 0))
     return pl.pallas_call(
         part_kernel,
-        grid=(PIECE // BLOCK,),
-        out_shape=jax.ShapeDtypeStruct((rows, PIECE), BF16),
+        grid=(piece // BLOCK,),
+        out_shape=jax.ShapeDtypeStruct((rows, piece), BF16),
         in_specs=[
             SMEM,
             SMEM,
@@ -211,7 +211,7 @@
         ],
         out_specs=pl.BlockSpec((rows, BLOCK), lambda j: (0, j)),
         compiler_params=params(),
-        cost_estimate=cost(2 * rows * width * PIECE, 2 * width * PIECE, rows * PIECE),
+        cost_estimate=cost(2 * rows * width * piece, 2 * width * piece, rows * piece),
     )(lengths, section, scales, xn, full, keys, values, x)
 
 
@@ -444,9 +444,11 @@
     )(xn0, full, kv_own, kv_other)
 
     made, passed = [], []
-    for at in range(0, width, PIECE):
-        made.append(layer_part(xn0, full, keys, values, x0, at, seq_lengths, section, scales))
+    at = 0
+    for piece in PIECES:
+        made.append(layer_part(xn0, full, keys, values, x0, at, piece, seq_lengths, section, scales))
         passed.append(hop(made[-1], [(0, 1), (2, 3)]))
+        at += piece
 
     scratch = [
         pltpu.VMEM((SLOTS, width, BLOCK), BF16),

time: 259 us -> 263 us (1.015)
  starting transfers between devices: 39.9 us -> 45 us
  waiting for transfers between devices: 144 us -> 140 us
  Pallas kernels: 48.5 us -> 51.8 us
    ppermute x9 -> x13, waiting for transfers between devices: 70.5 us -> 60.8 us  [shards(): hop = lambda value, pairs: lax.ppermute(value, 'section', pairs)]
    ppermute x10, waiting for transfers between devices: 16.1 us -> 23.6 us  [send(): return lax.ppermute(value, 'fsdp', pairs)]
    ppermute x9 -> x13, starting transfers between devices: 12.4 us -> 17.6 us  [shards(): hop = lambda value, pairs: lax.ppermute(value, 'section', pairs)]
    pallas_call x4 -> x8, Pallas kernels: 14.6 us -> 18.4 us  [layer_part(): pl.pallas_call(part_kernel, grid=(piece // BLOCK,), out_shape=jax.ShapeDt...]
  transfers between devices with their start and end apart: 27 -> 31, of which waited for: 15 -> 17; matrix products, arithmetic and copies ran while one was open for 2% -> 1% of each run, Pallas kernels for 7% -> 9%
where the time goes in v7:
time: 263 us; the launch traced here: 262 us
  waiting for transfers between devices  140 us (53%)
  Pallas kernels  51.8 us (20%)
  starting transfers between devices  45 us (17%)
  between operations  16.7 us (6%)
  other arithmetic  4.3 us (2%)
  local copies, waits for them, and re-layouts  3.65 us (1%)
    ppermute x13, waiting for transfers between devices, shards(): hop = lambda value, pairs: lax.ppermute(value, 'section', pairs)  60.8 us
    all_gather x1, waiting for transfers between devices, shards(): lax.all_gather(jnp.concatenate([weight, kv_part], 1), 'fsdp', axis=0, til...  55.4 us
    pallas_call x1, Pallas kernels, shards(): pl.pallas_call(functools.partial(decoder_kernel, n), out_shape=row_shape,...  23.7 us
    ppermute x10, waiting for transfers between devices, send(): return lax.ppermute(value, 'fsdp', pairs)  23.6 us
    ppermute x10, starting transfers between devices, send(): return lax.ppermute(value, 'fsdp', pairs)  21.2 us
    pallas_call x8, Pallas kernels, layer_part(): pl.pallas_call(part_kernel, grid=(piece // BLOCK,), out_shape=jax.ShapeDt...  18.4 us
    ppermute x13, starting transfers between devices, shards(): hop = lambda value, pairs: lax.ppermute(value, 'section', pairs)  17.6 us
    ppermute x7, starting transfers between devices, send_one(): lax.ppermute(value, ('section', 'fsdp'), [(32 + a, 32 + b) for a, b in pa...  6.1 us
  transfers between devices with their start and end apart: 31, of which 17 were waited for; matrix products, arithmetic and copies ran while one was open for 1% of the time, Pallas kernels for 9%

profile of v7, /device:TPU:24, one launch (start us, length us, event | category | flops | bytes accessed | tf_op | source)
XLA Modules:
  0.0 262.3 jit_solution(5633726865978436385)
XLA Ops:
  7.2 2.4 pad_maximum_fusion
  9.8 3.1 %collective-permute-start.12 = (bf16[144,256]{1,0:T(8,128)(2,1)S(1)}, bf16[144,256]{1,0:T(8,128)(2,1)S(1)}, u32[]{:S(2)}, u32[]{:S(2)}) collective-permute-start(bf16[144,256]{1,0:T(8,128)(2,1)S(1)} %pad_maximum_fusion.2), channel_id=1, source_target_pairs={{96,32},{97,33},{98,34},{99,35},{100,36},{101,37},{102,38},{103,39... | collective-permute-start | bytes 221192 | tf_op jit(solution)/shard_map/ppermute | solution.py:406
  19.4 2.0 collective-permute-start.1
  24.9 2.5 collective-permute-done.2
  27.3 4.1 %collective-permute-start.3 = (f32[34,128]{1,0:T(8,128)S(1)}, f32[34,128]{1,0:T(8,128)S(1)}, u32[]{:S(2)}, u32[]{:S(2)}) collective-permute-start(f32[34,128]{1,0:T(8,128)S(1)} %add.140), channel_id=1, source_target_pairs={{0,4},{1,5},{2,6},{3,7},{4,0},{5,1},{6,2},{7,3},{8,12},{9,13},{10,... | collective-permute-start | bytes 52232 | tf_op jit(solution)/shard_map/ppermute | solution.py:50
  31.4 2.2 collective-permute-done.3
  33.6 3.1 %collective-permute-start.4 = (f32[34,128]{1,0:T(8,128)S(1)}, f32[34,128]{1,0:T(8,128)S(1)}, u32[]{:S(2)}, u32[]{:S(2)}) collective-permute-start(f32[34,128]{1,0:T(8,128)S(1)} %add.141), channel_id=1, source_target_pairs={{0,16},{1,17},{2,18},{3,19},{4,20},{5,21},{6,22},{7,23},{8,24},{9,... | collective-permute-start | bytes 52232 | tf_op jit(solution)/shard_map/ppermute | solution.py:50
  36.7 2.6 %collective-permute-done.4 = f32[34,128]{1,0:T(8,128)S(1)} collective-permute-done((f32[34,128]{1,0:T(8,128)S(1)}, f32[34,128]{1,0:T(8,128)S(1)}, u32[]{:S(2)}, u32[]{:S(2)}) %collective-permute-start.4) | collective-permute-done | bytes 17440 | tf_op jit(solution)/shard_map/ppermute | solution.py:50
  45.7 2.0 collective-permute-start.19
  51.3 2.8 %collective-permute-done.6 = f32[3,128]{0,1:T(8,128)S(1)} collective-permute-done((f32[3,128]{0,1:T(8,128)S(1)}, f32[3,128]{0,1:T(8,128)S(1)}, u32[]{:S(2)}, u32[]{:S(2)}) %collective-permute-start.6) | collective-permute-done | bytes 1568 | tf_op jit(solution)/shard_map/ppermute | solution.py:50
  55.7 3.5 %collective-permute-done.7 = f32[3,128]{0,1:T(8,128)S(1)} collective-permute-done((f32[3,128]{0,1:T(8,128)S(1)}, f32[3,128]{0,1:T(8,128)S(1)}, u32[]{:S(2)}, u32[]{:S(2)}) %collective-permute-start.7) | collective-permute-done | bytes 1568 | tf_op jit(solution)/shard_map/ppermute | solution.py:50
  59.2 3.5 %collective-permute-start.8 = (f32[3,128]{0,1:T(8,128)S(1)}, f32[3,128]{0,1:T(8,128)S(1)}, u32[]{:S(2)}, u32[]{:S(2)}) collective-permute-start(f32[3,128]{0,1:T(8,128)S(1)} %add.148), channel_id=1, source_target_pairs={{0,4},{1,5},{2,6},{3,7},{4,0},{5,1},{6,2},{7,3},{8,12},{9,13},{10,... | collective-permute-start | bytes 4616 | tf_op jit(solution)/shard_map/ppermute | solution.py:50
  63.2 3.3 %collective-permute-done.8 = f32[3,128]{0,1:T(8,128)S(1)} collective-permute-done((f32[3,128]{0,1:T(8,128)S(1)}, f32[3,128]{0,1:T(8,128)S(1)}, u32[]{:S(2)}, u32[]{:S(2)}) %collective-permute-start.8) | collective-permute-done | bytes 1568 | tf_op jit(solution)/shard_map/ppermute | solution.py:50
  66.5 3.7 %collective-permute-start.9 = (f32[3,128]{0,1:T(8,128)S(1)}, f32[3,128]{0,1:T(8,128)S(1)}, u32[]{:S(2)}, u32[]{:S(2)}) collective-permute-start(f32[3,128]{0,1:T(8,128)S(1)} %add.149), channel_id=1, source_target_pairs={{0,16},{1,17},{2,18},{3,19},{4,20},{5,21},{6,22},{7,23},{8,24},{9,... | collective-permute-start | bytes 4616 | tf_op jit(solution)/shard_map/ppermute | solution.py:50
  70.2 3.6 %collective-permute-done.9 = f32[3,128]{0,1:T(8,128)S(1)} collective-permute-done((f32[3,128]{0,1:T(8,128)S(1)}, f32[3,128]{0,1:T(8,128)S(1)}, u32[]{:S(2)}, u32[]{:S(2)}) %collective-permute-start.9) | collective-permute-done | bytes 1568 | tf_op jit(solution)/shard_map/ppermute | solution.py:50
  75.2 3.7 %shard_map.106 = (bf16[256,4096]{1,0:T(8,128)(2,1)S(1)}, bf16[256,4096]{1,0:T(8,128)(2,1)S(1)}) custom-call(s32[1]{0:T(128)} %bitcast.section_ref.refs_0_, bf16[256,4096]{1,0:T(8,128)(2,1)} %bitcast.95, bf16[256,4096]{1,0:T(8,128)(2,1)} %bitcast.92, f32[1,4096]{1,0:T(1,128)S(1)} %get-tuple-element.23.gain_ref.refs_3_), custom_call_target="tpu_custom_call" | custom-call | flops 131072 | bytes 131072 | tf_op jit(solution)/shard_map/pallas_call | solution.py:425
  80.2 55.4 %all-gather.2.cloned.1.call-done.kv_ref.w_ref.refs_5_.refs_4_ = bf16[4096,4352]{1,0:T(8,128)(2,1)} async-done(((bf16[128,4352]{1,0:T(8,128)(2,1)}), bf16[4096,4352]{1,0:T(8,128)(2,1)}) %all-gather.2.cloned.1.call-update) | async-done | bytes 35651600 | tf_op jit(solution)/shard_map/all_gather | solution.py:416
  135.6 2.4 shard_map.107
  138.1 2.2 shard_map.108.refs_9_
  141.6 2.3 shard_map.109.refs_10_
  145.2 2.5 shard_map.110.refs_11_
  149.1 2.3 shard_map.111.refs_12_
  152.7 2.2 shard_map.112.refs_13_
  156.2 2.2 shard_map.115.refs_16_
  158.5 2.2 shard_map.114.refs_15_
  160.7 2.3 shard_map.113.refs_14_
  168.2 5.0 %collective-permute-done.24.refs_12_.refs_21_ = bf16[256,512]{1,0:T(8,128)(2,1)S(1)} collective-permute-done((bf16[256,512]{1,0:T(8,128)(2,1)S(1)}, bf16[256,512]{1,0:T(8,128)(2,1)S(1)}, u32[]{:S(2)}, u32[]{:S(2)}) %collective-permute-start.24) | collective-permute-done | bytes 262176 | tf_op jit(solution)/shard_map/ppermute | solution.py:406
  173.1 9.6 %collective-permute-done.25.refs_13_.refs_22_ = bf16[256,512]{1,0:T(8,128)(2,1)S(1)} collective-permute-done((bf16[256,512]{1,0:T(8,128)(2,1)S(1)}, bf16[256,512]{1,0:T(8,128)(2,1)S(1)}, u32[]{:S(2)}, u32[]{:S(2)}) %collective-permute-start.25) | collective-permute-done | bytes 262176 | tf_op jit(solution)/shard_map/ppermute | solution.py:406
  182.7 5.6 %collective-permute-done.26.refs_14_.refs_23_ = bf16[256,512]{1,0:T(8,128)(2,1)S(1)} collective-permute-done((bf16[256,512]{1,0:T(8,128)(2,1)S(1)}, bf16[256,512]{1,0:T(8,128)(2,1)S(1)}, u32[]{:S(2)}, u32[]{:S(2)}) %collective-permute-start.26) | collective-permute-done | bytes 262176 | tf_op jit(solution)/shard_map/ppermute | solution.py:406
  188.3 5.0 %collective-permute-done.27.refs_15_.refs_24_ = bf16[256,512]{1,0:T(8,128)(2,1)S(1)} collective-permute-done((bf16[256,512]{1,0:T(8,128)(2,1)S(1)}, bf16[256,512]{1,0:T(8,128)(2,1)S(1)}, u32[]{:S(2)}, u32[]{:S(2)}) %collective-permute-start.27) | collective-permute-done | bytes 262176 | tf_op jit(solution)/shard_map/ppermute | solution.py:406
  198.0 33.7 %collective-permute-done.29.refs_6_ = bf16[256,512]{1,0:T(8,128)(2,1)S(1)} collective-permute-done((bf16[256,512]{1,0:T(8,128)(2,1)S(1)}, bf16[256,512]{1,0:T(8,128)(2,1)S(1)}, u32[]{:S(2)}, u32[]{:S(2)}) %collective-permute-start.29) | collective-permute-done | bytes 262176 | tf_op jit(solution)/shard_map/ppermute | solution.py:406
  231.8 23.7 %shard_map.117 = bf16[256,4096]{1,0:T(8,128)(2,1)} custom-call(s32[1]{0:T(128)} %bitcast.section_ref.refs_0_, s32[2]{0:T(128)S(1)} %bitcast.90, f32[6]{0:T(128)S(1)} %pad_maximum_fusion.3.refs_2_, f32[1,4096]{1,0:T(1,128)S(1)} %get-tuple-element.23.gain_ref.refs_3_, bf16[4096,4352]{1,0:T(8,128)(2,1)} %all-gather.2.cloned.1.call-done.kv_ref.w_ref.refs_5_.refs_4_, ...), custom_call_target="tpu_custom_call" | custom-call | flops 134217728 | bytes 524288 | tf_op jit(solution)/shard_map/pallas_call | solution.py:482
  (114 shorter events, 38.8 us)
Async XLA Ops:
  7.2 128.4 %all-gather.2.cloned.1.call-start = ((), (), s32[]{:S(2)}) async-start(), calls=%async_computation | async-start | bytes 36765696 | tf_op jit(solution)/shard_map/all_gather | solution.py:416
  9.8 5.1 %collective-permute-start.12 = (bf16[144,256]{1,0:T(8,128)(2,1)S(1)}, bf16[144,256]{1,0:T(8,128)(2,1)S(1)}, u32[]{:S(2)}, u32[]{:S(2)}) collective-permute-start(bf16[144,256]{1,0:T(8,128)(2,1)S(1)} %pad_maximum_fusion.2), channel_id=1, source_target_pairs={{96,32},{97,33},{98,34},{99,35},{100,36},{101,37},{102,38},{103,39... | collective-permute-start | bytes 221192 | tf_op jit(solution)/shard_map/ppermute | solution.py:406
  12.9 2.0 collective-permute-start.11
  14.9 1.5 collective-permute-start.13
  15.8 1.5 collective-permute-start.14
  16.4 0.8 collective-permute-start.15
  17.1 2.3 collective-permute-start
  18.7 22.6 %collective-permute-start.16 = (bf16[512,512]{1,0:T(8,128)(2,1)S(1)}, bf16[512,512]{1,0:T(8,128)(2,1)S(1)}, u32[]{:S(2)}, u32[]{:S(2)}) collective-permute-start(bf16[512,512]{1,0:T(8,128)(2,1)S(1)} %shard_map.104.refs_0_), channel_id=1, source_target_pairs={{32,40},{33,35},{34,42},{35,37},{36,44},{37,39},{38,46},{39,33},{4... | collective-permute-start | bytes 1572872 | tf_op jit(solution)/shard_map/ppermute | solution.py:62
  19.4 3.9 %collective-permute-start.1 = (f32[34,128]{1,0:T(8,128)S(1)}, f32[34,128]{1,0:T(8,128)S(1)}, u32[]{:S(2)}, u32[]{:S(2)}) collective-permute-start(f32[34,128]{1,0:T(8,128)S(1)} %fusion.39), channel_id=1, source_target_pairs={{0,2},{1,3},{2,0},{3,1},{4,6},{5,7},{6,4},{7,5},{8,10},{9,11},{10,... | collective-permute-start | bytes 52232 | tf_op jit(solution)/shard_map/ppermute | solution.py:50
  23.3 4.0 %collective-permute-start.2 = (f32[34,128]{1,0:T(8,128)S(1)}, f32[34,128]{1,0:T(8,128)S(1)}, u32[]{:S(2)}, u32[]{:S(2)}) collective-permute-start(f32[34,128]{1,0:T(8,128)S(1)} %fusion.44), channel_id=1, source_target_pairs={{0,8},{1,9},{2,10},{3,11},{4,12},{5,13},{6,14},{7,15},{8,0},{9,1},... | collective-permute-start | bytes 52232 | tf_op jit(solution)/shard_map/ppermute | solution.py:50
  27.3 6.3 %collective-permute-start.3 = (f32[34,128]{1,0:T(8,128)S(1)}, f32[34,128]{1,0:T(8,128)S(1)}, u32[]{:S(2)}, u32[]{:S(2)}) collective-permute-start(f32[34,128]{1,0:T(8,128)S(1)} %add.140), channel_id=1, source_target_pairs={{0,4},{1,5},{2,6},{3,7},{4,0},{5,1},{6,2},{7,3},{8,12},{9,13},{10,... | collective-permute-start | bytes 52232 | tf_op jit(solution)/shard_map/ppermute | solution.py:50
  33.6 5.7 %collective-permute-start.4 = (f32[34,128]{1,0:T(8,128)S(1)}, f32[34,128]{1,0:T(8,128)S(1)}, u32[]{:S(2)}, u32[]{:S(2)}) collective-permute-start(f32[34,128]{1,0:T(8,128)S(1)} %add.141), channel_id=1, source_target_pairs={{0,16},{1,17},{2,18},{3,19},{4,20},{5,21},{6,22},{7,23},{8,24},{9,... | collective-permute-start | bytes 52232 | tf_op jit(solution)/shard_map/ppermute | solution.py:50
  40.6 3.6 %collective-permute-start.17 = (bf16[512,512]{1,0:T(8,128)(2,1)S(1)}, bf16[512,512]{1,0:T(8,128)(2,1)S(1)}, u32[]{:S(2)}, u32[]{:S(2)}) collective-permute-start(bf16[512,512]{1,0:T(8,128)(2,1)S(1)} %shard_map.104.refs_0_), channel_id=1, source_target_pairs={{32,56},{33,39},{34,58},{35,33},{36,60},{37,35},{38,62},{39,37},{4... | collective-permute-start | bytes 1572872 | tf_op jit(solution)/shard_map/ppermute | solution.py:62
  41.3 2.9 %collective-permute-start.18 = (bf16[512,512]{1,0:T(8,128)(2,1)S(1)}, bf16[512,512]{1,0:T(8,128)(2,1)S(1)}, u32[]{:S(2)}, u32[]{:S(2)}) collective-permute-start(bf16[512,512]{1,0:T(8,128)(2,1)S(1)} %collective-permute-done.16.refs_1_), channel_id=1, source_target_pairs={{32,40},{33,35},{34,42},{35,37},{36,44},{37,39},{38,46},{39,33},{4... | collective-permute-start | bytes 1572872 | tf_op jit(solution)/shard_map/ppermute | solution.py:62
  44.2 29.6 %copy-start.9 = (f32[1,3]{1,0:T(1,128)S(1)}, f32[1,3]{1,0:T(1,128)}, u32[]{:S(2)}) copy-start(f32[1,3]{1,0:T(1,128)} %param.11) | copy-start | bytes 40
  45.7 34.4 %collective-permute-start.19 = (bf16[2048,512]{1,0:T(8,128)(2,1)}, bf16[2048,512]{1,0:T(8,128)(2,1)}, u32[]{:S(2)}, u32[]{:S(2)}) collective-permute-start(bf16[2048,512]{1,0:T(8,128)(2,1)} %shard_map.105.refs_0_.refs_6_), channel_id=1, source_target_pairs={{32,33},{33,32},{34,35},{35,34},{36,37},{37,36},{38,39},{39,38},{4... | collective-permute-start | bytes 6291464 | tf_op jit(solution)/shard_map/ppermute | solution.py:62
  48.4 1.3 collective-permute-start.5
  49.7 4.3 %collective-permute-start.6 = (f32[3,128]{0,1:T(8,128)S(1)}, f32[3,128]{0,1:T(8,128)S(1)}, u32[]{:S(2)}, u32[]{:S(2)}) collective-permute-start(f32[3,128]{0,1:T(8,128)S(1)} %broadcast_add_fusion), channel_id=1, source_target_pairs={{0,2},{1,3},{2,0},{3,1},{4,6},{5,7},{6,4},{7,5},{8,10},{9,11},{10,... | collective-permute-start | bytes 4616 | tf_op jit(solution)/shard_map/ppermute | solution.py:50
  54.1 5.1 %collective-permute-start.7 = (f32[3,128]{0,1:T(8,128)S(1)}, f32[3,128]{0,1:T(8,128)S(1)}, u32[]{:S(2)}, u32[]{:S(2)}) collective-permute-start(f32[3,128]{0,1:T(8,128)S(1)} %fusion.43), channel_id=1, source_target_pairs={{0,8},{1,9},{2,10},{3,11},{4,12},{5,13},{6,14},{7,15},{8,0},{9,1},... | collective-permute-start | bytes 4616 | tf_op jit(solution)/shard_map/ppermute | solution.py:50
  59.2 7.2 %collective-permute-start.8 = (f32[3,128]{0,1:T(8,128)S(1)}, f32[3,128]{0,1:T(8,128)S(1)}, u32[]{:S(2)}, u32[]{:S(2)}) collective-permute-start(f32[3,128]{0,1:T(8,128)S(1)} %add.148), channel_id=1, source_target_pairs={{0,4},{1,5},{2,6},{3,7},{4,0},{5,1},{6,2},{7,3},{8,12},{9,13},{10,... | collective-permute-start | bytes 4616 | tf_op jit(solution)/shard_map/ppermute | solution.py:50
  66.5 7.3 %collective-permute-start.9 = (f32[3,128]{0,1:T(8,128)S(1)}, f32[3,128]{0,1:T(8,128)S(1)}, u32[]{:S(2)}, u32[]{:S(2)}) collective-permute-start(f32[3,128]{0,1:T(8,128)S(1)} %add.149), channel_id=1, source_target_pairs={{0,16},{1,17},{2,18},{3,19},{4,20},{5,21},{6,22},{7,23},{8,24},{9,... | collective-permute-start | bytes 4616 | tf_op jit(solution)/shard_map/ppermute | solution.py:50
  73.8 6.4 %collective-permute-start.10 = (f32[3,128]{0,1:T(8,128)S(1)}, f32[3,128]{0,1:T(8,128)S(1)}, u32[]{:S(2)}, u32[]{:S(2)}) collective-permute-start(f32[3,128]{0,1:T(8,128)S(1)} %broadcast_in_dim.33), channel_id=1, source_target_pairs={{64,96},{65,97},{66,98},{67,99},{68,100},{69,101},{70,102},{71,103... | collective-permute-start | bytes 4616 | tf_op jit(solution)/shard_map/ppermute | solution.py:406
  140.3 22.7 %collective-permute-start.20 = (bf16[256,512]{1,0:T(8,128)(2,1)S(1)}, bf16[256,512]{1,0:T(8,128)(2,1)S(1)}, u32[]{:S(2)}, u32[]{:S(2)}) collective-permute-start(bf16[256,512]{1,0:T(8,128)(2,1)S(1)} %shard_map.108.refs_9_), channel_id=1, source_target_pairs={{0,32},{64,96},{1,33},{65,97},{2,34},{66,98},{3,35},{67,99},{4,36}... | collective-permute-start | bytes 786440 | tf_op jit(solution)/shard_map/ppermute | solution.py:406
  143.9 20.4 %collective-permute-start.21 = (bf16[256,512]{1,0:T(8,128)(2,1)S(1)}, bf16[256,512]{1,0:T(8,128)(2,1)S(1)}, u32[]{:S(2)}, u32[]{:S(2)}) collective-permute-start(bf16[256,512]{1,0:T(8,128)(2,1)S(1)} %shard_map.109.refs_10_), channel_id=1, source_target_pairs={{0,32},{64,96},{1,33},{65,97},{2,34},{66,98},{3,35},{67,99},{4,36}... | collective-permute-start | bytes 786440 | tf_op jit(solution)/shard_map/ppermute | solution.py:406
  147.7 17.9 %collective-permute-start.22 = (bf16[256,512]{1,0:T(8,128)(2,1)S(1)}, bf16[256,512]{1,0:T(8,128)(2,1)S(1)}, u32[]{:S(2)}, u32[]{:S(2)}) collective-permute-start(bf16[256,512]{1,0:T(8,128)(2,1)S(1)} %shard_map.110.refs_11_), channel_id=1, source_target_pairs={{0,32},{64,96},{1,33},{65,97},{2,34},{66,98},{3,35},{67,99},{4,36}... | collective-permute-start | bytes 786440 | tf_op jit(solution)/shard_map/ppermute | solution.py:406
  151.4 16.8 %collective-permute-start.23 = (bf16[256,512]{1,0:T(8,128)(2,1)S(1)}, bf16[256,512]{1,0:T(8,128)(2,1)S(1)}, u32[]{:S(2)}, u32[]{:S(2)}) collective-permute-start(bf16[256,512]{1,0:T(8,128)(2,1)S(1)} %shard_map.111.refs_12_), channel_id=1, source_target_pairs={{0,32},{64,96},{1,33},{65,97},{2,34},{66,98},{3,35},{67,99},{4,36}... | collective-permute-start | bytes 786440 | tf_op jit(solution)/shard_map/ppermute | solution.py:406
  154.9 18.2 %collective-permute-start.24 = (bf16[256,512]{1,0:T(8,128)(2,1)S(1)}, bf16[256,512]{1,0:T(8,128)(2,1)S(1)}, u32[]{:S(2)}, u32[]{:S(2)}) collective-permute-start(bf16[256,512]{1,0:T(8,128)(2,1)S(1)} %shard_map.112.refs_13_), channel_id=1, source_target_pairs={{0,32},{64,96},{1,33},{65,97},{2,34},{66,98},{3,35},{67,99},{4,36}... | collective-permute-start | bytes 786440 | tf_op jit(solution)/shard_map/ppermute | solution.py:406
  163.1 19.6 %collective-permute-start.25 = (bf16[256,512]{1,0:T(8,128)(2,1)S(1)}, bf16[256,512]{1,0:T(8,128)(2,1)S(1)}, u32[]{:S(2)}, u32[]{:S(2)}) collective-permute-start(bf16[256,512]{1,0:T(8,128)(2,1)S(1)} %shard_map.113.refs_14_), channel_id=1, source_target_pairs={{0,32},{64,96},{1,33},{65,97},{2,34},{66,98},{3,35},{67,99},{4,36}... | collective-permute-start | bytes 786440 | tf_op jit(solution)/shard_map/ppermute | solution.py:406
  164.4 24.0 %collective-permute-start.26 = (bf16[256,512]{1,0:T(8,128)(2,1)S(1)}, bf16[256,512]{1,0:T(8,128)(2,1)S(1)}, u32[]{:S(2)}, u32[]{:S(2)}) collective-permute-start(bf16[256,512]{1,0:T(8,128)(2,1)S(1)} %shard_map.114.refs_15_), channel_id=1, source_target_pairs={{0,32},{64,96},{1,33},{65,97},{2,34},{66,98},{3,35},{67,99},{4,36}... | collective-permute-start | bytes 786440 | tf_op jit(solution)/shard_map/ppermute | solution.py:406
  165.7 27.6 %collective-permute-start.27 = (bf16[256,512]{1,0:T(8,128)(2,1)S(1)}, bf16[256,512]{1,0:T(8,128)(2,1)S(1)}, u32[]{:S(2)}, u32[]{:S(2)}) collective-permute-start(bf16[256,512]{1,0:T(8,128)(2,1)S(1)} %shard_map.115.refs_16_), channel_id=1, source_target_pairs={{0,32},{64,96},{1,33},{65,97},{2,34},{66,98},{3,35},{67,99},{4,36}... | collective-permute-start | bytes 786440 | tf_op jit(solution)/shard_map/ppermute | solution.py:406
  195.3 36.4 %collective-permute-start.29 = (bf16[256,512]{1,0:T(8,128)(2,1)S(1)}, bf16[256,512]{1,0:T(8,128)(2,1)S(1)}, u32[]{:S(2)}, u32[]{:S(2)}) collective-permute-start(bf16[256,512]{1,0:T(8,128)(2,1)S(1)} %get-tuple-element.12), channel_id=1, source_target_pairs={{32,96},{33,97},{34,98},{35,99},{36,100},{37,101},{38,102},{39,103... | collective-permute-start | bytes 786440 | tf_op jit(solution)/shard_map/ppermute | solution.py:406
  196.6 1.4 collective-permute-start.28
  (9 other events, 44.1 us)
Sparse Core Ops, SparseCore 0:
  10.3 125.2 all-gather.1
